TPU v7x, 32 devices: a whole 2x2x4 slice. The times are simulated.
32 devices in a mesh: blk: 16 (over z, y, core), par: 2 (over x).
Axes of the slice: x: 2, y: 2, z: 4, core: 2. Of those that a mesh axis runs over, the one named last changes fastest.
Arguments:
- logder: float32 [2048, 6144], P('blk', 'par'), may hold values from -50 to 50
Outputs:
- kernel_tiles: float32 [16, 9, 128, 128], P('blk', None, 'par')
All inputs are finite; a program needn't handle non-finite values.
Results may differ from a plain program's by a relative error of at most 0.00015.
Values sent between devices are 32-bit elements; how exact they have to be, the bound alone decides.
No kernel may reach another device: no remote copies, remote signals or barrier semaphores. Data moves between devices by JAX's collectives and lax.ppermute only.
A program may use at most 64 MiB of HBM per device.

v0:
```python
import jax
import jax.numpy as jnp
from jax import lax
from jax.sharding import PartitionSpec as P


def from_behind(value, axis, steps):
    count = lax.axis_size(axis)
    pairs = [(source, (source + steps) % count) for source in range(count)]
    return lax.ppermute(value, axis, pairs)


def pair_tile(left, right, factor):
    return (
        lax.dot_general(
            left,
            right,
            (((1,), (1,)), ((), ())),
            precision=lax.Precision.HIGHEST,
            preferred_element_type=jnp.float32,
        )
        * factor
    )


def on_device(logder):
    nblocks = lax.axis_size("blk")
    nshards = lax.axis_size("par")
    rows, width = logder.shape
    totals = lax.psum(jnp.sum(logder, axis=0), "blk")
    centered = logder - totals[None, :] / (rows * nblocks)
    factor = 1.0 / (width * nshards)
    half = nblocks // 2

    def advance(current):
        return from_behind(current, "blk", -1)

    def turn(current, unused):
        first = pair_tile(centered, current, factor)
        current = advance(current)
        second = pair_tile(centered, current, factor)
        current = advance(current)
        return (current, jnp.stack([first, second]))

    final, pairs = lax.scan(turn, centered, None, length=half // 2)
    stacked = jnp.concatenate(
        [pairs.reshape(half, rows, rows), pair_tile(centered, final, factor)[None]], axis=0
    )
    shares = lax.psum_scatter(stacked, "par", scatter_dimension=1, tiled=True)
    return shares[None]


def solution(mesh):
    placed = (P("blk", "par"),)
    return jax.shard_map(
        on_device,
        mesh=mesh,
        in_specs=placed,
        out_specs=P("blk", None, "par", None),
        check_vma=False,
    )
```

profile of v0, /device:TPU:0, one launch (start us, length us, event | category | flops | bytes accessed | tf_op | source)
XLA Modules:
  0.0 282.8 jit_solution(11224856560078877444)
XLA Ops:
  6.5 0.0 copy-start
  6.5 0.0 reduce-scatter.2.cloned.1.call-start
  6.5 1.6 reduce_sum.9
  8.2 63.0 %psum.7 = f32[3072]{0:T(1024)S(1)} all-reduce(f32[3072]{0:T(1024)S(1)} %reduce_sum.9), channel_id=1, replica_groups=mesh['blk'=16,'par'=2] {'blk'}, use_global_device_ids=true, to_apply=%region_1.0 | all-reduce | flops 3072 | bytes 24576 | tf_op jit(solution)/shard_map/psum | solution.py:30
  71.1 0.0 copy-done
  71.1 0.1 broadcast_subtract_fusion
  71.3 1.1 copy.4
  72.4 183.0 %while.12 = (s32[]{:T(128)}, f32[128,3072]{1,0:T(8,128)}, f32[4,2,128,128]{3,2,1,0:T(8,128)}, f32[128,3072]{1,0:T(8,128)S(1)}, s32[]{:T(128)}) while((s32[]{:T(128)}, f32[128,3072]{1,0:T(8,128)}, f32[4,2,128,128]{3,2,1,0:T(8,128)}, f32[128,3072]{1,0:T(8,128)S(1)}, s32[]{:T(128)}) %tuple.18), condition=%wide.region_3.4_spmd, body=%wide.region_2.3_spmd.sunk | while | flops 1208025088 | bytes 22413464 | solution.py:45
  72.4 1.4 copy.7
  73.8 0.0 collective-permute-start
  73.8 17.9 %collective-permute-done = f32[128,3072]{1,0:T(8,128)} collective-permute-done((f32[128,3072]{1,0:T(8,128)S(1)}, f32[128,3072]{1,0:T(8,128)}, u32[]{:S(2)}, u32[]{:S(2)}) %collective-permute-start) | collective-permute-done | bytes 1572896 | tf_op jit(solution)/shard_map/while/body/eval_jaxpr/ppermute | solution.py:10
  91.8 4.7 %collective-permute-start.1 = (f32[128,3072]{1,0:T(8,128)}, f32[128,3072]{1,0:T(8,128)}, u32[]{:S(2)}, u32[]{:S(2)}) collective-permute-start(f32[128,3072]{1,0:T(8,128)} %collective-permute-done), channel_id=1, source_target_pairs={{0,30},{2,0},{4,2},{6,4},{8,6},{10,8},{12,10},{14,12},{16,14},{18,... | collective-permute-start | bytes 4718600 | tf_op jit(solution)/shard_map/while/body/eval_jaxpr/ppermute | solution.py:10
  96.5 1.4 fusion.22
  97.9 2.8 fusion.21
  100.7 0.7 fusion.23
  101.4 13.3 %collective-permute-done.1 = f32[128,3072]{1,0:T(8,128)} collective-permute-done((f32[128,3072]{1,0:T(8,128)}, f32[128,3072]{1,0:T(8,128)}, u32[]{:S(2)}, u32[]{:S(2)}) %collective-permute-start.1) | collective-permute-done | bytes 1572896 | tf_op jit(solution)/shard_map/while/body/eval_jaxpr/ppermute | solution.py:10
  114.7 1.4 copy.7
  116.1 4.6 %collective-permute-start = (f32[128,3072]{1,0:T(8,128)S(1)}, f32[128,3072]{1,0:T(8,128)}, u32[]{:S(2)}, u32[]{:S(2)}) collective-permute-start(f32[128,3072]{1,0:T(8,128)S(1)} %copy.7), channel_id=1, source_target_pairs={{0,30},{2,0},{4,2},{6,4},{8,6},{10,8},{12,10},{14,12},{16,14},{18,... | collective-permute-start | bytes 4718600 | tf_op jit(solution)/shard_map/while/body/eval_jaxpr/ppermute | solution.py:10
  120.7 17.9 %collective-permute-done = f32[128,3072]{1,0:T(8,128)} collective-permute-done((f32[128,3072]{1,0:T(8,128)S(1)}, f32[128,3072]{1,0:T(8,128)}, u32[]{:S(2)}, u32[]{:S(2)}) %collective-permute-start) | collective-permute-done | bytes 1572896 | tf_op jit(solution)/shard_map/while/body/eval_jaxpr/ppermute | solution.py:10
  138.7 4.7 %collective-permute-start.1 = (f32[128,3072]{1,0:T(8,128)}, f32[128,3072]{1,0:T(8,128)}, u32[]{:S(2)}, u32[]{:S(2)}) collective-permute-start(f32[128,3072]{1,0:T(8,128)} %collective-permute-done), channel_id=1, source_target_pairs={{0,30},{2,0},{4,2},{6,4},{8,6},{10,8},{12,10},{14,12},{16,14},{18,... | collective-permute-start | bytes 4718600 | tf_op jit(solution)/shard_map/while/body/eval_jaxpr/ppermute | solution.py:10
  143.4 1.4 fusion.22
  144.8 2.8 fusion.21
  147.6 0.7 fusion.23
  148.3 13.3 %collective-permute-done.1 = f32[128,3072]{1,0:T(8,128)} collective-permute-done((f32[128,3072]{1,0:T(8,128)}, f32[128,3072]{1,0:T(8,128)}, u32[]{:S(2)}, u32[]{:S(2)}) %collective-permute-start.1) | collective-permute-done | bytes 1572896 | tf_op jit(solution)/shard_map/while/body/eval_jaxpr/ppermute | solution.py:10
  161.6 1.4 copy.7
  163.0 4.6 %collective-permute-start = (f32[128,3072]{1,0:T(8,128)S(1)}, f32[128,3072]{1,0:T(8,128)}, u32[]{:S(2)}, u32[]{:S(2)}) collective-permute-start(f32[128,3072]{1,0:T(8,128)S(1)} %copy.7), channel_id=1, source_target_pairs={{0,30},{2,0},{4,2},{6,4},{8,6},{10,8},{12,10},{14,12},{16,14},{18,... | collective-permute-start | bytes 4718600 | tf_op jit(solution)/shard_map/while/body/eval_jaxpr/ppermute | solution.py:10
  167.6 17.9 %collective-permute-done = f32[128,3072]{1,0:T(8,128)} collective-permute-done((f32[128,3072]{1,0:T(8,128)S(1)}, f32[128,3072]{1,0:T(8,128)}, u32[]{:S(2)}, u32[]{:S(2)}) %collective-permute-start) | collective-permute-done | bytes 1572896 | tf_op jit(solution)/shard_map/while/body/eval_jaxpr/ppermute | solution.py:10
  185.6 4.7 %collective-permute-start.1 = (f32[128,3072]{1,0:T(8,128)}, f32[128,3072]{1,0:T(8,128)}, u32[]{:S(2)}, u32[]{:S(2)}) collective-permute-start(f32[128,3072]{1,0:T(8,128)} %collective-permute-done), channel_id=1, source_target_pairs={{0,30},{2,0},{4,2},{6,4},{8,6},{10,8},{12,10},{14,12},{16,14},{18,... | collective-permute-start | bytes 4718600 | tf_op jit(solution)/shard_map/while/body/eval_jaxpr/ppermute | solution.py:10
  190.3 1.4 fusion.22
  191.7 2.8 fusion.21
  194.5 0.7 fusion.23
  195.2 13.3 %collective-permute-done.1 = f32[128,3072]{1,0:T(8,128)} collective-permute-done((f32[128,3072]{1,0:T(8,128)}, f32[128,3072]{1,0:T(8,128)}, u32[]{:S(2)}, u32[]{:S(2)}) %collective-permute-start.1) | collective-permute-done | bytes 1572896 | tf_op jit(solution)/shard_map/while/body/eval_jaxpr/ppermute | solution.py:10
  208.5 1.4 copy.7
  209.9 4.6 %collective-permute-start = (f32[128,3072]{1,0:T(8,128)S(1)}, f32[128,3072]{1,0:T(8,128)}, u32[]{:S(2)}, u32[]{:S(2)}) collective-permute-start(f32[128,3072]{1,0:T(8,128)S(1)} %copy.7), channel_id=1, source_target_pairs={{0,30},{2,0},{4,2},{6,4},{8,6},{10,8},{12,10},{14,12},{16,14},{18,... | collective-permute-start | bytes 4718600 | tf_op jit(solution)/shard_map/while/body/eval_jaxpr/ppermute | solution.py:10
  214.5 17.9 %collective-permute-done = f32[128,3072]{1,0:T(8,128)} collective-permute-done((f32[128,3072]{1,0:T(8,128)S(1)}, f32[128,3072]{1,0:T(8,128)}, u32[]{:S(2)}, u32[]{:S(2)}) %collective-permute-start) | collective-permute-done | bytes 1572896 | tf_op jit(solution)/shard_map/while/body/eval_jaxpr/ppermute | solution.py:10
  232.5 4.7 %collective-permute-start.1 = (f32[128,3072]{1,0:T(8,128)}, f32[128,3072]{1,0:T(8,128)}, u32[]{:S(2)}, u32[]{:S(2)}) collective-permute-start(f32[128,3072]{1,0:T(8,128)} %collective-permute-done), channel_id=1, source_target_pairs={{0,30},{2,0},{4,2},{6,4},{8,6},{10,8},{12,10},{14,12},{16,14},{18,... | collective-permute-start | bytes 4718600 | tf_op jit(solution)/shard_map/while/body/eval_jaxpr/ppermute | solution.py:10
  237.2 1.4 fusion.22
  238.6 2.8 fusion.21
  241.4 0.7 fusion.23
  242.1 13.3 %collective-permute-done.1 = f32[128,3072]{1,0:T(8,128)} collective-permute-done((f32[128,3072]{1,0:T(8,128)}, f32[128,3072]{1,0:T(8,128)}, u32[]{:S(2)}, u32[]{:S(2)}) %collective-permute-start.1) | collective-permute-done | bytes 1572896 | tf_op jit(solution)/shard_map/while/body/eval_jaxpr/ppermute | solution.py:10
  255.4 0.0 copy-start.1
  255.4 2.9 %fusion.3 = f32[1,128,128]{2,1,0:T(8,128)S(1)} fusion(f32[128,3072]{1,0:T(8,128)S(1)} %get-tuple-element.79, f32[128,3072]{1,0:T(8,128)} %get-tuple-element.29), kind=kOutput, calls=%fused_computation.7 | convolution fusion | flops 603996160 | bytes 3211264 | tf_op jit(solution)/shard_map/dot_general | solution.py:15
  258.3 0.0 copy-done.1
  258.3 0.9 pad_maximum_fusion
  259.2 0.0 reduce-scatter.2.cloned.1.call-update
  259.2 16.8 %reduce-scatter.2.cloned.1.call-done = f32[9,64,128]{2,1,0:T(8,128)} async-done(((f32[9,128,128]{2,1,0:T(8,128)}), f32[9,64,128]{2,1,0:T(8,128)}) %reduce-scatter.2.cloned.1.call-update) | async-done | bytes 294928 | tf_op jit(solution)/shard_map/reduce_scatter | solution.py:49
  (2 shorter events, 0.0 us)
Async XLA Ops:
  6.5 64.6 %copy-start = (f32[128,3072]{1,0:T(8,128)S(1)}, f32[128,3072]{1,0:T(8,128)}, u32[]{:S(2)}) copy-start(f32[128,3072]{1,0:T(8,128)} %param.3) | copy-start | bytes 4718596
  6.5 269.4 %reduce-scatter.2.cloned.1.call-start = ((), (), s32[]{:S(2)}) async-start(), calls=%async_computation.1 | async-start | bytes 884736 | tf_op jit(solution)/shard_map/reduce_scatter | solution.py:49
  73.8 17.9 %collective-permute-start = (f32[128,3072]{1,0:T(8,128)S(1)}, f32[128,3072]{1,0:T(8,128)}, u32[]{:S(2)}, u32[]{:S(2)}) collective-permute-start(f32[128,3072]{1,0:T(8,128)S(1)} %copy.7), channel_id=1, source_target_pairs={{0,30},{2,0},{4,2},{6,4},{8,6},{10,8},{12,10},{14,12},{16,14},{18,... | collective-permute-start | bytes 4718600 | tf_op jit(solution)/shard_map/while/body/eval_jaxpr/ppermute | solution.py:10
  91.8 23.0 %collective-permute-start.1 = (f32[128,3072]{1,0:T(8,128)}, f32[128,3072]{1,0:T(8,128)}, u32[]{:S(2)}, u32[]{:S(2)}) collective-permute-start(f32[128,3072]{1,0:T(8,128)} %collective-permute-done), channel_id=1, source_target_pairs={{0,30},{2,0},{4,2},{6,4},{8,6},{10,8},{12,10},{14,12},{16,14},{18,... | collective-permute-start | bytes 4718600 | tf_op jit(solution)/shard_map/while/body/eval_jaxpr/ppermute | solution.py:10
  116.1 22.5 %collective-permute-start = (f32[128,3072]{1,0:T(8,128)S(1)}, f32[128,3072]{1,0:T(8,128)}, u32[]{:S(2)}, u32[]{:S(2)}) collective-permute-start(f32[128,3072]{1,0:T(8,128)S(1)} %copy.7), channel_id=1, source_target_pairs={{0,30},{2,0},{4,2},{6,4},{8,6},{10,8},{12,10},{14,12},{16,14},{18,... | collective-permute-start | bytes 4718600 | tf_op jit(solution)/shard_map/while/body/eval_jaxpr/ppermute | solution.py:10
  138.7 23.0 %collective-permute-start.1 = (f32[128,3072]{1,0:T(8,128)}, f32[128,3072]{1,0:T(8,128)}, u32[]{:S(2)}, u32[]{:S(2)}) collective-permute-start(f32[128,3072]{1,0:T(8,128)} %collective-permute-done), channel_id=1, source_target_pairs={{0,30},{2,0},{4,2},{6,4},{8,6},{10,8},{12,10},{14,12},{16,14},{18,... | collective-permute-start | bytes 4718600 | tf_op jit(solution)/shard_map/while/body/eval_jaxpr/ppermute | solution.py:10
  163.0 22.5 %collective-permute-start = (f32[128,3072]{1,0:T(8,128)S(1)}, f32[128,3072]{1,0:T(8,128)}, u32[]{:S(2)}, u32[]{:S(2)}) collective-permute-start(f32[128,3072]{1,0:T(8,128)S(1)} %copy.7), channel_id=1, source_target_pairs={{0,30},{2,0},{4,2},{6,4},{8,6},{10,8},{12,10},{14,12},{16,14},{18,... | collective-permute-start | bytes 4718600 | tf_op jit(solution)/shard_map/while/body/eval_jaxpr/ppermute | solution.py:10
  185.6 23.0 %collective-permute-start.1 = (f32[128,3072]{1,0:T(8,128)}, f32[128,3072]{1,0:T(8,128)}, u32[]{:S(2)}, u32[]{:S(2)}) collective-permute-start(f32[128,3072]{1,0:T(8,128)} %collective-permute-done), channel_id=1, source_target_pairs={{0,30},{2,0},{4,2},{6,4},{8,6},{10,8},{12,10},{14,12},{16,14},{18,... | collective-permute-start | bytes 4718600 | tf_op jit(solution)/shard_map/while/body/eval_jaxpr/ppermute | solution.py:10
  209.9 22.5 %collective-permute-start = (f32[128,3072]{1,0:T(8,128)S(1)}, f32[128,3072]{1,0:T(8,128)}, u32[]{:S(2)}, u32[]{:S(2)}) collective-permute-start(f32[128,3072]{1,0:T(8,128)S(1)} %copy.7), channel_id=1, source_target_pairs={{0,30},{2,0},{4,2},{6,4},{8,6},{10,8},{12,10},{14,12},{16,14},{18,... | collective-permute-start | bytes 4718600 | tf_op jit(solution)/shard_map/while/body/eval_jaxpr/ppermute | solution.py:10
  232.5 23.0 %collective-permute-start.1 = (f32[128,3072]{1,0:T(8,128)}, f32[128,3072]{1,0:T(8,128)}, u32[]{:S(2)}, u32[]{:S(2)}) collective-permute-start(f32[128,3072]{1,0:T(8,128)} %collective-permute-done), channel_id=1, source_target_pairs={{0,30},{2,0},{4,2},{6,4},{8,6},{10,8},{12,10},{14,12},{16,14},{18,... | collective-permute-start | bytes 4718600 | tf_op jit(solution)/shard_map/while/body/eval_jaxpr/ppermute | solution.py:10
  255.4 2.9 %copy-start.1 = (f32[4,2,128,128]{3,2,1,0:T(8,128)S(1)}, f32[4,2,128,128]{3,2,1,0:T(8,128)}, u32[]{:S(2)}) copy-start(f32[4,2,128,128]{3,2,1,0:T(8,128)} %get-tuple-element.28) | copy-start | bytes 1572868
Sparse Core Ops, SparseCore 0:
  259.3 16.5 reduce-scatter.1
where the time goes:
time: 283 us
  waiting for transfers between devices  142 us (50%)
  blocking collectives  63 us (22%)
  starting transfers between devices  32.6 us (12%)
  matrix products  19.8 us (7%)
  between operations  13.4 us (5%)
  local copies, waits for them, and re-layouts  6.79 us (2%)
  other arithmetic  5.26 us (2%)
    ppermute x8, waiting for transfers between devices, from_behind(): return lax.ppermute(value, axis, pairs)  125 us
    psum x1, blocking collectives, on_device(): totals = lax.psum(jnp.sum(logder, axis=0), 'blk')  63 us
    ppermute x8, starting transfers between devices, from_behind(): return lax.ppermute(value, axis, pairs)  32.6 us
    dot_general x9, matrix products, pair_tile(): lax.dot_general(left, right, (((1,), (1,)), ((), ())), precision=lax.Prec...  19.8 us
    reduce_scatter x1, waiting for transfers between devices, on_device(): shares = lax.psum_scatter(stacked, 'par', scatter_dimension=1, tiled=True)  16.8 us
  transfers between devices with their start and end apart: 9, of which 9 were waited for; matrix products, arithmetic and copies ran while one was open for 7% of the time, Pallas kernels for 0%

commit v1 on v0

v1 whole, which is shorter than its diff:
```python
import jax
import jax.numpy as jnp
from jax import lax
from jax.sharding import PartitionSpec as P


def swap(value, axis, mask):
    return lax.ppermute(value, axis, [(k, k ^ mask) for k in range(lax.axis_size(axis))])


def pick(value, index, axis):
    return lax.dynamic_index_in_dim(value, index, axis, keepdims=False)


def on_device(logder):
    nblocks = lax.axis_size("blk")
    nshards = lax.axis_size("par")
    rows, width = logder.shape
    me = lax.axis_index("blk")
    levels = 2
    group = 1 << levels
    planes = nblocks // group
    tiles = nblocks // 2 + 1
    factor = 1.0 / (width * nshards)

    sums = lax.all_gather(jnp.sum(logder, axis=0), "blk")

    piece = logder[None]
    offset = 0
    for level in range(levels):
        bit = (me >> level) & 1
        part = piece.shape[-1] // 2
        mine = lax.dynamic_slice_in_dim(piece, bit * part, part, 2)
        other = lax.dynamic_slice_in_dim(piece, (1 - bit) * part, part, 2)
        offset = offset + bit * part
        got = swap(other, "blk", 1 << level)
        piece = jnp.where(
            bit == 0, jnp.concatenate([mine, got]), jnp.concatenate([got, mine])
        )
    part = piece.shape[-1]
    slab = piece.reshape(group * rows, part)
    mean = jnp.sum(lax.dynamic_slice_in_dim(sums, offset, part, 1), axis=0) / (rows * nblocks)

    left = slab - mean
    down = [(k, (k - group) % nblocks) for k in range(nblocks)]
    current = slab
    products = []
    for step in range(planes // 2 + 1):
        products.append(
            lax.dot_general(
                left,
                current - mean,
                (((1,), (1,)), ((), ())),
                precision=lax.Precision.HIGH,
                preferred_element_type=jnp.float32,
            )
        )
        if step < planes // 2:
            current = lax.ppermute(current, "blk", down)
    full = jnp.concatenate(products, axis=1)
    full = full.reshape(group, rows, -1)
    share = jnp.stack(
        [full[k, :, k * rows : (k + tiles) * rows] for k in range(group)]
    )
    for level in range(levels):
        bit = (me >> level) & 1
        share = share.reshape(share.shape[0] // 2, 2, rows, tiles * rows)
        got = swap(pick(share, 1 - bit, 1), "blk", 1 << level)
        share = pick(share, bit, 1) + got
    share = share[0]
    shard = lax.axis_index("par")
    mask = nshards // 2
    while mask:
        bit = (shard // mask) % 2
        share = share.reshape(2, share.shape[-2] // 2, tiles * rows)
        got = swap(pick(share, 1 - bit, 0), "par", mask)
        share = pick(share, bit, 0) + got
        mask //= 2
    out = (share * factor).reshape(rows // nshards, tiles, rows)
    return jnp.swapaxes(out, 0, 1)[None]


def solution(mesh):
    placed = (P("blk", "par"),)
    return jax.shard_map(
        on_device,
        mesh=mesh,
        in_specs=placed,
        out_specs=P("blk", None, "par", None),
        check_vma=False,
    )
```

time: 283 us -> 165 us (0.58)
  waiting for transfers between devices: 142 us -> 91.6 us
  blocking collectives: 63 us -> 33.6 us
  starting transfers between devices: 32.6 us -> 7.18 us
  between operations: 13.4 us -> 0.2 us
  local copies, waits for them, and re-layouts: 6.79 us -> 19.5 us
  matrix products: 19.8 us -> 7.1 us
    psum x1 -> x0, blocking collectives: 63 us -> none  [on_device(): totals = lax.psum(jnp.sum(logder, axis=0), 'blk')]
    all_gather x0 -> x1, blocking collectives: none -> 33.6 us  [on_device(): sums = lax.all_gather(jnp.sum(logder, axis=0), 'blk')]
    ppermute x8 -> x7, waiting for transfers between devices: 125 us -> 91.6 us  [the longest x2 66.5 us: on_device(): current = lax.ppermute(current, 'blk', down)]
    ppermute x8 -> x7, starting transfers between devices: 32.6 us -> 7.18 us  [the longest x5 5.04 us: swap(): lax.ppermute(value, axis, [(k, k ^ mask) for k in range(lax.axis_size(axi...]
    reduce_scatter x1 -> x0, waiting for transfers between devices: 16.8 us -> none  [on_device(): shares = lax.psum_scatter(stacked, 'par', scatter_dimension=1, tiled=True)]
    dot_general x9 -> x3, matrix products: 19.8 us -> 7.1 us  [on_device(): lax.dot_general(left, current - mean, (((1,), (1,)), ((), ())), precision...]
    another operation x4 -> x0, local copies, waits for them, and re-layouts: 5.63 us -> none
    slice x0 -> x1, local copies, waits for them, and re-layouts: none -> 5.21 us  [on_device(): full[k, :, k * rows:(k + tiles) * rows]]
  transfers between devices with their start and end apart: 9 -> 7, of which waited for: 9 -> 6; matrix products, arithmetic and copies ran while one was open for 7% -> 4% of each run, Pallas kernels for 0% -> 0%
where the time goes in v1:
time: 165 us; the launch traced here: 164 us
  waiting for transfers between devices  91.6 us (56%)
  blocking collectives  33.6 us (20%)
  local copies, waits for them, and re-layouts  19.5 us (12%)
  starting transfers between devices  7.18 us (4%)
  matrix products  7.1 us (4%)
  other arithmetic  5.2 us (3%)
    ppermute x2, waiting for transfers between devices, on_device(): current = lax.ppermute(current, 'blk', down)  66.5 us
    all_gather x1, blocking collectives, on_device(): sums = lax.all_gather(jnp.sum(logder, axis=0), 'blk')  33.6 us
    ppermute x5, waiting for transfers between devices, swap(): lax.ppermute(value, axis, [(k, k ^ mask) for k in range(lax.axis_size(axi...  25.1 us
    dot_general x3, matrix products, on_device(): lax.dot_general(left, current - mean, (((1,), (1,)), ((), ())), precision...  7.1 us
    unnamed x6, local copies, waits for them, and re-layouts  5.65 us
    slice x1, local copies, waits for them, and re-layouts, on_device(): full[k, :, k * rows:(k + tiles) * rows]  5.21 us
    ppermute x5, starting transfers between devices, swap(): lax.ppermute(value, axis, [(k, k ^ mask) for k in range(lax.axis_size(axi...  5.04 us
  transfers between devices with their start and end apart: 7, of which 6 were waited for; matrix products, arithmetic and copies ran while one was open for 4% of the time, Pallas kernels for 0%

profile of v1, /device:TPU:0, one launch (start us, length us, event | category | flops | bytes accessed | tf_op | source)
XLA Modules:
  0.0 164.4 jit_solution(17767396494205004572)
XLA Ops:
  0.0 1.5 dynamic-slice_bitcast_fusion.1
  1.5 0.5 collective-permute-start
  2.0 1.9 %collective-permute-done = f32[1,128,1536]{2,1,0:T(8,128)S(1)} collective-permute-done((f32[1,128,1536]{2,1,0:T(8,128)S(1)}, f32[1,128,1536]{2,1,0:T(8,128)S(1)}, u32[]{:S(2)}, u32[]{:S(2)}) %collective-permute-start) | collective-permute-done | bytes 786464 | tf_op jit(solution)/shard_map/ppermute | solution.py:8
  3.9 0.1 maximum_select_fusion
  4.0 0.0 copy-start
  4.0 1.0 constant_dynamic-slice_fusion.3
  5.0 2.9 %collective-permute-start.1 = (f32[2,128,768]{2,1,0:T(8,128)S(1)}, f32[2,128,768]{2,1,0:T(8,128)S(1)}, u32[]{:S(2)}, u32[]{:S(2)}) collective-permute-start(f32[2,128,768]{2,1,0:T(8,128)S(1)} %get-tuple-element.13), channel_id=1, source_target_pairs={{0,4},{2,6},{4,0},{6,2},{8,12},{10,14},{12,8},{14,10},{16,20},{18,... | collective-permute-start | bytes 2359304 | tf_op jit(solution)/shard_map/ppermute | solution.py:8
  7.9 0.0 copy-done
  7.9 0.1 reduce_sum.18
  8.0 33.6 %all-gather = f32[49152]{0:T(1024)S(1)} all-gather(f32[3072]{0:T(1024)S(1)} %reduce_sum.18), channel_id=2, replica_groups=mesh['blk'=16,'par'=2] {'blk'}, dimensions={0}, use_global_device_ids=true | all-gather | bytes 208896 | tf_op jit(solution)/shard_map/all_gather | solution.py:26
  41.7 0.0 collective-permute-done.1
  41.7 0.0 copy-start.1
  41.8 0.9 copy-done.1
  42.6 2.2 %broadcast_subtract_fusion = (f32[4,128,768]{2,1,0:T(8,128)S(1)}, f32[4,128,768]{2,1,0:T(8,128)S(1)}) fusion(f32[768]{0:T(1024)S(1)} %broadcast_multiply_fusion, f32[2,128,768]{2,1,0:T(8,128)} %get-tuple-element.14, f32[2,128,768]{2,1,0:T(8,128)} %copy-done.1, pred[]{:T(512)S(6)} %eq.8), kind=kLoop, calls=%fused_computation.13 | loop fusion | flops 1572864 | bytes 4721665 | tf_op jit(solution)/shard_map/sub | solution.py:44
  44.8 0.1 collective-permute-start.2
  44.9 36.7 %collective-permute-done.2 = f32[512,768]{1,0:T(8,128)} collective-permute-done((f32[512,768]{1,0:T(8,128)S(1)}, f32[512,768]{1,0:T(8,128)}, u32[]{:S(2)}, u32[]{:S(2)}) %collective-permute-start.2) | collective-permute-done | bytes 1572896 | tf_op jit(solution)/shard_map/ppermute | solution.py:59
  81.6 2.1 %collective-permute-start.3 = (f32[512,768]{1,0:T(8,128)}, f32[512,768]{1,0:T(8,128)}, u32[]{:S(2)}, u32[]{:S(2)}) collective-permute-start(f32[512,768]{1,0:T(8,128)} %collective-permute-done.2), channel_id=1, source_target_pairs={{0,24},{2,26},{4,28},{6,30},{8,0},{10,2},{12,4},{14,6},{16,8},{18,... | collective-permute-start | bytes 4718600 | tf_op jit(solution)/shard_map/ppermute | solution.py:59
  83.7 1.4 fusion.10
  85.1 2.8 %fusion.2 = f32[512,512]{0,1:T(8,128)S(1)} fusion(f32[512,768]{1,0:T(8,128)} %collective-permute-done.2, f32[512,768]{1,0:T(8,128)S(1)} %bitcast.26, f32[768]{0:T(1024)S(1)} %broadcast_multiply_fusion), kind=kOutput, calls=%fused_computation.6 | convolution fusion | flops 1208745984 | bytes 4197376 | tf_op jit(solution)/shard_map/dot_general | solution.py:50
  88.0 29.8 %collective-permute-done.3 = f32[512,768]{1,0:T(8,128)} collective-permute-done((f32[512,768]{1,0:T(8,128)}, f32[512,768]{1,0:T(8,128)}, u32[]{:S(2)}, u32[]{:S(2)}) %collective-permute-start.3) | collective-permute-done | bytes 1572896 | tf_op jit(solution)/shard_map/ppermute | solution.py:59
  117.8 2.8 %fusion = f32[512,512]{0,1:T(8,128)S(1)} fusion(f32[512,768]{1,0:T(8,128)} %collective-permute-done.3, f32[512,768]{1,0:T(8,128)S(1)} %bitcast.27, f32[768]{0:T(1024)S(1)} %broadcast_multiply_fusion), kind=kOutput, calls=%fused_computation.4 | convolution fusion | flops 1208745984 | bytes 4197376 | tf_op jit(solution)/shard_map/dot_general | solution.py:50
  120.6 0.3 pad_maximum_fusion
  120.9 2.7 %reshape.72 = f32[4,128,1536]{1,0,2:T(4,128)} reshape(f32[512,1536]{0,1:T(8,128)S(1)} %pad_maximum_fusion) | data formatting | bytes 6291456 | tf_op jit(solution)/shard_map/reshape | solution.py:61
  123.6 5.2 %fusion.9 = (f32[1,128,1152]{1,0,2:T(1,128)S(1)}, f32[1,128,1152]{1,0,2:T(1,128)S(1)}, f32[1,128,1152]{1,0,2:T(1,128)S(1)}, f32[1,128,1152]{1,0,2:T(1,128)S(1)}) fusion(f32[4,128,1536]{1,0,2:T(4,128)} %reshape.72), kind=kLoop, calls=%fused_computation.27 | loop fusion | bytes 4718592 | tf_op jit(solution)/shard_map/slice | solution.py:63
  128.9 2.3 %pad_maximum_fusion.1 = f32[4,128,1152]{1,0,2:T(4,128)S(1)} fusion(f32[1,128,1152]{1,0,2:T(1,128)S(1)} %get-tuple-element.8, f32[1,128,1152]{1,0,2:T(1,128)S(1)} %get-tuple-element.9, f32[1,128,1152]{1,0,2:T(1,128)S(1)} %get-tuple-element.10, f32[1,128,1152]{1,0,2:T(1,128)S(1)} %get-tuple-element.7), kind=kLoop, calls=%fused_computation.1 | loop fusion | flops 1769472 | bytes 4718592 | tf_op jit(solution)/shard_map/stack | solution.py:62
  131.1 2.5 %constant_dynamic-slice_fusion.2 = (f32[2,1,128,1152]{2,1,0,3:T(1,128)S(1)}, f32[2,1,128,1152]{2,1,0,3:T(1,128)S(1)}) fusion(f32[2,2,128,1152]{2,1,0,3:T(2,128)S(1)} %bitcast.28, s32[]{:T(128)S(6)} %select_n.86, s32[]{:T(128)S(6)} %select_n.87), kind=kLoop, calls=%fused_computation.23 | loop fusion | bytes 4718600 | tf_op jit(solution)/shard_map/jit(dynamic_index_in_dim)/dynamic_slice | solution.py:12
  133.6 2.8 %copy.12 = f32[2,1,128,1152]{3,2,0,1:T(8,128)} copy(f32[2,1,128,1152]{2,1,0,3:T(1,128)S(1)} %get-tuple-element.12) | data formatting | bytes 2359296
  136.5 0.0 collective-permute-start.4
  136.5 1.9 %copy.11 = f32[2,1,128,1152]{3,2,0,1:T(8,128)S(1)} copy(f32[2,1,128,1152]{2,1,0,3:T(1,128)S(1)} %get-tuple-element.11) | data formatting | bytes 2359296
  138.4 1.1 collective-permute-done.4
  139.5 0.1 bitcast_add_fusion
  139.7 0.1 collective-permute-start.5
  139.8 15.3 %collective-permute-done.5 = f32[1,128,1152]{2,1,0:T(8,128)S(1)} collective-permute-done((f32[1,128,1152]{2,1,0:T(8,128)S(1)}, f32[1,128,1152]{2,1,0:T(8,128)S(1)}, u32[]{:S(2)}, u32[]{:S(2)}) %collective-permute-start.5) | collective-permute-done | bytes 589856 | tf_op jit(solution)/shard_map/ppermute | solution.py:8
  155.1 0.1 dynamic-slice_add_fusion
  155.2 1.6 collective-permute-start.6
  156.8 6.7 %collective-permute-done.6 = f32[64,1152]{1,0:T(8,128)S(1)} collective-permute-done((f32[64,1152]{1,0:T(8,128)S(1)}, f32[64,1152]{1,0:T(8,128)S(1)}, u32[]{:S(2)}, u32[]{:S(2)}) %collective-permute-start.6) | collective-permute-done | bytes 294944 | tf_op jit(solution)/shard_map/ppermute | solution.py:8
  163.6 0.8 copy.10
  (7 shorter events, 0.2 us)
Async XLA Ops:
  1.5 2.4 %collective-permute-start = (f32[1,128,1536]{2,1,0:T(8,128)S(1)}, f32[1,128,1536]{2,1,0:T(8,128)S(1)}, u32[]{:S(2)}, u32[]{:S(2)}) collective-permute-start(f32[1,128,1536]{2,1,0:T(8,128)S(1)} %get-tuple-element.16), channel_id=1, source_target_pairs={{0,2},{2,0},{4,6},{6,4},{8,10},{10,8},{12,14},{14,12},{16,18},{18,... | collective-permute-start | bytes 2359304 | tf_op jit(solution)/shard_map/ppermute | solution.py:8
  4.0 3.9 %copy-start = (f32[128,3072]{1,0:T(8,128)S(1)}, f32[128,3072]{1,0:T(8,128)}, u32[]{:S(2)}) copy-start(f32[128,3072]{1,0:T(8,128)} %param.1) | copy-start | bytes 4718596
  5.0 36.7 %collective-permute-start.1 = (f32[2,128,768]{2,1,0:T(8,128)S(1)}, f32[2,128,768]{2,1,0:T(8,128)S(1)}, u32[]{:S(2)}, u32[]{:S(2)}) collective-permute-start(f32[2,128,768]{2,1,0:T(8,128)S(1)} %get-tuple-element.13), channel_id=1, source_target_pairs={{0,4},{2,6},{4,0},{6,2},{8,12},{10,14},{12,8},{14,10},{16,20},{18,... | collective-permute-start | bytes 2359304 | tf_op jit(solution)/shard_map/ppermute | solution.py:8
  41.7 0.9 copy-start.1
  44.8 36.8 %collective-permute-start.2 = (f32[512,768]{1,0:T(8,128)S(1)}, f32[512,768]{1,0:T(8,128)}, u32[]{:S(2)}, u32[]{:S(2)}) collective-permute-start(f32[512,768]{1,0:T(8,128)S(1)} %bitcast.25), channel_id=1, source_target_pairs={{0,24},{2,26},{4,28},{6,30},{8,0},{10,2},{12,4},{14,6},{16,8},{18,... | collective-permute-start | bytes 4718600 | tf_op jit(solution)/shard_map/ppermute | solution.py:59
  81.6 36.2 %collective-permute-start.3 = (f32[512,768]{1,0:T(8,128)}, f32[512,768]{1,0:T(8,128)}, u32[]{:S(2)}, u32[]{:S(2)}) collective-permute-start(f32[512,768]{1,0:T(8,128)} %collective-permute-done.2), channel_id=1, source_target_pairs={{0,24},{2,26},{4,28},{6,30},{8,0},{10,2},{12,4},{14,6},{16,8},{18,... | collective-permute-start | bytes 4718600 | tf_op jit(solution)/shard_map/ppermute | solution.py:59
  136.5 3.1 %collective-permute-start.4 = (f32[2,128,1152]{2,1,0:T(8,128)}, f32[2,128,1152]{2,1,0:T(8,128)S(1)}, u32[]{:S(2)}, u32[]{:S(2)}) collective-permute-start(f32[2,128,1152]{2,1,0:T(8,128)} %bitcast.6), channel_id=1, source_target_pairs={{0,2},{2,0},{4,6},{6,4},{8,10},{10,8},{12,14},{14,12},{16,18},{18,... | collective-permute-start | bytes 3538952 | tf_op jit(solution)/shard_map/ppermute | solution.py:8
  139.7 15.4 %collective-permute-start.5 = (f32[1,128,1152]{2,1,0:T(8,128)S(1)}, f32[1,128,1152]{2,1,0:T(8,128)S(1)}, u32[]{:S(2)}, u32[]{:S(2)}) collective-permute-start(f32[1,128,1152]{2,1,0:T(8,128)S(1)} %constant_dynamic-slice_fusion), channel_id=1, source_target_pairs={{0,4},{2,6},{4,0},{6,2},{8,12},{10,14},{12,8},{14,10},{16,20},{18,... | collective-permute-start | bytes 1769480 | tf_op jit(solution)/shard_map/ppermute | solution.py:8
  155.2 8.3 %collective-permute-start.6 = (f32[64,1152]{1,0:T(8,128)S(1)}, f32[64,1152]{1,0:T(8,128)S(1)}, u32[]{:S(2)}, u32[]{:S(2)}) collective-permute-start(f32[64,1152]{1,0:T(8,128)S(1)} %dynamic-slice_bitcast_fusion.2), channel_id=1, source_target_pairs={{0,1},{1,0},{2,3},{3,2},{4,5},{5,4},{6,7},{7,6},{8,9},{9,8},{10,11... | collective-permute-start | bytes 884744 | tf_op jit(solution)/shard_map/ppermute | solution.py:8

commit v2 on v0

v2 whole, which is shorter than its diff:
```python
import functools
import jax
import jax.numpy as jnp
from jax import lax
from jax.experimental import pallas as pl
from jax.experimental.pallas import tpu as pltpu
from jax.sharding import PartitionSpec as P


def swap(value, mask):
    return lax.ppermute(value, "blk", [(k, k ^ mask) for k in range(lax.axis_size("blk"))])


def pick(value, index, axis=0):
    return lax.dynamic_index_in_dim(value, index, axis, keepdims=False)


def hop(value, mask, turn):
    shards = lax.axis_size("par")
    pairs = [
        (k * shards + s, (k ^ mask) * shards + (s + turn) % shards)
        for k in range(lax.axis_size("blk"))
        for s in range(shards)
    ]
    return lax.ppermute(value, ("blk", "par"), pairs)


def split(value):
    high = value.astype(jnp.bfloat16)
    return high, (value - high.astype(jnp.float32)).astype(jnp.bfloat16)


def product(left, right):
    def dot(a, b):
        return lax.dot_general(
            a, b, (((1,), (1,)), ((), ())), preferred_element_type=jnp.float32
        )

    return dot(left[0], right[0]) + (dot(left[0], right[1]) + dot(left[1], right[0]))


def pair_kernel(near_l, far_l, near_r, far_r, mean_ref, keep_ref, send_ref):
    mean = mean_ref[...]
    rows = near_l.shape[1]
    shards, part = keep_ref.shape[1], keep_ref.shape[3]

    def centered(ref):
        value = ref[...]
        return split(value.reshape(2 * rows, value.shape[2]) - mean)

    rights = [centered(near_r), centered(far_r)]
    for a, ref in enumerate((near_l, far_l)):
        left = centered(ref)
        for b, right in enumerate(rights):
            block = product(left, right)
            for core, out in enumerate((keep_ref, send_ref)):
                for other in range(2):
                    place = (2 * b + other) ^ (2 * a + core)
                    tile = block[core * rows : (core + 1) * rows, other * rows : (other + 1) * rows]
                    for s in range(shards):
                        out[a, s, place] = tile[s * part : (s + 1) * part]


def pair(left, right, mean, shards):
    _, rows, width = left[0].shape
    shape = jax.ShapeDtypeStruct((2, shards, 4, rows // shards, rows), jnp.float32)
    return pl.pallas_call(
        pair_kernel,
        out_shape=(shape, shape),
        compiler_params=pltpu.CompilerParams(vmem_limit_bytes=40 << 20),
        cost_estimate=pl.CostEstimate(
            flops=6 * 16 * rows * rows * width,
            bytes_accessed=4 * (8 * rows * width + 16 * rows * rows),
            transcendentals=0,
        ),
    )(*left, *right, mean)


def gather_share(keep, send, shard):
    shards = keep.shape[1]
    total = keep + swap(send, 1)
    near, far = total[0], total[1]
    result = pick(near, shard)
    for turn in range(shards):
        to = (shard + turn) % shards
        result = result + hop(pick(far, to), 2, turn)
        if turn:
            result = result + hop(pick(near, to), 0, turn)
    return result


def final_kernel(factor, where_ref, share_ref, out_ref):
    for d in range(out_ref.shape[0]):
        out_ref[d] = share_ref[where_ref[d]] * factor


def on_device(logder):
    nblocks = lax.axis_size("blk")
    nshards = lax.axis_size("par")
    rows, width = logder.shape
    me = lax.axis_index("blk")
    shard = lax.axis_index("par")
    planes = nblocks // 4
    tiles = nblocks // 2 + 1
    factor = 1.0 / (width * nshards)
    half, quarter = width // 2, width // 4
    core, side = me & 1, (me >> 1) & 1

    theirs = swap(lax.dynamic_slice_in_dim(logder, (1 - core) * half, half, 1), 1)

    def both(which):
        mine = lax.dynamic_slice_in_dim(logder, core * half + which * quarter, quarter, 1)
        return jnp.stack([mine, lax.dynamic_slice_in_dim(theirs, which * quarter, quarter, 1)])

    near, away = both(side), both(1 - side)
    far = swap(away, 2)
    sums = jnp.sum(near, axis=(0, 1))[None]
    sums = sums + swap(jnp.sum(away, axis=(0, 1))[None], 2)
    mask = 4
    while mask < nblocks:
        sums = sums + swap(sums, mask)
        mask *= 2
    mean = sums / (rows * nblocks)

    down = [(k, (k - 4) % nblocks) for k in range(nblocks)]
    left = (near, far)
    right = left
    shares = []
    for step in range(planes // 2 + 1):
        keep, send = pair(left, right, mean, nshards)
        shares.append(gather_share(keep, send, shard))
        if step < planes // 2:
            right = tuple(lax.ppermute(value, "blk", down) for value in right)
    share = jnp.concatenate(shares, axis=0)

    place = me % 4
    position = place + jnp.arange(tiles, dtype=jnp.int32)
    where = position - position % 4 + ((position % 4) ^ place)
    out = pl.pallas_call(
        functools.partial(final_kernel, factor),
        out_shape=jax.ShapeDtypeStruct((tiles, rows // nshards, rows), jnp.float32),
        in_specs=[
            pl.BlockSpec(memory_space=pltpu.SMEM),
            pl.BlockSpec(memory_space=pltpu.VMEM),
        ],
    )(where, share)
    return out[None]


def solution(mesh):
    placed = (P("blk", "par"),)
    return jax.shard_map(
        on_device,
        mesh=mesh,
        in_specs=placed,
        out_specs=P("blk", None, "par", None),
        check_vma=False,
    )
```

time: 283 us -> 113 us (0.40)
  waiting for transfers between devices: 142 us -> 67.4 us
  blocking collectives: 63 us -> 0 us
  matrix products: 19.8 us -> 0 us
  between operations: 13.4 us -> 0.23 us
  Pallas kernels: 0 us -> 8.6 us
  local copies, waits for them, and re-layouts: 6.79 us -> 2.31 us
  starting transfers between devices: 32.6 us -> 28.8 us
    psum x1 -> x0, blocking collectives: 63 us -> none  [on_device(): totals = lax.psum(jnp.sum(logder, axis=0), 'blk')]
    ppermute x8 -> x21, waiting for transfers between devices: 125 us -> 67.4 us  [the longest x8 34.8 us: swap(): lax.ppermute(value, 'blk', [(k, k ^ mask) for k in range(lax.axis_size('b...]
    dot_general x9 -> x0, matrix products: 19.8 us -> none  [pair_tile(): lax.dot_general(left, right, (((1,), (1,)), ((), ())), precision=lax.Prec...]
    reduce_scatter x1 -> x0, waiting for transfers between devices: 16.8 us -> none  [on_device(): shares = lax.psum_scatter(stacked, 'par', scatter_dimension=1, tiled=True)]
    pallas_call x0 -> x4, Pallas kernels: none -> 8.6 us  [the longest x3 6.85 us: pair(): pl.pallas_call(pair_kernel, out_shape=(shape, shape), compiler_params=plt...]
    another operation x4 -> x0, local copies, waits for them, and re-layouts: 5.63 us -> none
    add x0 -> x9, other arithmetic: none -> 3.94 us  [the longest x3 2.27 us: gather_share(): total = keep + swap(send, 1)]
    ppermute x8 -> x21, starting transfers between devices: 32.6 us -> 28.8 us  [the longest x9 12.6 us: hop(): return lax.ppermute(value, ('blk', 'par'), pairs)]
  transfers between devices with their start and end apart: 9 -> 21, of which waited for: 9 -> 10; matrix products, arithmetic and copies ran while one was open for 7% -> 4% of each run, Pallas kernels for 0% -> 6%
where the time goes in v2:
time: 113 us; the launch traced here: 112 us
  waiting for transfers between devices  67.4 us (60%)
  starting transfers between devices  28.8 us (25%)
  Pallas kernels  8.6 us (8%)
  other arithmetic  4.98 us (4%)
  local copies, waits for them, and re-layouts  2.31 us (2%)
    ppermute x8, waiting for transfers between devices, swap(): lax.ppermute(value, 'blk', [(k, k ^ mask) for k in range(lax.axis_size('b...  34.8 us
    ppermute x4, waiting for transfers between devices, on_device(): right = tuple((lax.ppermute(value, 'blk', down) for value in right))  25.2 us
    ppermute x9, starting transfers between devices, hop(): return lax.ppermute(value, ('blk', 'par'), pairs)  12.6 us
    ppermute x4, starting transfers between devices, on_device(): right = tuple((lax.ppermute(value, 'blk', down) for value in right))  10.9 us
    ppermute x9, waiting for transfers between devices, hop(): return lax.ppermute(value, ('blk', 'par'), pairs)  7.29 us
    pallas_call x3, Pallas kernels, pair(): pl.pallas_call(pair_kernel, out_shape=(shape, shape), compiler_params=plt...  6.85 us
    ppermute x8, starting transfers between devices, swap(): lax.ppermute(value, 'blk', [(k, k ^ mask) for k in range(lax.axis_size('b...  5.32 us
    add x3, other arithmetic, gather_share(): total = keep + swap(send, 1)  2.27 us
  transfers between devices with their start and end apart: 21, of which 10 were waited for; matrix products, arithmetic and copies ran while one was open for 4% of the time, Pallas kernels for 6%

profile of v2, /device:TPU:0, one launch (start us, length us, event | category | flops | bytes accessed | tf_op | source)
XLA Modules:
  0.0 112.3 jit_solution(107888086156924852)
XLA Ops:
  0.0 0.0 copy-start
  0.0 1.3 %constant_dynamic-slice_fusion = f32[128,1536]{1,0:T(8,128)S(1)} fusion(f32[128,3072]{1,0:T(8,128)} %param.1, s32[]{:T(128)S(6)} %select_n.68), kind=kLoop, calls=%fused_computation.29 | loop fusion | bytes 1572868 | tf_op jit(solution)/shard_map/dynamic_slice | solution.py:109
  1.3 0.5 collective-permute-start
  1.8 0.0 copy-done
  1.8 0.1 dynamic-slice_reduce_fusion.3
  1.9 1.8 %collective-permute-done = f32[128,1536]{1,0:T(8,128)S(1)} collective-permute-done((f32[128,1536]{1,0:T(8,128)S(1)}, f32[128,1536]{1,0:T(8,128)S(1)}, u32[]{:S(2)}, u32[]{:S(2)}) %collective-permute-start) | collective-permute-done | bytes 786464 | tf_op jit(solution)/shard_map/ppermute | solution.py:11
  3.7 0.1 dynamic-slice_reduce_fusion.2
  3.8 0.1 pad_maximum_fusion.1
  3.9 3.0 %collective-permute-start.1 = (f32[2,128,768]{2,1,0:T(8,128)S(1)}, f32[2,128,768]{2,1,0:T(8,128)S(1)}, u32[]{:S(2)}, u32[]{:S(2)}) collective-permute-start(f32[2,128,768]{2,1,0:T(8,128)S(1)} %pad_maximum_fusion.1), channel_id=1, source_target_pairs={{0,4},{2,6},{4,0},{6,2},{8,12},{10,14},{12,8},{14,10},{16,20},{18,... | collective-permute-start | bytes 2359304 | tf_op jit(solution)/shard_map/ppermute | solution.py:11
  6.8 0.1 collective-permute-start.2
  6.9 0.1 pad_maximum_fusion.near_l.near_r
  7.0 4.1 %collective-permute-start.9 = (f32[2,128,768]{2,1,0:T(8,128)S(1)}, f32[2,128,768]{2,1,0:T(8,128)}, u32[]{:S(2)}, u32[]{:S(2)}) collective-permute-start(f32[2,128,768]{2,1,0:T(8,128)S(1)} %pad_maximum_fusion.near_l.near_r), channel_id=1, source_target_pairs={{0,24},{2,26},{4,28},{6,30},{8,0},{10,2},{12,4},{14,6},{16,8},{18,... | collective-permute-start | bytes 2359304 | tf_op jit(solution)/shard_map/ppermute | solution.py:133
  11.1 13.6 %collective-permute-done.1.far_l.far_r = f32[2,128,768]{2,1,0:T(8,128)S(1)} collective-permute-done((f32[2,128,768]{2,1,0:T(8,128)S(1)}, f32[2,128,768]{2,1,0:T(8,128)S(1)}, u32[]{:S(2)}, u32[]{:S(2)}) %collective-permute-start.1) | collective-permute-done | bytes 786464 | tf_op jit(solution)/shard_map/ppermute | solution.py:11
  24.7 3.8 %collective-permute-start.10 = (f32[2,128,768]{2,1,0:T(8,128)S(1)}, f32[2,128,768]{2,1,0:T(8,128)S(1)}, u32[]{:S(2)}, u32[]{:S(2)}) collective-permute-start(f32[2,128,768]{2,1,0:T(8,128)S(1)} %collective-permute-done.1.far_l.far_r), channel_id=1, source_target_pairs={{0,24},{2,26},{4,28},{6,30},{8,0},{10,2},{12,4},{14,6},{16,8},{18,... | collective-permute-start | bytes 2359304 | tf_op jit(solution)/shard_map/ppermute | solution.py:133
  28.5 0.0 collective-permute-done.2
  28.5 0.1 collective-permute-start.3
  28.6 16.3 %collective-permute-done.3 = f32[1,768]{1,0:T(1,128)S(1)} collective-permute-done((f32[1,768]{1,0:T(1,128)S(1)}, f32[1,768]{1,0:T(1,128)S(1)}, u32[]{:S(2)}, u32[]{:S(2)}) %collective-permute-start.3) | collective-permute-done | bytes 3104 | tf_op jit(solution)/shard_map/ppermute | solution.py:11
  44.9 1.5 %collective-permute-start.4 = (f32[1,768]{1,0:T(1,128)S(1)}, f32[1,768]{1,0:T(1,128)S(1)}, u32[]{:S(2)}, u32[]{:S(2)}) collective-permute-start(f32[1,768]{1,0:T(1,128)S(1)} %add.134), channel_id=1, source_target_pairs={{0,16},{2,18},{4,20},{6,22},{8,24},{10,26},{12,28},{14,30},{16,0},... | collective-permute-start | bytes 9224 | tf_op jit(solution)/shard_map/ppermute | solution.py:11
  46.4 3.0 %collective-permute-done.4 = f32[1,768]{1,0:T(1,128)S(1)} collective-permute-done((f32[1,768]{1,0:T(1,128)S(1)}, f32[1,768]{1,0:T(1,128)S(1)}, u32[]{:S(2)}, u32[]{:S(2)}) %collective-permute-start.4) | collective-permute-done | bytes 3104 | tf_op jit(solution)/shard_map/ppermute | solution.py:11
  49.4 1.5 %shard_map.17 = (f32[2,2,4,64,128]{4,3,2,1,0:T(8,128)S(1)}, f32[2,2,4,64,128]{4,3,2,1,0:T(8,128)S(1)}) custom-call(f32[2,128,768]{2,1,0:T(8,128)S(1)} %pad_maximum_fusion.near_l.near_r, f32[2,128,768]{2,1,0:T(8,128)S(1)} %collective-permute-done.1.far_l.far_r, f32[2,128,768]{2,1,0:T(8,128)S(1)} %pad_maximum_fusion.near_l.near_r, ...), custom_call_target="tpu_custom_call" | custom-call | flops 1207959552 | bytes 4194304 | tf_op jit(solution)/shard_map/pallas_call | solution.py:67
  50.9 0.1 collective-permute-start.5
  51.0 0.0 collective-permute-done.9.near_r
  51.0 2.0 %collective-permute-start.15 = (f32[2,128,768]{2,1,0:T(8,128)}, f32[2,128,768]{2,1,0:T(8,128)}, u32[]{:S(2)}, u32[]{:S(2)}) collective-permute-start(f32[2,128,768]{2,1,0:T(8,128)} %collective-permute-done.9.near_r), channel_id=1, source_target_pairs={{0,24},{2,26},{4,28},{6,30},{8,0},{10,2},{12,4},{14,6},{16,8},{18,... | collective-permute-start | bytes 2359304 | tf_op jit(solution)/shard_map/ppermute | solution.py:133
  53.0 0.0 collective-permute-done.10.far_r
  53.0 1.0 collective-permute-start.16
  54.0 0.0 collective-permute-done.5
  54.0 1.1 add.136
  55.1 0.0 copy-start.1
  55.2 0.8 dynamic-slice_bitcast_fusion.12
  55.9 1.5 %collective-permute-start.6 = (f32[4,64,128]{2,1,0:T(8,128)}, f32[4,64,128]{2,1,0:T(8,128)}, u32[]{:S(2)}, u32[]{:S(2)}) collective-permute-start(f32[4,64,128]{2,1,0:T(8,128)} %get-tuple-element.31), channel_id=1, source_target_pairs={{0,4},{1,5},{2,6},{3,7},{4,0},{5,1},{6,2},{7,3},{8,12},{9,13},{10,... | collective-permute-start | bytes 393224 | tf_op jit(solution)/shard_map/ppermute | solution.py:25
  57.4 1.5 %collective-permute-start.7 = (f32[4,64,128]{2,1,0:T(8,128)}, f32[4,64,128]{2,1,0:T(8,128)}, u32[]{:S(2)}, u32[]{:S(2)}) collective-permute-start(f32[4,64,128]{2,1,0:T(8,128)} %get-tuple-element.32), channel_id=1, source_target_pairs={{0,5},{1,4},{2,7},{3,6},{4,1},{5,0},{6,3},{7,2},{8,13},{9,12},{10,... | collective-permute-start | bytes 393224 | tf_op jit(solution)/shard_map/ppermute | solution.py:25
  58.9 2.6 %shard_map.18 = (f32[2,2,4,64,128]{4,3,2,1,0:T(8,128)S(1)}, f32[2,2,4,64,128]{4,3,2,1,0:T(8,128)S(1)}) custom-call(f32[2,128,768]{2,1,0:T(8,128)S(1)} %pad_maximum_fusion.near_l.near_r, f32[2,128,768]{2,1,0:T(8,128)S(1)} %collective-permute-done.1.far_l.far_r, f32[2,128,768]{2,1,0:T(8,128)} %collective-permute-done.9.near_r, ...), custom_call_target="tpu_custom_call" | custom-call | flops 1207959552 | bytes 4194304 | tf_op jit(solution)/shard_map/pallas_call | solution.py:67
  61.5 0.1 collective-permute-start.11
  61.6 0.0 copy-done.1
  61.6 10.7 %collective-permute-done.15.near_r = f32[2,128,768]{2,1,0:T(8,128)} collective-permute-done((f32[2,128,768]{2,1,0:T(8,128)}, f32[2,128,768]{2,1,0:T(8,128)}, u32[]{:S(2)}, u32[]{:S(2)}) %collective-permute-start.15) | collective-permute-done | bytes 786464 | tf_op jit(solution)/shard_map/ppermute | solution.py:133
  72.2 1.5 %collective-permute-start.8 = (f32[4,64,128]{2,1,0:T(8,128)S(1)}, f32[4,64,128]{2,1,0:T(8,128)}, u32[]{:S(2)}, u32[]{:S(2)}) collective-permute-start(f32[4,64,128]{2,1,0:T(8,128)S(1)} %dynamic-slice_bitcast_fusion.10), channel_id=1, source_target_pairs={{0,1},{1,0},{2,3},{3,2},{4,5},{5,4},{6,7},{7,6},{8,9},{9,8},{10,11... | collective-permute-start | bytes 393224 | tf_op jit(solution)/shard_map/ppermute | solution.py:25
  73.7 0.5 xor_add_fusion.where_ref
  74.3 0.0 copy-start.2
  74.3 14.6 %collective-permute-done.16.far_r = f32[2,128,768]{2,1,0:T(8,128)} collective-permute-done((f32[2,128,768]{2,1,0:T(8,128)S(1)}, f32[2,128,768]{2,1,0:T(8,128)}, u32[]{:S(2)}, u32[]{:S(2)}) %collective-permute-start.16) | collective-permute-done | bytes 786464 | tf_op jit(solution)/shard_map/ppermute | solution.py:133
  88.8 2.8 %shard_map.19 = (f32[2,2,4,64,128]{4,3,2,1,0:T(8,128)S(1)}, f32[2,2,4,64,128]{4,3,2,1,0:T(8,128)S(1)}) custom-call(f32[2,128,768]{2,1,0:T(8,128)S(1)} %pad_maximum_fusion.near_l.near_r, f32[2,128,768]{2,1,0:T(8,128)S(1)} %collective-permute-done.1.far_l.far_r, f32[2,128,768]{2,1,0:T(8,128)} %collective-permute-done.15.near_r, ...), custom_call_target="tpu_custom_call" | custom-call | flops 1207959552 | bytes 4194304 | tf_op jit(solution)/shard_map/pallas_call | solution.py:67
  91.7 0.1 collective-permute-start.17
  91.7 0.0 collective-permute-done.6
  91.8 0.0 collective-permute-done.7
  91.8 0.0 collective-permute-done.8
  91.8 0.0 copy-done.2
  91.8 1.1 fusion.5
  92.9 0.0 collective-permute-done.11
  92.9 1.1 add.146
  94.1 1.6 %collective-permute-start.12 = (f32[4,64,128]{2,1,0:T(8,128)S(1)}, f32[4,64,128]{2,1,0:T(8,128)S(1)}, u32[]{:S(2)}, u32[]{:S(2)}) collective-permute-start(f32[4,64,128]{2,1,0:T(8,128)S(1)} %get-tuple-element.33), channel_id=1, source_target_pairs={{0,4},{1,5},{2,6},{3,7},{4,0},{5,1},{6,2},{7,3},{8,12},{9,13},{10,... | collective-permute-start | bytes 393224 | tf_op jit(solution)/shard_map/ppermute | solution.py:25
  95.6 1.5 %collective-permute-start.13 = (f32[4,64,128]{2,1,0:T(8,128)S(1)}, f32[4,64,128]{2,1,0:T(8,128)S(1)}, u32[]{:S(2)}, u32[]{:S(2)}) collective-permute-start(f32[4,64,128]{2,1,0:T(8,128)S(1)} %get-tuple-element.34), channel_id=1, source_target_pairs={{0,5},{1,4},{2,7},{3,6},{4,1},{5,0},{6,3},{7,2},{8,13},{9,12},{10,... | collective-permute-start | bytes 393224 | tf_op jit(solution)/shard_map/ppermute | solution.py:25
  97.1 0.6 collective-permute-start.14
  97.7 0.0 collective-permute-done.17
  97.7 0.1 add.150
  97.9 1.6 %collective-permute-start.18 = (f32[4,64,128]{2,1,0:T(8,128)S(1)}, f32[4,64,128]{2,1,0:T(8,128)S(1)}, u32[]{:S(2)}, u32[]{:S(2)}) collective-permute-start(f32[4,64,128]{2,1,0:T(8,128)S(1)} %get-tuple-element.35), channel_id=1, source_target_pairs={{0,4},{1,5},{2,6},{3,7},{4,0},{5,1},{6,2},{7,3},{8,12},{9,13},{10,... | collective-permute-start | bytes 393224 | tf_op jit(solution)/shard_map/ppermute | solution.py:25
  99.4 1.5 %collective-permute-start.19 = (f32[4,64,128]{2,1,0:T(8,128)S(1)}, f32[4,64,128]{2,1,0:T(8,128)S(1)}, u32[]{:S(2)}, u32[]{:S(2)}) collective-permute-start(f32[4,64,128]{2,1,0:T(8,128)S(1)} %get-tuple-element.36), channel_id=1, source_target_pairs={{0,5},{1,4},{2,7},{3,6},{4,1},{5,0},{6,3},{7,2},{8,13},{9,12},{10,... | collective-permute-start | bytes 393224 | tf_op jit(solution)/shard_map/ppermute | solution.py:25
  100.9 2.3 %collective-permute-done.12 = f32[4,64,128]{2,1,0:T(8,128)S(1)} collective-permute-done((f32[4,64,128]{2,1,0:T(8,128)S(1)}, f32[4,64,128]{2,1,0:T(8,128)S(1)}, u32[]{:S(2)}, u32[]{:S(2)}) %collective-permute-start.12) | collective-permute-done | bytes 131104 | tf_op jit(solution)/shard_map/ppermute | solution.py:25
  103.2 1.5 %collective-permute-start.20 = (f32[4,64,128]{2,1,0:T(8,128)S(1)}, f32[4,64,128]{2,1,0:T(8,128)S(1)}, u32[]{:S(2)}, u32[]{:S(2)}) collective-permute-start(f32[4,64,128]{2,1,0:T(8,128)S(1)} %dynamic-slice_bitcast_fusion.4), channel_id=1, source_target_pairs={{0,1},{1,0},{2,3},{3,2},{4,5},{5,4},{6,7},{7,6},{8,9},{9,8},{10,11... | collective-permute-start | bytes 393224 | tf_op jit(solution)/shard_map/ppermute | solution.py:25
  104.7 0.0 collective-permute-done.13
  104.7 0.0 collective-permute-done.14
  104.8 3.5 %collective-permute-done.18 = f32[4,64,128]{2,1,0:T(8,128)S(1)} collective-permute-done((f32[4,64,128]{2,1,0:T(8,128)S(1)}, f32[4,64,128]{2,1,0:T(8,128)S(1)}, u32[]{:S(2)}, u32[]{:S(2)}) %collective-permute-start.18) | collective-permute-done | bytes 131104 | tf_op jit(solution)/shard_map/ppermute | solution.py:25
  108.3 0.3 collective-permute-done.19
  108.6 1.1 %collective-permute-done.20 = f32[4,64,128]{2,1,0:T(8,128)S(1)} collective-permute-done((f32[4,64,128]{2,1,0:T(8,128)S(1)}, f32[4,64,128]{2,1,0:T(8,128)S(1)}, u32[]{:S(2)}, u32[]{:S(2)}) %collective-permute-start.20) | collective-permute-done | bytes 131104 | tf_op jit(solution)/shard_map/ppermute | solution.py:25
  109.7 0.8 pad_maximum_fusion.2.share_ref
  110.5 1.7 %shard_map.20 = f32[9,64,128]{2,1,0:T(8,128)} custom-call(s32[9]{0:T(128)} %xor_add_fusion.where_ref, f32[12,64,128]{2,1,0:T(8,128)} %pad_maximum_fusion.2.share_ref), custom_call_target="tpu_custom_call" | custom-call | tf_op jit(solution)/shard_map/pallas_call | solution.py:139
  (16 shorter events, 0.3 us)
Async XLA Ops:
  0.0 1.8 %copy-start = (f32[128,3072]{1,0:T(8,128)S(1)}, f32[128,3072]{1,0:T(8,128)}, u32[]{:S(2)}) copy-start(f32[128,3072]{1,0:T(8,128)} %param.1) | copy-start | bytes 4718596
  1.3 2.4 %collective-permute-start = (f32[128,1536]{1,0:T(8,128)S(1)}, f32[128,1536]{1,0:T(8,128)S(1)}, u32[]{:S(2)}, u32[]{:S(2)}) collective-permute-start(f32[128,1536]{1,0:T(8,128)S(1)} %constant_dynamic-slice_fusion), channel_id=1, source_target_pairs={{0,2},{2,0},{4,6},{6,4},{8,10},{10,8},{12,14},{14,12},{16,18},{18,... | collective-permute-start | bytes 2359304 | tf_op jit(solution)/shard_map/ppermute | solution.py:11
  3.9 20.8 %collective-permute-start.1 = (f32[2,128,768]{2,1,0:T(8,128)S(1)}, f32[2,128,768]{2,1,0:T(8,128)S(1)}, u32[]{:S(2)}, u32[]{:S(2)}) collective-permute-start(f32[2,128,768]{2,1,0:T(8,128)S(1)} %pad_maximum_fusion.1), channel_id=1, source_target_pairs={{0,4},{2,6},{4,0},{6,2},{8,12},{10,14},{12,8},{14,10},{16,20},{18,... | collective-permute-start | bytes 2359304 | tf_op jit(solution)/shard_map/ppermute | solution.py:11
  6.8 21.7 %collective-permute-start.2 = (f32[1,768]{1,0:T(1,128)S(1)}, f32[1,768]{1,0:T(1,128)S(1)}, u32[]{:S(2)}, u32[]{:S(2)}) collective-permute-start(f32[1,768]{1,0:T(1,128)S(1)} %reduce_sum.59), channel_id=1, source_target_pairs={{0,4},{2,6},{4,0},{6,2},{8,12},{10,14},{12,8},{14,10},{16,20},{18,... | collective-permute-start | bytes 9224 | tf_op jit(solution)/shard_map/ppermute | solution.py:11
  7.0 44.0 %collective-permute-start.9 = (f32[2,128,768]{2,1,0:T(8,128)S(1)}, f32[2,128,768]{2,1,0:T(8,128)}, u32[]{:S(2)}, u32[]{:S(2)}) collective-permute-start(f32[2,128,768]{2,1,0:T(8,128)S(1)} %pad_maximum_fusion.near_l.near_r), channel_id=1, source_target_pairs={{0,24},{2,26},{4,28},{6,30},{8,0},{10,2},{12,4},{14,6},{16,8},{18,... | collective-permute-start | bytes 2359304 | tf_op jit(solution)/shard_map/ppermute | solution.py:133
  24.7 28.3 %collective-permute-start.10 = (f32[2,128,768]{2,1,0:T(8,128)S(1)}, f32[2,128,768]{2,1,0:T(8,128)S(1)}, u32[]{:S(2)}, u32[]{:S(2)}) collective-permute-start(f32[2,128,768]{2,1,0:T(8,128)S(1)} %collective-permute-done.1.far_l.far_r), channel_id=1, source_target_pairs={{0,24},{2,26},{4,28},{6,30},{8,0},{10,2},{12,4},{14,6},{16,8},{18,... | collective-permute-start | bytes 2359304 | tf_op jit(solution)/shard_map/ppermute | solution.py:133
  28.5 16.4 %collective-permute-start.3 = (f32[1,768]{1,0:T(1,128)S(1)}, f32[1,768]{1,0:T(1,128)S(1)}, u32[]{:S(2)}, u32[]{:S(2)}) collective-permute-start(f32[1,768]{1,0:T(1,128)S(1)} %reshape_add_fusion), channel_id=1, source_target_pairs={{0,8},{2,10},{4,12},{6,14},{8,0},{10,2},{12,4},{14,6},{16,24},{18,... | collective-permute-start | bytes 9224 | tf_op jit(solution)/shard_map/ppermute | solution.py:11
  44.9 4.5 %collective-permute-start.4 = (f32[1,768]{1,0:T(1,128)S(1)}, f32[1,768]{1,0:T(1,128)S(1)}, u32[]{:S(2)}, u32[]{:S(2)}) collective-permute-start(f32[1,768]{1,0:T(1,128)S(1)} %add.134), channel_id=1, source_target_pairs={{0,16},{2,18},{4,20},{6,22},{8,24},{10,26},{12,28},{14,30},{16,0},... | collective-permute-start | bytes 9224 | tf_op jit(solution)/shard_map/ppermute | solution.py:11
  50.9 3.1 %collective-permute-start.5 = (f32[2,2,4,64,128]{4,3,2,1,0:T(8,128)S(1)}, f32[2,2,4,64,128]{4,3,2,1,0:T(8,128)}, u32[]{:S(2)}, u32[]{:S(2)}) collective-permute-start(f32[2,2,4,64,128]{4,3,2,1,0:T(8,128)S(1)} %get-tuple-element.12), channel_id=1, source_target_pairs={{0,2},{2,0},{4,6},{6,4},{8,10},{10,8},{12,14},{14,12},{16,18},{18,... | collective-permute-start | bytes 1572872 | tf_op jit(solution)/shard_map/ppermute | solution.py:11
  51.0 21.2 %collective-permute-start.15 = (f32[2,128,768]{2,1,0:T(8,128)}, f32[2,128,768]{2,1,0:T(8,128)}, u32[]{:S(2)}, u32[]{:S(2)}) collective-permute-start(f32[2,128,768]{2,1,0:T(8,128)} %collective-permute-done.9.near_r), channel_id=1, source_target_pairs={{0,24},{2,26},{4,28},{6,30},{8,0},{10,2},{12,4},{14,6},{16,8},{18,... | collective-permute-start | bytes 2359304 | tf_op jit(solution)/shard_map/ppermute | solution.py:133
  53.0 35.9 %collective-permute-start.16 = (f32[2,128,768]{2,1,0:T(8,128)S(1)}, f32[2,128,768]{2,1,0:T(8,128)}, u32[]{:S(2)}, u32[]{:S(2)}) collective-permute-start(f32[2,128,768]{2,1,0:T(8,128)S(1)} %collective-permute-done.10.far_r), channel_id=1, source_target_pairs={{0,24},{2,26},{4,28},{6,30},{8,0},{10,2},{12,4},{14,6},{16,8},{18,... | collective-permute-start | bytes 2359304 | tf_op jit(solution)/shard_map/ppermute | solution.py:133
  55.1 6.4 %copy-start.1 = (f32[1,2,4,64,128]{4,3,2,1,0:T(8,128)}, f32[1,2,4,64,128]{4,3,2,1,0:T(8,128)S(1)}, u32[]{:S(2)}) copy-start(f32[1,2,4,64,128]{4,3,2,1,0:T(8,128)S(1)} %get-tuple-element.26) | copy-start | bytes 786436
  55.9 35.8 %collective-permute-start.6 = (f32[4,64,128]{2,1,0:T(8,128)}, f32[4,64,128]{2,1,0:T(8,128)}, u32[]{:S(2)}, u32[]{:S(2)}) collective-permute-start(f32[4,64,128]{2,1,0:T(8,128)} %get-tuple-element.31), channel_id=1, source_target_pairs={{0,4},{1,5},{2,6},{3,7},{4,0},{5,1},{6,2},{7,3},{8,12},{9,13},{10,... | collective-permute-start | bytes 393224 | tf_op jit(solution)/shard_map/ppermute | solution.py:25
  57.4 34.3 %collective-permute-start.7 = (f32[4,64,128]{2,1,0:T(8,128)}, f32[4,64,128]{2,1,0:T(8,128)}, u32[]{:S(2)}, u32[]{:S(2)}) collective-permute-start(f32[4,64,128]{2,1,0:T(8,128)} %get-tuple-element.32), channel_id=1, source_target_pairs={{0,5},{1,4},{2,7},{3,6},{4,1},{5,0},{6,3},{7,2},{8,13},{9,12},{10,... | collective-permute-start | bytes 393224 | tf_op jit(solution)/shard_map/ppermute | solution.py:25
  61.5 31.4 %collective-permute-start.11 = (f32[2,2,4,64,128]{4,3,2,1,0:T(8,128)S(1)}, f32[2,2,4,64,128]{4,3,2,1,0:T(8,128)}, u32[]{:S(2)}, u32[]{:S(2)}) collective-permute-start(f32[2,2,4,64,128]{4,3,2,1,0:T(8,128)S(1)} %get-tuple-element.14), channel_id=1, source_target_pairs={{0,2},{2,0},{4,6},{6,4},{8,10},{10,8},{12,14},{14,12},{16,18},{18,... | collective-permute-start | bytes 1572872 | tf_op jit(solution)/shard_map/ppermute | solution.py:11
  72.2 19.5 %collective-permute-start.8 = (f32[4,64,128]{2,1,0:T(8,128)S(1)}, f32[4,64,128]{2,1,0:T(8,128)}, u32[]{:S(2)}, u32[]{:S(2)}) collective-permute-start(f32[4,64,128]{2,1,0:T(8,128)S(1)} %dynamic-slice_bitcast_fusion.10), channel_id=1, source_target_pairs={{0,1},{1,0},{2,3},{3,2},{4,5},{5,4},{6,7},{7,6},{8,9},{9,8},{10,11... | collective-permute-start | bytes 393224 | tf_op jit(solution)/shard_map/ppermute | solution.py:25
  74.3 17.5 %copy-start.2 = (f32[1,2,4,64,128]{4,3,2,1,0:T(8,128)S(1)}, f32[1,2,4,64,128]{4,3,2,1,0:T(8,128)}, u32[]{:S(2)}) copy-start(f32[1,2,4,64,128]{4,3,2,1,0:T(8,128)} %copy-done.1) | copy-start | bytes 786436
  91.7 6.0 %collective-permute-start.17 = (f32[2,2,4,64,128]{4,3,2,1,0:T(8,128)S(1)}, f32[2,2,4,64,128]{4,3,2,1,0:T(8,128)S(1)}, u32[]{:S(2)}, u32[]{:S(2)}) collective-permute-start(f32[2,2,4,64,128]{4,3,2,1,0:T(8,128)S(1)} %get-tuple-element.16), channel_id=1, source_target_pairs={{0,2},{2,0},{4,6},{6,4},{8,10},{10,8},{12,14},{14,12},{16,18},{18,... | collective-permute-start | bytes 1572872 | tf_op jit(solution)/shard_map/ppermute | solution.py:11
  94.1 9.2 %collective-permute-start.12 = (f32[4,64,128]{2,1,0:T(8,128)S(1)}, f32[4,64,128]{2,1,0:T(8,128)S(1)}, u32[]{:S(2)}, u32[]{:S(2)}) collective-permute-start(f32[4,64,128]{2,1,0:T(8,128)S(1)} %get-tuple-element.33), channel_id=1, source_target_pairs={{0,4},{1,5},{2,6},{3,7},{4,0},{5,1},{6,2},{7,3},{8,12},{9,13},{10,... | collective-permute-start | bytes 393224 | tf_op jit(solution)/shard_map/ppermute | solution.py:25
  95.6 9.1 %collective-permute-start.13 = (f32[4,64,128]{2,1,0:T(8,128)S(1)}, f32[4,64,128]{2,1,0:T(8,128)S(1)}, u32[]{:S(2)}, u32[]{:S(2)}) collective-permute-start(f32[4,64,128]{2,1,0:T(8,128)S(1)} %get-tuple-element.34), channel_id=1, source_target_pairs={{0,5},{1,4},{2,7},{3,6},{4,1},{5,0},{6,3},{7,2},{8,13},{9,12},{10,... | collective-permute-start | bytes 393224 | tf_op jit(solution)/shard_map/ppermute | solution.py:25
  97.1 7.7 %collective-permute-start.14 = (f32[4,64,128]{2,1,0:T(8,128)S(1)}, f32[4,64,128]{2,1,0:T(8,128)S(1)}, u32[]{:S(2)}, u32[]{:S(2)}) collective-permute-start(f32[4,64,128]{2,1,0:T(8,128)S(1)} %dynamic-slice_bitcast_fusion.7), channel_id=1, source_target_pairs={{0,1},{1,0},{2,3},{3,2},{4,5},{5,4},{6,7},{7,6},{8,9},{9,8},{10,11... | collective-permute-start | bytes 393224 | tf_op jit(solution)/shard_map/ppermute | solution.py:25
  97.9 10.4 %collective-permute-start.18 = (f32[4,64,128]{2,1,0:T(8,128)S(1)}, f32[4,64,128]{2,1,0:T(8,128)S(1)}, u32[]{:S(2)}, u32[]{:S(2)}) collective-permute-start(f32[4,64,128]{2,1,0:T(8,128)S(1)} %get-tuple-element.35), channel_id=1, source_target_pairs={{0,4},{1,5},{2,6},{3,7},{4,0},{5,1},{6,2},{7,3},{8,12},{9,13},{10,... | collective-permute-start | bytes 393224 | tf_op jit(solution)/shard_map/ppermute | solution.py:25
  99.4 9.1 %collective-permute-start.19 = (f32[4,64,128]{2,1,0:T(8,128)S(1)}, f32[4,64,128]{2,1,0:T(8,128)S(1)}, u32[]{:S(2)}, u32[]{:S(2)}) collective-permute-start(f32[4,64,128]{2,1,0:T(8,128)S(1)} %get-tuple-element.36), channel_id=1, source_target_pairs={{0,5},{1,4},{2,7},{3,6},{4,1},{5,0},{6,3},{7,2},{8,13},{9,12},{10,... | collective-permute-start | bytes 393224 | tf_op jit(solution)/shard_map/ppermute | solution.py:25
  103.2 6.5 %collective-permute-start.20 = (f32[4,64,128]{2,1,0:T(8,128)S(1)}, f32[4,64,128]{2,1,0:T(8,128)S(1)}, u32[]{:S(2)}, u32[]{:S(2)}) collective-permute-start(f32[4,64,128]{2,1,0:T(8,128)S(1)} %dynamic-slice_bitcast_fusion.4), channel_id=1, source_target_pairs={{0,1},{1,0},{2,3},{3,2},{4,5},{5,4},{6,7},{7,6},{8,9},{9,8},{10,11... | collective-permute-start | bytes 393224 | tf_op jit(solution)/shard_map/ppermute | solution.py:25

commit v3 on v0

v3 whole, which is shorter than its diff:
```python
import functools
import jax
import jax.numpy as jnp
from jax import lax
from jax.experimental import pallas as pl
from jax.experimental.pallas import tpu as pltpu
from jax.sharding import PartitionSpec as P


def swap(value, mask):
    return lax.ppermute(value, "blk", [(k, k ^ mask) for k in range(lax.axis_size("blk"))])


def shift(value, steps):
    count = lax.axis_size("blk")
    return lax.ppermute(value, "blk", [(k, (k + steps) % count) for k in range(count)])


def hop(value, mask, turn):
    shards = lax.axis_size("par")
    pairs = [
        (k * shards + s, (k ^ mask) * shards + (s + turn) % shards)
        for k in range(lax.axis_size("blk"))
        for s in range(shards)
    ]
    return lax.ppermute(value, ("blk", "par"), pairs)


def pick(value, index, axis=0):
    return lax.dynamic_index_in_dim(value, index, axis, keepdims=False)


def split(value):
    high = value.astype(jnp.bfloat16)
    return high, (value - high.astype(jnp.float32)).astype(jnp.bfloat16)


def product(left, right):
    def dot(a, b):
        return lax.dot_general(
            a, b, (((1,), (1,)), ((), ())), preferred_element_type=jnp.float32
        )

    return dot(left[0], right[0]) + (dot(left[0], right[1]) + dot(left[1], right[0]))


def store(block, out_refs, a, b, first):
    keep_ref = out_refs[0]
    shards, part, rows = keep_ref.shape[1], keep_ref.shape[3], keep_ref.shape[4]
    for core, out in enumerate(out_refs):
        for other in range(2):
            place = first + ((2 * b + other) ^ (2 * a + core))
            tile = block[core * rows : (core + 1) * rows, other * rows : (other + 1) * rows]
            for s in range(shards):
                out[a, s, place] = tile[s * part : (s + 1) * part]


def centered(ref, mean):
    value = ref[...]
    return split(value.reshape(value.shape[0] * value.shape[1], value.shape[2]) - mean)


def own_kernel(near0, far0, near1, far1, mean_ref, keep_ref, send_ref, high_ref, low_ref):
    sides = []
    for chunk, refs in enumerate(((near0, far0), (near1, far1))):
        for a, ref in enumerate(refs):
            high, low = centered(ref, mean_ref[chunk])
            high_ref[chunk, a], low_ref[chunk, a] = high, low
            sides.append((high, low))
    for a in range(2):
        for b in range(2):
            block = product(sides[a], sides[b]) + product(sides[2 + a], sides[2 + b])
            store(block, (keep_ref, send_ref), a, b, 0)


def pair_kernel(columns, flag_ref, mean_ref, high_ref, low_ref, *refs):
    out_refs = refs[-2:]
    flag = flag_ref[0]
    if len(refs) > 2 * len(columns) + 2:
        for old, new in zip(refs[-4:-2], out_refs):
            for a in range(2):
                for place in range(4):
                    if (place ^ (2 * a)) // 2 not in columns:
                        new[a, :, place] = old[a, :, place]
    for position, b in enumerate(columns):
        rights = [
            centered(refs[2 * position + chunk], mean_ref[chunk ^ flag]) for chunk in range(2)
        ]
        for a in range(2):
            block = None
            for chunk in range(2):
                at = chunk ^ flag
                term = product((high_ref[at, a], low_ref[at, a]), rights[chunk])
                block = term if block is None else block + term
            store(block, out_refs, a, b, 0)


def half_kernel(mean_ref, high_ref, low_ref, near_ref, far_ref, keep_ref, send_ref):
    lefts = [(high_ref[1, a], low_ref[1, a]) for a in range(2)]
    rights = [centered(ref, mean_ref[1]) for ref in (near_ref, far_ref)]
    for a in range(2):
        for b in range(2):
            store(product(lefts[a], rights[b]), (keep_ref, send_ref), a, b, 0)
            store(product(rights[a], lefts[b]), (keep_ref, send_ref), a, b, 4)


VMEM = pl.BlockSpec(memory_space=pltpu.VMEM)
SMEM = pl.BlockSpec(memory_space=pltpu.SMEM)


def call(kernel, outs, scalars, arrays, flops):
    moved = sum(4 * v.size for v in arrays) + sum(4 * v.size for v in outs)
    return pl.pallas_call(
        kernel,
        out_shape=outs,
        in_specs=[SMEM] * len(scalars) + [VMEM] * len(arrays),
        out_specs=(VMEM,) * len(outs),
        compiler_params=pltpu.CompilerParams(vmem_limit_bytes=16 << 20),
        cost_estimate=pl.CostEstimate(flops=0, bytes_accessed=0, transcendentals=0),
    )(*scalars, *arrays)


def exchange(keep, send):
    return keep + swap(send, 1)


def messages(total, shard):
    shards = total.shape[1]
    parts = [pick(total[0], shard)]
    for turn in range(shards):
        to = (shard + turn) % shards
        parts.append(hop(pick(total[1], to), 2, turn))
        if turn:
            parts.append(hop(pick(total[0], to), 0, turn))
    return parts


def after(value, *others):
    return lax.optimization_barrier((value, *others))[0]


def final_kernel(factor, counts, where_ref, *refs):
    out_ref, share_ref = refs[-2:]
    begin = 0
    for step, count in enumerate(counts):
        total = refs[begin][...]
        for ref in refs[begin + 1 : begin + count]:
            total = total + ref[...]
        share_ref[4 * step : 4 * step + 4] = total
        begin += count
    for d in range(out_ref.shape[0]):
        out_ref[d] = share_ref[where_ref[d]] * factor


def on_device(logder):
    nblocks = lax.axis_size("blk")
    nshards = lax.axis_size("par")
    rows, width = logder.shape
    me = lax.axis_index("blk")
    shard = lax.axis_index("par")
    planes = nblocks // 4
    steps = planes // 2
    tiles = nblocks // 2 + 1
    factor = 1.0 / (width * nshards)
    half, quarter, eighth = width // 2, width // 4, width // 8
    core, side = me & 1, (me >> 1) & 1
    plane = me // 4
    lead = plane // steps

    theirs = swap(lax.dynamic_slice_in_dim(logder, (1 - core) * half, half, 1), 1)
    sums = after(jnp.sum(logder, axis=0)[None], theirs)
    stride = 4
    while stride < nblocks:
        radix = min(4, nblocks // stride)
        moved = [swap(sums, k * stride) for k in range(1, radix)]
        sums = sum(moved, sums)
        stride *= radix

    def both(which, part):
        start = which * quarter + part * eighth
        mine = lax.dynamic_slice_in_dim(logder, core * half + start, eighth, 1)
        return jnp.stack([mine, lax.dynamic_slice_in_dim(theirs, start, eighth, 1)])

    near = both(side, lead), both(side, 1 - lead)
    far = swap(both(1 - side, lead), 2), swap(both(1 - side, 1 - lead), 2)
    first = [(near[0], far[0])]
    for step in range(steps):
        first.append(tuple(shift(value, -4) for value in first[-1]))
    second = [(after(near[1], *first[steps]), after(far[1], *first[steps]))]
    for step in range(steps - 1):
        second.append(tuple(shift(value, -4) for value in second[-1]))

    sums = after(sums, far[0])
    sums = lax.dynamic_slice_in_dim(sums, core * half, half, 1) + swap(
        lax.dynamic_slice_in_dim(sums, (1 - core) * half, half, 1), 1
    )
    sums = lax.dynamic_slice_in_dim(sums, side * quarter, quarter, 1) + swap(
        lax.dynamic_slice_in_dim(sums, (1 - side) * quarter, quarter, 1), 2
    )
    mean = after(sums, *first[steps]) / (rows * nblocks)
    mean = jnp.stack(
        [lax.dynamic_slice_in_dim(mean, part * eighth, eighth, 1) for part in (lead, 1 - lead)]
    )

    def tile_shape(count):
        return jax.ShapeDtypeStruct((2, nshards, count, rows // nshards, rows), jnp.float32)

    flops = 6 * 4 * rows * rows * quarter
    copies = jax.ShapeDtypeStruct((2, 2, 2 * rows, eighth), jnp.bfloat16)
    keep, send, high, low = call(
        own_kernel,
        (tile_shape(4), tile_shape(4), copies, copies),
        (),
        (near[0], far[0], near[1], far[1], mean),
        4 * flops,
    )
    own = keep, send

    keep, send = call(
        half_kernel,
        (tile_shape(8), tile_shape(8)),
        (),
        (mean, high, low, *first[steps]),
        4 * flops,
    )
    total = exchange(keep, send)
    last = messages(total, shard)
    shares = [messages(after(exchange(*own), total), shard)]
    pending = last

    mean = after(mean, total)
    for step in range(1, steps):
        flag = (((plane + step) % planes) // steps != lead).astype(jnp.int32)[None]
        keep, send = call(
            functools.partial(pair_kernel, (0,)),
            (tile_shape(4), tile_shape(4)),
            (flag,),
            (mean, high, low, first[step][0], second[step][0]),
            2 * flops,
        )
        keep, send = call(
            functools.partial(pair_kernel, (1,)),
            (tile_shape(4), tile_shape(4)),
            (flag,),
            (mean, high, low, first[step][1], second[step][1], keep, send),
            2 * flops,
        )
        total = exchange(keep, send)
        total = after(total, *pending)
        shares.append(messages(total, shard))
        pending = shares[-1]
    moved = sum(last[1:], last[0])
    tail = [moved[:4], shift(moved[4:], nblocks // 2)]
    shares.append(tail)

    place = me % 4
    position = place + jnp.arange(tiles, dtype=jnp.int32)
    where = position - position % 4 + ((position % 4) ^ place)
    counts = tuple(len(parts) for parts in shares)
    flat = [value for parts in shares for value in parts]
    out = pl.pallas_call(
        functools.partial(final_kernel, factor, counts),
        out_shape=jax.ShapeDtypeStruct((tiles, rows // nshards, rows), jnp.float32),
        in_specs=[SMEM] + [VMEM] * len(flat),
        out_specs=VMEM,
        scratch_shapes=[pltpu.VMEM((4 * (steps + 1), rows // nshards, rows), jnp.float32)],
    )(where, *flat)
    return out[None]


def solution(mesh):
    placed = (P("blk", "par"),)
    return jax.shard_map(
        on_device,
        mesh=mesh,
        in_specs=placed,
        out_specs=P("blk", None, "par", None),
        check_vma=False,
    )
```

time: 283 us -> 96.7 us (0.34)
  waiting for transfers between devices: 142 us -> 39.5 us
  blocking collectives: 63 us -> 0 us
  matrix products: 19.8 us -> 0 us
  between operations: 13.4 us -> 0.29 us
  Pallas kernels: 0 us -> 9.68 us
  starting transfers between devices: 32.6 us -> 38.6 us
    ppermute x8 -> x27, waiting for transfers between devices: 125 us -> 39.5 us  [the longest x7 27.4 us: shift(): lax.ppermute(value, 'blk', [(k, (k + steps) % count) for k in range(count)])]
    psum x1 -> x0, blocking collectives: 63 us -> none  [on_device(): totals = lax.psum(jnp.sum(logder, axis=0), 'blk')]
    dot_general x9 -> x0, matrix products: 19.8 us -> none  [pair_tile(): lax.dot_general(left, right, (((1,), (1,)), ((), ())), precision=lax.Prec...]
    reduce_scatter x1 -> x0, waiting for transfers between devices: 16.8 us -> none  [on_device(): shares = lax.psum_scatter(stacked, 'par', scatter_dimension=1, tiled=True)]
    pallas_call x0 -> x5, Pallas kernels: none -> 9.68 us  [the longest x4 7.5 us: call(): pl.pallas_call(kernel, out_shape=outs, in_specs=[SMEM] * len(scalars) + [...]
    ppermute x8 -> x27, starting transfers between devices: 32.6 us -> 38.6 us  [the longest x7 18.4 us: shift(): lax.ppermute(value, 'blk', [(k, (k + steps) % count) for k in range(count)])]
    another operation x4 -> x3, local copies, waits for them, and re-layouts: 5.63 us -> 0.17 us  [the longest x2 0.17 us: both(): return jnp.stack([mine, lax.dynamic_slice_in_dim(theirs, start, eighth, 1)])]
    add x0 -> x8, other arithmetic: none -> 3.13 us  [the longest x3 2.52 us: exchange(): return keep + swap(send, 1)]
  transfers between devices with their start and end apart: 9 -> 27, of which waited for: 9 -> 12; matrix products, arithmetic and copies ran while one was open for 7% -> 6% of each run, Pallas kernels for 0% -> 2%
where the time goes in v3:
time: 96.7 us; the launch traced here: 95.9 us
  waiting for transfers between devices  39.5 us (41%)
  starting transfers between devices  38.6 us (40%)
  Pallas kernels  9.68 us (10%)
  local copies, waits for them, and re-layouts  4.42 us (5%)
  other arithmetic  3.42 us (4%)
    ppermute x7, waiting for transfers between devices, shift(): lax.ppermute(value, 'blk', [(k, (k + steps) % count) for k in range(count)])  27.4 us
    ppermute x7, starting transfers between devices, shift(): lax.ppermute(value, 'blk', [(k, (k + steps) % count) for k in range(count)])  18.4 us
    ppermute x11, starting transfers between devices, swap(): lax.ppermute(value, 'blk', [(k, k ^ mask) for k in range(lax.axis_size('b...  10.5 us
    ppermute x11, waiting for transfers between devices, swap(): lax.ppermute(value, 'blk', [(k, k ^ mask) for k in range(lax.axis_size('b...  9.85 us
    ppermute x9, starting transfers between devices, hop(): return lax.ppermute(value, ('blk', 'par'), pairs)  9.64 us
    pallas_call x4, Pallas kernels, call(): pl.pallas_call(kernel, out_shape=outs, in_specs=[SMEM] * len(scalars) + [...  7.5 us
    add x3, other arithmetic, exchange(): return keep + swap(send, 1)  2.52 us
    ppermute x9, waiting for transfers between devices, hop(): return lax.ppermute(value, ('blk', 'par'), pairs)  2.27 us
  transfers between devices with their start and end apart: 27, of which 12 were waited for; matrix products, arithmetic and copies ran while one was open for 6% of the time, Pallas kernels for 2%

profile of v3, /device:TPU:0, one launch (start us, length us, event | category | flops | bytes accessed | tf_op | source)
XLA Modules:
  0.0 95.9 jit_solution(6461510221596356959)
XLA Ops:
  0.0 1.3 %constant_dynamic-slice_fusion.6 = f32[128,1536]{1,0:T(8,128)S(1)} fusion(f32[128,3072]{1,0:T(8,128)} %param.1, s32[]{:T(128)S(6)} %select_n.113), kind=kLoop, calls=%fused_computation.32 | loop fusion | bytes 1572868 | tf_op jit(solution)/shard_map/dynamic_slice | solution.py:170
  1.3 0.5 collective-permute-start
  1.8 0.1 reduce_sum.9
  2.0 0.1 dynamic-slice_bitcast_fusion.5
  2.1 1.7 %collective-permute-done = f32[128,1536]{1,0:T(8,128)S(1)} collective-permute-done((f32[128,1536]{1,0:T(8,128)S(1)}, f32[128,1536]{1,0:T(8,128)S(1)}, u32[]{:S(2)}, u32[]{:S(2)}) %collective-permute-start) | collective-permute-done | bytes 786464 | tf_op jit(solution)/shard_map/ppermute | solution.py:11
  3.7 5.0 %collective-permute-start.5 = (f32[1,3072]{1,0:T(1,128)S(1)}, f32[1,3072]{1,0:T(1,128)S(1)}, u32[]{:S(2)}, u32[]{:S(2)}) collective-permute-start(f32[1,3072]{1,0:T(1,128)S(1)} %bitcast.48), channel_id=1, source_target_pairs={{0,24},{2,26},{4,28},{6,30},{8,16},{10,18},{12,20},{14,22},{16,8},... | collective-permute-start | bytes 36872 | tf_op jit(solution)/shard_map/ppermute | solution.py:11
  8.7 0.0 collective-permute-start.4
  8.7 0.6 collective-permute-start.3
  9.3 0.1 dynamic-slice_bitcast_fusion.4
  9.4 1.8 %collective-permute-start.1 = (f32[2,128,384]{2,1,0:T(8,128)S(1)}, f32[2,128,384]{2,1,0:T(8,128)S(1)}, u32[]{:S(2)}, u32[]{:S(2)}) collective-permute-start(f32[2,128,384]{2,1,0:T(8,128)S(1)} %pad_maximum_fusion.1), channel_id=1, source_target_pairs={{0,4},{2,6},{4,0},{6,2},{8,12},{10,14},{12,8},{14,10},{16,20},{18,... | collective-permute-start | bytes 1179656 | tf_op jit(solution)/shard_map/ppermute | solution.py:11
  11.3 3.6 %collective-permute-start.8 = (f32[2,128,384]{2,1,0:T(8,128)S(1)}, f32[2,128,384]{2,1,0:T(8,128)S(1)}, u32[]{:S(2)}, u32[]{:S(2)}) collective-permute-start(f32[2,128,384]{2,1,0:T(8,128)S(1)} %pad_maximum_fusion.near0), channel_id=1, source_target_pairs={{0,24},{2,26},{4,28},{6,30},{8,0},{10,2},{12,4},{14,6},{16,8},{18,... | collective-permute-start | bytes 1179656 | tf_op jit(solution)/shard_map/ppermute | solution.py:16
  15.0 5.1 %collective-permute-done.1.far0 = f32[2,128,384]{2,1,0:T(8,128)S(1)} collective-permute-done((f32[2,128,384]{2,1,0:T(8,128)S(1)}, f32[2,128,384]{2,1,0:T(8,128)S(1)}, u32[]{:S(2)}, u32[]{:S(2)}) %collective-permute-start.1) | collective-permute-done | bytes 393248 | tf_op jit(solution)/shard_map/ppermute | solution.py:11
  20.1 1.6 %collective-permute-start.2 = (f32[2,128,384]{2,1,0:T(8,128)S(1)}, f32[2,128,384]{2,1,0:T(8,128)S(1)}, u32[]{:S(2)}, u32[]{:S(2)}) collective-permute-start(f32[2,128,384]{2,1,0:T(8,128)S(1)} %pad_maximum_fusion.3), channel_id=1, source_target_pairs={{0,4},{2,6},{4,0},{6,2},{8,12},{10,14},{12,8},{14,10},{16,20},{18,... | collective-permute-start | bytes 1179656 | tf_op jit(solution)/shard_map/ppermute | solution.py:11
  21.7 3.5 %collective-permute-start.10 = (f32[2,128,384]{2,1,0:T(8,128)S(1)}, f32[2,128,384]{2,1,0:T(8,128)S(1)}, u32[]{:S(2)}, u32[]{:S(2)}) collective-permute-start(f32[2,128,384]{2,1,0:T(8,128)S(1)} %collective-permute-done.1.far0), channel_id=1, source_target_pairs={{0,24},{2,26},{4,28},{6,30},{8,0},{10,2},{12,4},{14,6},{16,8},{18,... | collective-permute-start | bytes 1179656 | tf_op jit(solution)/shard_map/ppermute | solution.py:16
  25.3 1.5 %collective-permute-start.9 = (f32[2,128,384]{2,1,0:T(8,128)S(1)}, f32[2,128,384]{2,1,0:T(8,128)S(1)}, u32[]{:S(2)}, u32[]{:S(2)}) collective-permute-start(f32[2,128,384]{2,1,0:T(8,128)S(1)} %collective-permute-done.8.refs_0_), channel_id=1, source_target_pairs={{0,24},{2,26},{4,28},{6,30},{8,0},{10,2},{12,4},{14,6},{16,8},{18,... | collective-permute-start | bytes 1179656 | tf_op jit(solution)/shard_map/ppermute | solution.py:16
  26.7 0.0 collective-permute-done.6
  26.8 7.9 %collective-permute-done.10.refs_0_ = f32[2,128,384]{2,1,0:T(8,128)S(1)} collective-permute-done((f32[2,128,384]{2,1,0:T(8,128)S(1)}, f32[2,128,384]{2,1,0:T(8,128)S(1)}, u32[]{:S(2)}, u32[]{:S(2)}) %collective-permute-start.10) | collective-permute-done | bytes 393248 | tf_op jit(solution)/shard_map/ppermute | solution.py:16
  34.7 4.3 %collective-permute-start.11 = (f32[2,128,384]{2,1,0:T(8,128)S(1)}, f32[2,128,384]{2,1,0:T(8,128)S(1)}, u32[]{:S(2)}, u32[]{:S(2)}) collective-permute-start(f32[2,128,384]{2,1,0:T(8,128)S(1)} %collective-permute-done.10.refs_0_), channel_id=1, source_target_pairs={{0,24},{2,26},{4,28},{6,30},{8,0},{10,2},{12,4},{14,6},{16,8},{18,... | collective-permute-start | bytes 1179656 | tf_op jit(solution)/shard_map/ppermute | solution.py:16
  39.0 0.5 collective-permute-start.7
  39.6 3.0 %collective-permute-done.7 = f32[1,768]{1,0:T(1,128)S(1)} collective-permute-done((f32[1,768]{1,0:T(1,128)S(1)}, f32[1,768]{1,0:T(1,128)S(1)}, u32[]{:S(2)}, u32[]{:S(2)}) %collective-permute-start.7) | collective-permute-done | bytes 3104 | tf_op jit(solution)/shard_map/ppermute | solution.py:11
  42.6 0.5 collective-permute-done.9.near_ref
  43.1 7.7 %collective-permute-done.11.far_ref = f32[2,128,384]{2,1,0:T(8,128)S(1)} collective-permute-done((f32[2,128,384]{2,1,0:T(8,128)S(1)}, f32[2,128,384]{2,1,0:T(8,128)S(1)}, u32[]{:S(2)}, u32[]{:S(2)}) %collective-permute-start.11) | collective-permute-done | bytes 393248 | tf_op jit(solution)/shard_map/ppermute | solution.py:16
  50.9 0.0 collective-permute-done.2.far1
  50.9 2.7 %shard_map.17 = (f32[2,2,4,64,128]{4,3,2,1,0:T(8,128)S(1)}, f32[2,2,4,64,128]{4,3,2,1,0:T(8,128)}, bf16[2,2,256,384]{3,2,1,0:T(8,128)(2,1)S(1)}, bf16[2,2,256,384]{3,2,1,0:T(8,128)(2,1)S(1)}) custom-call(f32[2,128,384]{2,1,0:T(8,128)S(1)} %pad_maximum_fusion.near0, f32[2,128,384]{2,1,0:T(8,128)S(1)} %collective-permute-done.1.far0, ...), custom_call_target="tpu_custom_call" | custom-call | tf_op jit(solution)/shard_map/pallas_call | solution.py:113
  53.6 2.8 %shard_map.18 = (f32[2,2,8,64,128]{4,3,2,1,0:T(8,128)S(1)}, f32[2,2,8,64,128]{4,3,2,1,0:T(8,128)}) custom-call(f32[2,1,384]{2,1,0:T(1,128)S(1)} %pad_maximum_fusion.4.mean_ref, bf16[2,2,256,384]{3,2,1,0:T(8,128)(2,1)S(1)} %get-tuple-element.28.high_ref, bf16[2,2,256,384]{3,2,1,0:T(8,128)(2,1)S(1)} %get-tuple-element.29.low_ref, ...), custom_call_target="tpu_custom_call" | custom-call | tf_op jit(solution)/shard_map/pallas_call | solution.py:113
  56.4 0.0 collective-permute-start.13
  56.4 0.5 collective-permute-start.12
  56.9 4.3 %collective-permute-start.18 = (f32[2,128,384]{2,1,0:T(8,128)S(1)}, f32[2,128,384]{2,1,0:T(8,128)S(1)}, u32[]{:S(2)}, u32[]{:S(2)}) collective-permute-start(f32[2,128,384]{2,1,0:T(8,128)S(1)} %pad_maximum_fusion.2.near1), channel_id=1, source_target_pairs={{0,24},{2,26},{4,28},{6,30},{8,0},{10,2},{12,4},{14,6},{16,8},{18,... | collective-permute-start | bytes 1179656 | tf_op jit(solution)/shard_map/ppermute | solution.py:16
  61.2 0.0 collective-permute-start.17
  61.2 1.1 %add.197 = f32[2,2,4,64,128]{4,3,2,1,0:T(8,128)S(1)} add(f32[2,2,4,64,128]{4,3,2,1,0:T(8,128)S(1)} %get-tuple-element.26, f32[2,2,4,64,128]{4,3,2,1,0:T(8,128)} %collective-permute-done.12) | non-fusion elementwise | flops 131072 | bytes 1572864 | tf_op jit(solution)/shard_map/add | solution.py:124
  62.3 0.0 collective-permute-done.13
  62.4 1.4 %add.198 = f32[2,2,8,64,128]{4,3,2,1,0:T(8,128)S(1)} add(f32[2,2,8,64,128]{4,3,2,1,0:T(8,128)S(1)} %get-tuple-element.30, f32[2,2,8,64,128]{4,3,2,1,0:T(8,128)} %collective-permute-done.13) | non-fusion elementwise | flops 262144 | bytes 3145728 | tf_op jit(solution)/shard_map/add | solution.py:124
  63.7 0.1 fusion.5
  63.8 1.6 %collective-permute-start.22 = (f32[8,64,128]{2,1,0:T(8,128)S(1)}, f32[8,64,128]{2,1,0:T(8,128)S(1)}, u32[]{:S(2)}, u32[]{:S(2)}) collective-permute-start(f32[8,64,128]{2,1,0:T(8,128)S(1)} %dynamic-slice_bitcast_fusion), channel_id=1, source_target_pairs={{0,1},{1,0},{2,3},{3,2},{4,5},{5,4},{6,7},{7,6},{8,9},{9,8},{10,11... | collective-permute-start | bytes 786440 | tf_op jit(solution)/shard_map/ppermute | solution.py:26
  65.4 0.6 collective-permute-start.20
  66.0 1.5 %collective-permute-start.21 = (f32[8,64,128]{2,1,0:T(8,128)S(1)}, f32[8,64,128]{2,1,0:T(8,128)S(1)}, u32[]{:S(2)}, u32[]{:S(2)}) collective-permute-start(f32[8,64,128]{2,1,0:T(8,128)S(1)} %get-tuple-element.56), channel_id=1, source_target_pairs={{0,5},{1,4},{2,7},{3,6},{4,1},{5,0},{6,3},{7,2},{8,13},{9,12},{10,... | collective-permute-start | bytes 786440 | tf_op jit(solution)/shard_map/ppermute | solution.py:26
  67.6 3.1 %collective-permute-done.18.refs_1_ = f32[2,128,384]{2,1,0:T(8,128)S(1)} collective-permute-done((f32[2,128,384]{2,1,0:T(8,128)S(1)}, f32[2,128,384]{2,1,0:T(8,128)S(1)}, u32[]{:S(2)}, u32[]{:S(2)}) %collective-permute-start.18) | collective-permute-done | bytes 393248 | tf_op jit(solution)/shard_map/ppermute | solution.py:16
  70.7 1.4 %collective-permute-start.15 = (f32[4,64,128]{2,1,0:T(8,128)S(1)}, f32[4,64,128]{2,1,0:T(8,128)S(1)}, u32[]{:S(2)}, u32[]{:S(2)}) collective-permute-start(f32[4,64,128]{2,1,0:T(8,128)S(1)} %get-tuple-element.67), channel_id=1, source_target_pairs={{0,5},{1,4},{2,7},{3,6},{4,1},{5,0},{6,3},{7,2},{8,13},{9,12},{10,... | collective-permute-start | bytes 393224 | tf_op jit(solution)/shard_map/ppermute | solution.py:26
  72.2 1.0 %shard_map.19 = (f32[2,2,4,64,128]{4,3,2,1,0:T(8,128)S(1)}, f32[2,2,4,64,128]{4,3,2,1,0:T(8,128)S(1)}) custom-call(s32[1]{0:T(128)} %bitcast.15.flag_ref, f32[2,1,384]{2,1,0:T(1,128)S(1)} %pad_maximum_fusion.4.mean_ref, bf16[2,2,256,384]{3,2,1,0:T(8,128)(2,1)S(1)} %get-tuple-element.28.high_ref, bf16[2,2,256,384]{3,2,1,0:T(8,128)(2,1)S(1)} %get-tuple-element.29.low_ref, ...), custom_call_target="tpu_custom_call" | custom-call | tf_op jit(solution)/shard_map/pallas_call | solution.py:113
  73.2 5.1 %collective-permute-done.17.refs_1_ = f32[2,128,384]{2,1,0:T(8,128)S(1)} collective-permute-done((f32[2,128,384]{2,1,0:T(8,128)}, f32[2,128,384]{2,1,0:T(8,128)S(1)}, u32[]{:S(2)}, u32[]{:S(2)}) %collective-permute-start.17) | collective-permute-done | bytes 393248 | tf_op jit(solution)/shard_map/ppermute | solution.py:16
  78.3 1.0 %shard_map.20 = (f32[2,2,4,64,128]{4,3,2,1,0:T(8,128)S(1)}, f32[2,2,4,64,128]{4,3,2,1,0:T(8,128)S(1)}) custom-call(s32[1]{0:T(128)} %bitcast.15.flag_ref, f32[2,1,384]{2,1,0:T(1,128)S(1)} %pad_maximum_fusion.4.mean_ref, bf16[2,2,256,384]{3,2,1,0:T(8,128)(2,1)S(1)} %get-tuple-element.28.high_ref, bf16[2,2,256,384]{3,2,1,0:T(8,128)(2,1)S(1)} %get-tuple-element.29.low_ref, ...), custom_call_target="tpu_custom_call" | custom-call | tf_op jit(solution)/shard_map/pallas_call | solution.py:113
  79.3 0.1 collective-permute-start.19
  79.4 0.7 dynamic-slice_bitcast_fusion.16
  80.1 0.5 collective-permute-start.14
  80.6 1.0 %collective-permute-done.20 = f32[8,64,128]{2,1,0:T(8,128)S(1)} collective-permute-done((f32[8,64,128]{2,1,0:T(8,128)S(1)}, f32[8,64,128]{2,1,0:T(8,128)S(1)}, u32[]{:S(2)}, u32[]{:S(2)}) %collective-permute-start.20) | collective-permute-done | bytes 262176 | tf_op jit(solution)/shard_map/ppermute | solution.py:26
  81.6 0.5 collective-permute-start.16
  82.1 0.1 add_add_fusion
  82.2 0.7 fusion.8
  82.9 1.1 %collective-permute-start.26 = (f32[4,64,128]{2,1,0:T(8,128)S(1)}, f32[4,64,128]{2,1,0:T(8,128)S(1)}, u32[]{:S(2)}, u32[]{:S(2)}) collective-permute-start(f32[4,64,128]{2,1,0:T(8,128)S(1)} %get-tuple-element.59), channel_id=1, source_target_pairs={{0,16},{2,18},{4,20},{6,22},{8,24},{10,26},{12,28},{14,30},{16,0},... | collective-permute-start | bytes 393224 | tf_op jit(solution)/shard_map/ppermute | solution.py:16
  84.0 0.1 add.207
  84.1 1.6 %collective-permute-start.24 = (f32[4,64,128]{2,1,0:T(8,128)S(1)}, f32[4,64,128]{2,1,0:T(8,128)S(1)}, u32[]{:S(2)}, u32[]{:S(2)}) collective-permute-start(f32[4,64,128]{2,1,0:T(8,128)S(1)} %get-tuple-element.63), channel_id=1, source_target_pairs={{0,5},{1,4},{2,7},{3,6},{4,1},{5,0},{6,3},{7,2},{8,13},{9,12},{10,... | collective-permute-start | bytes 393224 | tf_op jit(solution)/shard_map/ppermute | solution.py:26
  85.7 0.7 dynamic-slice_bitcast_fusion.12
  86.4 0.0 collective-permute-done.15.refs_2_
  86.4 1.0 %collective-permute-start.23 = (f32[4,64,128]{2,1,0:T(8,128)S(1)}, f32[4,64,128]{2,1,0:T(8,128)S(1)}, u32[]{:S(2)}, u32[]{:S(2)}) collective-permute-start(f32[4,64,128]{2,1,0:T(8,128)S(1)} %get-tuple-element.64), channel_id=1, source_target_pairs={{0,4},{1,5},{2,6},{3,7},{4,0},{5,1},{6,2},{7,3},{8,12},{9,13},{10,... | collective-permute-start | bytes 393224 | tf_op jit(solution)/shard_map/ppermute | solution.py:26
  87.4 0.0 collective-permute-done.14.refs_1_
  87.4 1.0 %collective-permute-start.25 = (f32[4,64,128]{2,1,0:T(8,128)S(1)}, f32[4,64,128]{2,1,0:T(8,128)S(1)}, u32[]{:S(2)}, u32[]{:S(2)}) collective-permute-start(f32[4,64,128]{2,1,0:T(8,128)S(1)} %get-tuple-element.61), channel_id=1, source_target_pairs={{0,1},{1,0},{2,3},{3,2},{4,5},{5,4},{6,7},{7,6},{8,9},{9,8},{10,11... | collective-permute-start | bytes 393224 | tf_op jit(solution)/shard_map/ppermute | solution.py:26
  88.4 0.5 xor_add_fusion.where_ref
  88.9 2.9 %collective-permute-done.26.refs_9_ = f32[4,64,128]{2,1,0:T(8,128)S(1)} collective-permute-done((f32[4,64,128]{2,1,0:T(8,128)S(1)}, f32[4,64,128]{2,1,0:T(8,128)S(1)}, u32[]{:S(2)}, u32[]{:S(2)}) %collective-permute-start.26) | collective-permute-done | bytes 131104 | tf_op jit(solution)/shard_map/ppermute | solution.py:16
  91.8 0.0 collective-permute-done.24.refs_6_
  91.8 1.1 %collective-permute-done.23.refs_5_ = f32[4,64,128]{2,1,0:T(8,128)S(1)} collective-permute-done((f32[4,64,128]{2,1,0:T(8,128)S(1)}, f32[4,64,128]{2,1,0:T(8,128)S(1)}, u32[]{:S(2)}, u32[]{:S(2)}) %collective-permute-start.23) | collective-permute-done | bytes 131104 | tf_op jit(solution)/shard_map/ppermute | solution.py:26
  93.0 0.1 collective-permute-done.25.refs_7_
  93.1 0.5 copy-done.11
  93.6 0.1 copy-done.12
  93.7 2.2 %shard_map.21 = f32[9,64,128]{2,1,0:T(8,128)} custom-call(s32[9]{0:T(128)} %xor_add_fusion.where_ref, f32[4,64,128]{2,1,0:T(8,128)} %get-tuple-element.66.refs_0_, f32[4,64,128]{2,1,0:T(8,128)} %copy-done.7, f32[4,64,128]{2,1,0:T(8,128)} %copy-done.6, f32[4,64,128]{2,1,0:T(8,128)} %copy-done.8, f32[4,64,128]{2,1,0:T(8,128)} %get-tuple-element.62.refs_4_, ...), custom_call_target="tpu_custom_call" | custom-call | tf_op jit(solution)/shard_map/pallas_call | solution.py:261
  (52 shorter events, 0.5 us)
Async XLA Ops:
  0.0 1.8 %copy-start.5 = (f32[128,3072]{1,0:T(8,128)S(1)}, f32[128,3072]{1,0:T(8,128)}, u32[]{:S(2)}) copy-start(f32[128,3072]{1,0:T(8,128)} %param.1) | copy-start | bytes 4718596
  1.3 2.4 %collective-permute-start = (f32[128,1536]{1,0:T(8,128)S(1)}, f32[128,1536]{1,0:T(8,128)S(1)}, u32[]{:S(2)}, u32[]{:S(2)}) collective-permute-start(f32[128,1536]{1,0:T(8,128)S(1)} %constant_dynamic-slice_fusion.6), channel_id=1, source_target_pairs={{0,2},{2,0},{4,6},{6,4},{8,10},{10,8},{12,14},{14,12},{16,18},{18,... | collective-permute-start | bytes 2359304 | tf_op jit(solution)/shard_map/ppermute | solution.py:11
  3.7 11.2 %collective-permute-start.5 = (f32[1,3072]{1,0:T(1,128)S(1)}, f32[1,3072]{1,0:T(1,128)S(1)}, u32[]{:S(2)}, u32[]{:S(2)}) collective-permute-start(f32[1,3072]{1,0:T(1,128)S(1)} %bitcast.48), channel_id=1, source_target_pairs={{0,24},{2,26},{4,28},{6,30},{8,16},{10,18},{12,20},{14,22},{16,8},... | collective-permute-start | bytes 36872 | tf_op jit(solution)/shard_map/ppermute | solution.py:11
  8.7 6.2 %collective-permute-start.4 = (f32[1,3072]{1,0:T(1,128)S(1)}, f32[1,3072]{1,0:T(1,128)S(1)}, u32[]{:S(2)}, u32[]{:S(2)}) collective-permute-start(f32[1,3072]{1,0:T(1,128)S(1)} %bitcast.49), channel_id=1, source_target_pairs={{0,16},{2,18},{4,20},{6,22},{8,24},{10,26},{12,28},{14,30},{16,0},... | collective-permute-start | bytes 36872 | tf_op jit(solution)/shard_map/ppermute | solution.py:11
  8.7 6.2 %collective-permute-start.3 = (f32[1,3072]{1,0:T(1,128)S(1)}, f32[1,3072]{1,0:T(1,128)S(1)}, u32[]{:S(2)}, u32[]{:S(2)}) collective-permute-start(f32[1,3072]{1,0:T(1,128)S(1)} %bitcast.50), channel_id=1, source_target_pairs={{0,8},{2,10},{4,12},{6,14},{8,0},{10,2},{12,4},{14,6},{16,24},{18,... | collective-permute-start | bytes 36872 | tf_op jit(solution)/shard_map/ppermute | solution.py:11
  9.4 10.7 %collective-permute-start.1 = (f32[2,128,384]{2,1,0:T(8,128)S(1)}, f32[2,128,384]{2,1,0:T(8,128)S(1)}, u32[]{:S(2)}, u32[]{:S(2)}) collective-permute-start(f32[2,128,384]{2,1,0:T(8,128)S(1)} %pad_maximum_fusion.1), channel_id=1, source_target_pairs={{0,4},{2,6},{4,0},{6,2},{8,12},{10,14},{12,8},{14,10},{16,20},{18,... | collective-permute-start | bytes 1179656 | tf_op jit(solution)/shard_map/ppermute | solution.py:11
  11.3 14.0 %collective-permute-start.8 = (f32[2,128,384]{2,1,0:T(8,128)S(1)}, f32[2,128,384]{2,1,0:T(8,128)S(1)}, u32[]{:S(2)}, u32[]{:S(2)}) collective-permute-start(f32[2,128,384]{2,1,0:T(8,128)S(1)} %pad_maximum_fusion.near0), channel_id=1, source_target_pairs={{0,24},{2,26},{4,28},{6,30},{8,0},{10,2},{12,4},{14,6},{16,8},{18,... | collective-permute-start | bytes 1179656 | tf_op jit(solution)/shard_map/ppermute | solution.py:16
  20.1 6.7 %collective-permute-start.6 = (f32[1,1536]{1,0:T(1,128)S(1)}, f32[1,1536]{1,0:T(1,128)S(1)}, u32[]{:S(2)}, u32[]{:S(2)}) collective-permute-start(f32[1,1536]{1,0:T(1,128)S(1)} %constant_dynamic-slice_fusion.4), channel_id=1, source_target_pairs={{0,2},{2,0},{4,6},{6,4},{8,10},{10,8},{12,14},{14,12},{16,18},{18,... | collective-permute-start | bytes 18440 | tf_op jit(solution)/shard_map/ppermute | solution.py:11
  20.1 30.8 %collective-permute-start.2 = (f32[2,128,384]{2,1,0:T(8,128)S(1)}, f32[2,128,384]{2,1,0:T(8,128)S(1)}, u32[]{:S(2)}, u32[]{:S(2)}) collective-permute-start(f32[2,128,384]{2,1,0:T(8,128)S(1)} %pad_maximum_fusion.3), channel_id=1, source_target_pairs={{0,4},{2,6},{4,0},{6,2},{8,12},{10,14},{12,8},{14,10},{16,20},{18,... | collective-permute-start | bytes 1179656 | tf_op jit(solution)/shard_map/ppermute | solution.py:11
  21.7 13.0 %collective-permute-start.10 = (f32[2,128,384]{2,1,0:T(8,128)S(1)}, f32[2,128,384]{2,1,0:T(8,128)S(1)}, u32[]{:S(2)}, u32[]{:S(2)}) collective-permute-start(f32[2,128,384]{2,1,0:T(8,128)S(1)} %collective-permute-done.1.far0), channel_id=1, source_target_pairs={{0,24},{2,26},{4,28},{6,30},{8,0},{10,2},{12,4},{14,6},{16,8},{18,... | collective-permute-start | bytes 1179656 | tf_op jit(solution)/shard_map/ppermute | solution.py:16
  25.2 28.3 %copy-start.3 = (f32[2,128,384]{2,1,0:T(8,128)}, f32[2,128,384]{2,1,0:T(8,128)S(1)}, u32[]{:S(2)}) copy-start(f32[2,128,384]{2,1,0:T(8,128)S(1)} %collective-permute-done.8.refs_0_) | copy-start | bytes 1179652
  25.3 17.9 %collective-permute-start.9 = (f32[2,128,384]{2,1,0:T(8,128)S(1)}, f32[2,128,384]{2,1,0:T(8,128)S(1)}, u32[]{:S(2)}, u32[]{:S(2)}) collective-permute-start(f32[2,128,384]{2,1,0:T(8,128)S(1)} %collective-permute-done.8.refs_0_), channel_id=1, source_target_pairs={{0,24},{2,26},{4,28},{6,30},{8,0},{10,2},{12,4},{14,6},{16,8},{18,... | collective-permute-start | bytes 1179656 | tf_op jit(solution)/shard_map/ppermute | solution.py:16
  34.7 16.2 %copy-start = (f32[2,128,384]{2,1,0:T(8,128)}, f32[2,128,384]{2,1,0:T(8,128)S(1)}, u32[]{:S(2)}) copy-start(f32[2,128,384]{2,1,0:T(8,128)S(1)} %collective-permute-done.10.refs_0_) | copy-start | bytes 1179652
  34.7 16.1 %collective-permute-start.11 = (f32[2,128,384]{2,1,0:T(8,128)S(1)}, f32[2,128,384]{2,1,0:T(8,128)S(1)}, u32[]{:S(2)}, u32[]{:S(2)}) collective-permute-start(f32[2,128,384]{2,1,0:T(8,128)S(1)} %collective-permute-done.10.refs_0_), channel_id=1, source_target_pairs={{0,24},{2,26},{4,28},{6,30},{8,0},{10,2},{12,4},{14,6},{16,8},{18,... | collective-permute-start | bytes 1179656 | tf_op jit(solution)/shard_map/ppermute | solution.py:16
  39.0 3.6 %collective-permute-start.7 = (f32[1,768]{1,0:T(1,128)S(1)}, f32[1,768]{1,0:T(1,128)S(1)}, u32[]{:S(2)}, u32[]{:S(2)}) collective-permute-start(f32[1,768]{1,0:T(1,128)S(1)} %constant_dynamic-slice_fusion.2), channel_id=1, source_target_pairs={{0,4},{2,6},{4,0},{6,2},{8,12},{10,14},{12,8},{14,10},{16,20},{18,... | collective-permute-start | bytes 9224 | tf_op jit(solution)/shard_map/ppermute | solution.py:11
  50.9 2.7 %copy-start.2 = (f32[2,128,384]{2,1,0:T(8,128)}, f32[2,128,384]{2,1,0:T(8,128)S(1)}, u32[]{:S(2)}) copy-start(f32[2,128,384]{2,1,0:T(8,128)S(1)} %collective-permute-done.2.far1) | copy-start | bytes 1179652
  56.4 5.9 %collective-permute-start.13 = (f32[2,2,8,64,128]{4,3,2,1,0:T(8,128)}, f32[2,2,8,64,128]{4,3,2,1,0:T(8,128)}, u32[]{:S(2)}, u32[]{:S(2)}) collective-permute-start(f32[2,2,8,64,128]{4,3,2,1,0:T(8,128)} %get-tuple-element.31), channel_id=1, source_target_pairs={{0,2},{2,0},{4,6},{6,4},{8,10},{10,8},{12,14},{14,12},{16,18},{18,... | collective-permute-start | bytes 3145736 | tf_op jit(solution)/shard_map/ppermute | solution.py:11
  56.4 4.8 %collective-permute-start.12 = (f32[2,2,4,64,128]{4,3,2,1,0:T(8,128)}, f32[2,2,4,64,128]{4,3,2,1,0:T(8,128)}, u32[]{:S(2)}, u32[]{:S(2)}) collective-permute-start(f32[2,2,4,64,128]{4,3,2,1,0:T(8,128)} %get-tuple-element.27), channel_id=1, source_target_pairs={{0,2},{2,0},{4,6},{6,4},{8,10},{10,8},{12,14},{14,12},{16,18},{18,... | collective-permute-start | bytes 1572872 | tf_op jit(solution)/shard_map/ppermute | solution.py:11
  56.9 13.8 %collective-permute-start.18 = (f32[2,128,384]{2,1,0:T(8,128)S(1)}, f32[2,128,384]{2,1,0:T(8,128)S(1)}, u32[]{:S(2)}, u32[]{:S(2)}) collective-permute-start(f32[2,128,384]{2,1,0:T(8,128)S(1)} %pad_maximum_fusion.2.near1), channel_id=1, source_target_pairs={{0,24},{2,26},{4,28},{6,30},{8,0},{10,2},{12,4},{14,6},{16,8},{18,... | collective-permute-start | bytes 1179656 | tf_op jit(solution)/shard_map/ppermute | solution.py:16
  61.2 17.1 %collective-permute-start.17 = (f32[2,128,384]{2,1,0:T(8,128)}, f32[2,128,384]{2,1,0:T(8,128)S(1)}, u32[]{:S(2)}, u32[]{:S(2)}) collective-permute-start(f32[2,128,384]{2,1,0:T(8,128)} %copy-done.2), channel_id=1, source_target_pairs={{0,24},{2,26},{4,28},{6,30},{8,0},{10,2},{12,4},{14,6},{16,8},{18,... | collective-permute-start | bytes 1179656 | tf_op jit(solution)/shard_map/ppermute | solution.py:16
  63.8 8.3 %copy-start.4 = (f32[2,128,384]{2,1,0:T(8,128)S(1)}, f32[2,128,384]{2,1,0:T(8,128)}, u32[]{:S(2)}) copy-start(f32[2,128,384]{2,1,0:T(8,128)} %copy-done.3) | copy-start | bytes 1179652
  63.8 16.2 %collective-permute-start.22 = (f32[8,64,128]{2,1,0:T(8,128)S(1)}, f32[8,64,128]{2,1,0:T(8,128)S(1)}, u32[]{:S(2)}, u32[]{:S(2)}) collective-permute-start(f32[8,64,128]{2,1,0:T(8,128)S(1)} %dynamic-slice_bitcast_fusion), channel_id=1, source_target_pairs={{0,1},{1,0},{2,3},{3,2},{4,5},{5,4},{6,7},{7,6},{8,9},{9,8},{10,11... | collective-permute-start | bytes 786440 | tf_op jit(solution)/shard_map/ppermute | solution.py:26
  65.4 16.1 %collective-permute-start.20 = (f32[8,64,128]{2,1,0:T(8,128)S(1)}, f32[8,64,128]{2,1,0:T(8,128)S(1)}, u32[]{:S(2)}, u32[]{:S(2)}) collective-permute-start(f32[8,64,128]{2,1,0:T(8,128)S(1)} %get-tuple-element.55), channel_id=1, source_target_pairs={{0,4},{1,5},{2,6},{3,7},{4,0},{5,1},{6,2},{7,3},{8,12},{9,13},{10,... | collective-permute-start | bytes 786440 | tf_op jit(solution)/shard_map/ppermute | solution.py:26
  66.0 16.1 %collective-permute-start.21 = (f32[8,64,128]{2,1,0:T(8,128)S(1)}, f32[8,64,128]{2,1,0:T(8,128)S(1)}, u32[]{:S(2)}, u32[]{:S(2)}) collective-permute-start(f32[8,64,128]{2,1,0:T(8,128)S(1)} %get-tuple-element.56), channel_id=1, source_target_pairs={{0,5},{1,4},{2,7},{3,6},{4,1},{5,0},{6,3},{7,2},{8,13},{9,12},{10,... | collective-permute-start | bytes 786440 | tf_op jit(solution)/shard_map/ppermute | solution.py:26
  67.6 10.7 %copy-start.1 = (f32[2,128,384]{2,1,0:T(8,128)S(1)}, f32[2,128,384]{2,1,0:T(8,128)}, u32[]{:S(2)}) copy-start(f32[2,128,384]{2,1,0:T(8,128)} %copy-done) | copy-start | bytes 1179652
  70.7 15.7 %collective-permute-start.15 = (f32[4,64,128]{2,1,0:T(8,128)S(1)}, f32[4,64,128]{2,1,0:T(8,128)S(1)}, u32[]{:S(2)}, u32[]{:S(2)}) collective-permute-start(f32[4,64,128]{2,1,0:T(8,128)S(1)} %get-tuple-element.67), channel_id=1, source_target_pairs={{0,5},{1,4},{2,7},{3,6},{4,1},{5,0},{6,3},{7,2},{8,13},{9,12},{10,... | collective-permute-start | bytes 393224 | tf_op jit(solution)/shard_map/ppermute | solution.py:26
  79.3 4.7 %collective-permute-start.19 = (f32[2,2,4,64,128]{4,3,2,1,0:T(8,128)S(1)}, f32[2,2,4,64,128]{4,3,2,1,0:T(8,128)S(1)}, u32[]{:S(2)}, u32[]{:S(2)}) collective-permute-start(f32[2,2,4,64,128]{4,3,2,1,0:T(8,128)S(1)} %get-tuple-element.39), channel_id=1, source_target_pairs={{0,2},{2,0},{4,6},{6,4},{8,10},{10,8},{12,14},{14,12},{16,18},{18,... | collective-permute-start | bytes 1572872 | tf_op jit(solution)/shard_map/ppermute | solution.py:11
  80.1 7.3 %collective-permute-start.14 = (f32[4,64,128]{2,1,0:T(8,128)S(1)}, f32[4,64,128]{2,1,0:T(8,128)S(1)}, u32[]{:S(2)}, u32[]{:S(2)}) collective-permute-start(f32[4,64,128]{2,1,0:T(8,128)S(1)} %get-tuple-element.68), channel_id=1, source_target_pairs={{0,4},{1,5},{2,6},{3,7},{4,0},{5,1},{6,2},{7,3},{8,12},{9,13},{10,... | collective-permute-start | bytes 393224 | tf_op jit(solution)/shard_map/ppermute | solution.py:26
  81.6 7.3 %collective-permute-start.16 = (f32[4,64,128]{2,1,0:T(8,128)S(1)}, f32[4,64,128]{2,1,0:T(8,128)S(1)}, u32[]{:S(2)}, u32[]{:S(2)}) collective-permute-start(f32[4,64,128]{2,1,0:T(8,128)S(1)} %get-tuple-element.65), channel_id=1, source_target_pairs={{0,1},{1,0},{2,3},{3,2},{4,5},{5,4},{6,7},{7,6},{8,9},{9,8},{10,11... | collective-permute-start | bytes 393224 | tf_op jit(solution)/shard_map/ppermute | solution.py:26
  82.9 9.0 %collective-permute-start.26 = (f32[4,64,128]{2,1,0:T(8,128)S(1)}, f32[4,64,128]{2,1,0:T(8,128)S(1)}, u32[]{:S(2)}, u32[]{:S(2)}) collective-permute-start(f32[4,64,128]{2,1,0:T(8,128)S(1)} %get-tuple-element.59), channel_id=1, source_target_pairs={{0,16},{2,18},{4,20},{6,22},{8,24},{10,26},{12,28},{14,30},{16,0},... | collective-permute-start | bytes 393224 | tf_op jit(solution)/shard_map/ppermute | solution.py:16
  84.1 7.7 %collective-permute-start.24 = (f32[4,64,128]{2,1,0:T(8,128)S(1)}, f32[4,64,128]{2,1,0:T(8,128)S(1)}, u32[]{:S(2)}, u32[]{:S(2)}) collective-permute-start(f32[4,64,128]{2,1,0:T(8,128)S(1)} %get-tuple-element.63), channel_id=1, source_target_pairs={{0,5},{1,4},{2,7},{3,6},{4,1},{5,0},{6,3},{7,2},{8,13},{9,12},{10,... | collective-permute-start | bytes 393224 | tf_op jit(solution)/shard_map/ppermute | solution.py:26
  86.4 6.7 %copy-start.6 = (f32[4,64,128]{2,1,0:T(8,128)}, f32[4,64,128]{2,1,0:T(8,128)S(1)}, u32[]{:S(2)}) copy-start(f32[4,64,128]{2,1,0:T(8,128)S(1)} %collective-permute-done.15.refs_2_) | copy-start | bytes 393220
  86.4 6.6 %collective-permute-start.23 = (f32[4,64,128]{2,1,0:T(8,128)S(1)}, f32[4,64,128]{2,1,0:T(8,128)S(1)}, u32[]{:S(2)}, u32[]{:S(2)}) collective-permute-start(f32[4,64,128]{2,1,0:T(8,128)S(1)} %get-tuple-element.64), channel_id=1, source_target_pairs={{0,4},{1,5},{2,6},{3,7},{4,0},{5,1},{6,2},{7,3},{8,12},{9,13},{10,... | collective-permute-start | bytes 393224 | tf_op jit(solution)/shard_map/ppermute | solution.py:26
  87.4 5.7 %copy-start.7 = (f32[4,64,128]{2,1,0:T(8,128)}, f32[4,64,128]{2,1,0:T(8,128)S(1)}, u32[]{:S(2)}) copy-start(f32[4,64,128]{2,1,0:T(8,128)S(1)} %collective-permute-done.14.refs_1_) | copy-start | bytes 393220
  87.4 5.7 %collective-permute-start.25 = (f32[4,64,128]{2,1,0:T(8,128)S(1)}, f32[4,64,128]{2,1,0:T(8,128)S(1)}, u32[]{:S(2)}, u32[]{:S(2)}) collective-permute-start(f32[4,64,128]{2,1,0:T(8,128)S(1)} %get-tuple-element.61), channel_id=1, source_target_pairs={{0,1},{1,0},{2,3},{3,2},{4,5},{5,4},{6,7},{7,6},{8,9},{9,8},{10,11... | collective-permute-start | bytes 393224 | tf_op jit(solution)/shard_map/ppermute | solution.py:26
  88.9 4.2 %copy-start.8 = (f32[4,64,128]{2,1,0:T(8,128)}, f32[4,64,128]{2,1,0:T(8,128)S(1)}, u32[]{:S(2)}) copy-start(f32[4,64,128]{2,1,0:T(8,128)S(1)} %collective-permute-done.16.refs_3_) | copy-start | bytes 393220
  91.8 1.2 %copy-start.9 = (f32[4,64,128]{2,1,0:T(8,128)}, f32[4,64,128]{2,1,0:T(8,128)S(1)}, u32[]{:S(2)}) copy-start(f32[4,64,128]{2,1,0:T(8,128)S(1)} %collective-permute-done.26.refs_9_) | copy-start | bytes 393220
  91.8 1.2 %copy-start.10 = (f32[4,64,128]{2,1,0:T(8,128)}, f32[4,64,128]{2,1,0:T(8,128)S(1)}, u32[]{:S(2)}) copy-start(f32[4,64,128]{2,1,0:T(8,128)S(1)} %collective-permute-done.24.refs_6_) | copy-start | bytes 393220
  93.0 0.6 copy-start.11
  93.1 0.6 copy-start.12

commit v4 on v3

--- a/solution.py
+++ b/solution.py
@@ -168,7 +168,7 @@
     lead = plane // steps
 
     theirs = swap(lax.dynamic_slice_in_dim(logder, (1 - core) * half, half, 1), 1)
-    sums = after(jnp.sum(logder, axis=0)[None], theirs)
+    sums = jnp.sum(logder, axis=0)[None]
     stride = 4
     while stride < nblocks:
         radix = min(4, nblocks // stride)
@@ -225,7 +225,7 @@
     )
     total = exchange(keep, send)
     last = messages(total, shard)
-    shares = [messages(after(exchange(*own), total), shard)]
+    shares = [messages(exchange(after(own[0], total), own[1]), shard)]
     pending = last
 
     mean = after(mean, total)

time: 96.7 us -> 95.1 us (0.983)
  waiting for transfers between devices: 39.5 us -> 37.1 us
    ppermute x11, waiting for transfers between devices: 9.85 us -> 8.4 us  [swap(): lax.ppermute(value, 'blk', [(k, k ^ mask) for k in range(lax.axis_size('b...]
    ppermute x9, waiting for transfers between devices: 2.27 us -> 1.25 us  [hop(): return lax.ppermute(value, ('blk', 'par'), pairs)]
  transfers between devices with their start and end apart: 27 -> 27, of which waited for: 12 -> 10; matrix products, arithmetic and copies ran while one was open for 6% -> 6% of each run, Pallas kernels for 2% -> 2%
where the time goes in v4:
time: 95.1 us; the launch traced here: 94.2 us
  starting transfers between devices  39.5 us (42%)
  waiting for transfers between devices  37.1 us (39%)
  Pallas kernels  9.67 us (10%)
  local copies, waits for them, and re-layouts  4.43 us (5%)
  other arithmetic  3.34 us (4%)
    ppermute x7, waiting for transfers between devices, shift(): lax.ppermute(value, 'blk', [(k, (k + steps) % count) for k in range(count)])  27.4 us
    ppermute x7, starting transfers between devices, shift(): lax.ppermute(value, 'blk', [(k, (k + steps) % count) for k in range(count)])  18.4 us
    ppermute x9, starting transfers between devices, hop(): return lax.ppermute(value, ('blk', 'par'), pairs)  10.6 us
    ppermute x11, starting transfers between devices, swap(): lax.ppermute(value, 'blk', [(k, k ^ mask) for k in range(lax.axis_size('b...  10.5 us
    ppermute x11, waiting for transfers between devices, swap(): lax.ppermute(value, 'blk', [(k, k ^ mask) for k in range(lax.axis_size('b...  8.4 us
    pallas_call x4, Pallas kernels, call(): pl.pallas_call(kernel, out_shape=outs, in_specs=[SMEM] * len(scalars) + [...  7.49 us
    add x3, other arithmetic, exchange(): return keep + swap(send, 1)  2.51 us
    pallas_call x1, Pallas kernels, on_device(): pl.pallas_call(functools.partial(final_kernel, factor, counts), out_shape...  2.18 us
  transfers between devices with their start and end apart: 27, of which 10 were waited for; matrix products, arithmetic and copies ran while one was open for 6% of the time, Pallas kernels for 2%

profile of v4, /device:TPU:0, one launch (start us, length us, event | category | flops | bytes accessed | tf_op | source)
XLA Modules:
  0.0 94.2 jit_solution(4307836457940662371)
XLA Ops:
  0.0 1.3 %constant_dynamic-slice_fusion.6 = f32[128,1536]{1,0:T(8,128)S(1)} fusion(f32[128,3072]{1,0:T(8,128)} %param.1, s32[]{:T(128)S(6)} %select_n.113), kind=kLoop, calls=%fused_computation.32 | loop fusion | bytes 1572868 | tf_op jit(solution)/shard_map/dynamic_slice | solution.py:170
  1.3 0.5 collective-permute-start
  1.8 0.1 reduce_sum.9
  1.9 4.9 %collective-permute-start.5 = (f32[1,3072]{1,0:T(1,128)S(1)}, f32[1,3072]{1,0:T(1,128)S(1)}, u32[]{:S(2)}, u32[]{:S(2)}) collective-permute-start(f32[1,3072]{1,0:T(1,128)S(1)} %bitcast.48), channel_id=1, source_target_pairs={{0,24},{2,26},{4,28},{6,30},{8,16},{10,18},{12,20},{14,22},{16,8},... | collective-permute-start | bytes 36872 | tf_op jit(solution)/shard_map/ppermute | solution.py:11
  6.8 0.6 collective-permute-start.3
  7.5 0.1 dynamic-slice_bitcast_fusion.5
  7.6 0.1 dynamic-slice_bitcast_fusion.4
  7.7 1.7 %collective-permute-start.1 = (f32[2,128,384]{2,1,0:T(8,128)S(1)}, f32[2,128,384]{2,1,0:T(8,128)S(1)}, u32[]{:S(2)}, u32[]{:S(2)}) collective-permute-start(f32[2,128,384]{2,1,0:T(8,128)S(1)} %pad_maximum_fusion.1), channel_id=1, source_target_pairs={{0,4},{2,6},{4,0},{6,2},{8,12},{10,14},{12,8},{14,10},{16,20},{18,... | collective-permute-start | bytes 1179656 | tf_op jit(solution)/shard_map/ppermute | solution.py:11
  9.5 3.7 %collective-permute-start.8 = (f32[2,128,384]{2,1,0:T(8,128)S(1)}, f32[2,128,384]{2,1,0:T(8,128)S(1)}, u32[]{:S(2)}, u32[]{:S(2)}) collective-permute-start(f32[2,128,384]{2,1,0:T(8,128)S(1)} %pad_maximum_fusion.near0), channel_id=1, source_target_pairs={{0,24},{2,26},{4,28},{6,30},{8,0},{10,2},{12,4},{14,6},{16,8},{18,... | collective-permute-start | bytes 1179656 | tf_op jit(solution)/shard_map/ppermute | solution.py:16
  13.1 0.0 collective-permute-done.4
  13.1 0.0 collective-permute-done.3
  13.2 5.3 %collective-permute-done.1.far0 = f32[2,128,384]{2,1,0:T(8,128)S(1)} collective-permute-done((f32[2,128,384]{2,1,0:T(8,128)S(1)}, f32[2,128,384]{2,1,0:T(8,128)S(1)}, u32[]{:S(2)}, u32[]{:S(2)}) %collective-permute-start.1) | collective-permute-done | bytes 393248 | tf_op jit(solution)/shard_map/ppermute | solution.py:11
  18.5 0.0 collective-permute-start.6
  18.5 1.6 %collective-permute-start.2 = (f32[2,128,384]{2,1,0:T(8,128)S(1)}, f32[2,128,384]{2,1,0:T(8,128)S(1)}, u32[]{:S(2)}, u32[]{:S(2)}) collective-permute-start(f32[2,128,384]{2,1,0:T(8,128)S(1)} %pad_maximum_fusion.3), channel_id=1, source_target_pairs={{0,4},{2,6},{4,0},{6,2},{8,12},{10,14},{12,8},{14,10},{16,20},{18,... | collective-permute-start | bytes 1179656 | tf_op jit(solution)/shard_map/ppermute | solution.py:11
  20.1 3.5 %collective-permute-start.10 = (f32[2,128,384]{2,1,0:T(8,128)S(1)}, f32[2,128,384]{2,1,0:T(8,128)S(1)}, u32[]{:S(2)}, u32[]{:S(2)}) collective-permute-start(f32[2,128,384]{2,1,0:T(8,128)S(1)} %collective-permute-done.1.far0), channel_id=1, source_target_pairs={{0,24},{2,26},{4,28},{6,30},{8,0},{10,2},{12,4},{14,6},{16,8},{18,... | collective-permute-start | bytes 1179656 | tf_op jit(solution)/shard_map/ppermute | solution.py:16
  23.6 1.5 %collective-permute-start.9 = (f32[2,128,384]{2,1,0:T(8,128)S(1)}, f32[2,128,384]{2,1,0:T(8,128)S(1)}, u32[]{:S(2)}, u32[]{:S(2)}) collective-permute-start(f32[2,128,384]{2,1,0:T(8,128)S(1)} %collective-permute-done.8.refs_0_), channel_id=1, source_target_pairs={{0,24},{2,26},{4,28},{6,30},{8,0},{10,2},{12,4},{14,6},{16,8},{18,... | collective-permute-start | bytes 1179656 | tf_op jit(solution)/shard_map/ppermute | solution.py:16
  25.1 0.0 collective-permute-done.6
  25.1 7.9 %collective-permute-done.10.refs_0_ = f32[2,128,384]{2,1,0:T(8,128)S(1)} collective-permute-done((f32[2,128,384]{2,1,0:T(8,128)S(1)}, f32[2,128,384]{2,1,0:T(8,128)S(1)}, u32[]{:S(2)}, u32[]{:S(2)}) %collective-permute-start.10) | collective-permute-done | bytes 393248 | tf_op jit(solution)/shard_map/ppermute | solution.py:16
  33.0 4.3 %collective-permute-start.11 = (f32[2,128,384]{2,1,0:T(8,128)S(1)}, f32[2,128,384]{2,1,0:T(8,128)S(1)}, u32[]{:S(2)}, u32[]{:S(2)}) collective-permute-start(f32[2,128,384]{2,1,0:T(8,128)S(1)} %collective-permute-done.10.refs_0_), channel_id=1, source_target_pairs={{0,24},{2,26},{4,28},{6,30},{8,0},{10,2},{12,4},{14,6},{16,8},{18,... | collective-permute-start | bytes 1179656 | tf_op jit(solution)/shard_map/ppermute | solution.py:16
  37.3 0.5 collective-permute-start.7
  37.9 3.1 %collective-permute-done.7 = f32[1,768]{1,0:T(1,128)S(1)} collective-permute-done((f32[1,768]{1,0:T(1,128)S(1)}, f32[1,768]{1,0:T(1,128)S(1)}, u32[]{:S(2)}, u32[]{:S(2)}) %collective-permute-start.7) | collective-permute-done | bytes 3104 | tf_op jit(solution)/shard_map/ppermute | solution.py:11
  40.9 0.5 collective-permute-done.9.near_ref
  41.5 7.7 %collective-permute-done.11.far_ref = f32[2,128,384]{2,1,0:T(8,128)S(1)} collective-permute-done((f32[2,128,384]{2,1,0:T(8,128)S(1)}, f32[2,128,384]{2,1,0:T(8,128)S(1)}, u32[]{:S(2)}, u32[]{:S(2)}) %collective-permute-start.11) | collective-permute-done | bytes 393248 | tf_op jit(solution)/shard_map/ppermute | solution.py:16
  49.2 0.0 collective-permute-done.2.far1
  49.2 2.7 %shard_map.17 = (f32[2,2,4,64,128]{4,3,2,1,0:T(8,128)S(1)}, f32[2,2,4,64,128]{4,3,2,1,0:T(8,128)}, bf16[2,2,256,384]{3,2,1,0:T(8,128)(2,1)S(1)}, bf16[2,2,256,384]{3,2,1,0:T(8,128)(2,1)S(1)}) custom-call(f32[2,128,384]{2,1,0:T(8,128)S(1)} %pad_maximum_fusion.near0, f32[2,128,384]{2,1,0:T(8,128)S(1)} %collective-permute-done.1.far0, ...), custom_call_target="tpu_custom_call" | custom-call | tf_op jit(solution)/shard_map/pallas_call | solution.py:113
  51.9 2.8 %shard_map.18 = (f32[2,2,8,64,128]{4,3,2,1,0:T(8,128)S(1)}, f32[2,2,8,64,128]{4,3,2,1,0:T(8,128)}) custom-call(f32[2,1,384]{2,1,0:T(1,128)S(1)} %pad_maximum_fusion.4.mean_ref, bf16[2,2,256,384]{3,2,1,0:T(8,128)(2,1)S(1)} %get-tuple-element.25.high_ref, bf16[2,2,256,384]{3,2,1,0:T(8,128)(2,1)S(1)} %get-tuple-element.26.low_ref, ...), custom_call_target="tpu_custom_call" | custom-call | tf_op jit(solution)/shard_map/pallas_call | solution.py:113
  54.8 0.5 collective-permute-start.13
  55.3 4.3 %collective-permute-start.18 = (f32[2,128,384]{2,1,0:T(8,128)S(1)}, f32[2,128,384]{2,1,0:T(8,128)S(1)}, u32[]{:S(2)}, u32[]{:S(2)}) collective-permute-start(f32[2,128,384]{2,1,0:T(8,128)S(1)} %pad_maximum_fusion.2.near1), channel_id=1, source_target_pairs={{0,24},{2,26},{4,28},{6,30},{8,0},{10,2},{12,4},{14,6},{16,8},{18,... | collective-permute-start | bytes 1179656 | tf_op jit(solution)/shard_map/ppermute | solution.py:16
  59.5 0.0 collective-permute-start.17
  59.6 0.0 collective-permute-done.12
  59.6 1.4 %add.197 = f32[2,2,8,64,128]{4,3,2,1,0:T(8,128)S(1)} add(f32[2,2,8,64,128]{4,3,2,1,0:T(8,128)S(1)} %get-tuple-element.27, f32[2,2,8,64,128]{4,3,2,1,0:T(8,128)} %collective-permute-done.12) | non-fusion elementwise | flops 262144 | bytes 3145728 | tf_op jit(solution)/shard_map/add | solution.py:124
  60.9 0.1 fusion.5
  61.1 1.6 %collective-permute-start.22 = (f32[8,64,128]{2,1,0:T(8,128)S(1)}, f32[8,64,128]{2,1,0:T(8,128)S(1)}, u32[]{:S(2)}, u32[]{:S(2)}) collective-permute-start(f32[8,64,128]{2,1,0:T(8,128)S(1)} %dynamic-slice_bitcast_fusion), channel_id=1, source_target_pairs={{0,1},{1,0},{2,3},{3,2},{4,5},{5,4},{6,7},{7,6},{8,9},{9,8},{10,11... | collective-permute-start | bytes 786440 | tf_op jit(solution)/shard_map/ppermute | solution.py:26
  62.7 0.6 collective-permute-start.20
  63.2 1.5 %collective-permute-start.21 = (f32[8,64,128]{2,1,0:T(8,128)S(1)}, f32[8,64,128]{2,1,0:T(8,128)S(1)}, u32[]{:S(2)}, u32[]{:S(2)}) collective-permute-start(f32[8,64,128]{2,1,0:T(8,128)S(1)} %get-tuple-element.54), channel_id=1, source_target_pairs={{0,5},{1,4},{2,7},{3,6},{4,1},{5,0},{6,3},{7,2},{8,13},{9,12},{10,... | collective-permute-start | bytes 786440 | tf_op jit(solution)/shard_map/ppermute | solution.py:26
  64.7 1.1 %add.198 = f32[2,2,4,64,128]{4,3,2,1,0:T(8,128)S(1)} add(f32[2,2,4,64,128]{4,3,2,1,0:T(8,128)S(1)} %get-tuple-element.29, f32[2,2,4,64,128]{4,3,2,1,0:T(8,128)} %collective-permute-done.13) | non-fusion elementwise | flops 131072 | bytes 1572864 | tf_op jit(solution)/shard_map/add | solution.py:124
  65.9 3.1 %collective-permute-done.18.refs_1_ = f32[2,128,384]{2,1,0:T(8,128)S(1)} collective-permute-done((f32[2,128,384]{2,1,0:T(8,128)S(1)}, f32[2,128,384]{2,1,0:T(8,128)S(1)}, u32[]{:S(2)}, u32[]{:S(2)}) %collective-permute-start.18) | collective-permute-done | bytes 393248 | tf_op jit(solution)/shard_map/ppermute | solution.py:16
  69.0 1.4 %collective-permute-start.15 = (f32[4,64,128]{2,1,0:T(8,128)S(1)}, f32[4,64,128]{2,1,0:T(8,128)S(1)}, u32[]{:S(2)}, u32[]{:S(2)}) collective-permute-start(f32[4,64,128]{2,1,0:T(8,128)S(1)} %get-tuple-element.65), channel_id=1, source_target_pairs={{0,5},{1,4},{2,7},{3,6},{4,1},{5,0},{6,3},{7,2},{8,13},{9,12},{10,... | collective-permute-start | bytes 393224 | tf_op jit(solution)/shard_map/ppermute | solution.py:26
  70.5 1.0 %shard_map.19 = (f32[2,2,4,64,128]{4,3,2,1,0:T(8,128)S(1)}, f32[2,2,4,64,128]{4,3,2,1,0:T(8,128)S(1)}) custom-call(s32[1]{0:T(128)} %bitcast.15.flag_ref, f32[2,1,384]{2,1,0:T(1,128)S(1)} %pad_maximum_fusion.4.mean_ref, bf16[2,2,256,384]{3,2,1,0:T(8,128)(2,1)S(1)} %get-tuple-element.25.high_ref, bf16[2,2,256,384]{3,2,1,0:T(8,128)(2,1)S(1)} %get-tuple-element.26.low_ref, ...), custom_call_target="tpu_custom_call" | custom-call | tf_op jit(solution)/shard_map/pallas_call | solution.py:113
  71.5 5.1 %collective-permute-done.17.refs_1_ = f32[2,128,384]{2,1,0:T(8,128)S(1)} collective-permute-done((f32[2,128,384]{2,1,0:T(8,128)}, f32[2,128,384]{2,1,0:T(8,128)S(1)}, u32[]{:S(2)}, u32[]{:S(2)}) %collective-permute-start.17) | collective-permute-done | bytes 393248 | tf_op jit(solution)/shard_map/ppermute | solution.py:16
  76.6 1.0 %shard_map.20 = (f32[2,2,4,64,128]{4,3,2,1,0:T(8,128)S(1)}, f32[2,2,4,64,128]{4,3,2,1,0:T(8,128)S(1)}) custom-call(s32[1]{0:T(128)} %bitcast.15.flag_ref, f32[2,1,384]{2,1,0:T(1,128)S(1)} %pad_maximum_fusion.4.mean_ref, bf16[2,2,256,384]{3,2,1,0:T(8,128)(2,1)S(1)} %get-tuple-element.25.high_ref, bf16[2,2,256,384]{3,2,1,0:T(8,128)(2,1)S(1)} %get-tuple-element.26.low_ref, ...), custom_call_target="tpu_custom_call" | custom-call | tf_op jit(solution)/shard_map/pallas_call | solution.py:113
  77.6 0.1 collective-permute-start.19
  77.7 0.7 dynamic-slice_bitcast_fusion.16
  78.4 0.5 collective-permute-start.14
  78.9 0.0 collective-permute-done.20
  78.9 1.5 %collective-permute-start.16 = (f32[4,64,128]{2,1,0:T(8,128)S(1)}, f32[4,64,128]{2,1,0:T(8,128)S(1)}, u32[]{:S(2)}, u32[]{:S(2)}) collective-permute-start(f32[4,64,128]{2,1,0:T(8,128)S(1)} %get-tuple-element.63), channel_id=1, source_target_pairs={{0,1},{1,0},{2,3},{3,2},{4,5},{5,4},{6,7},{7,6},{8,9},{9,8},{10,11... | collective-permute-start | bytes 393224 | tf_op jit(solution)/shard_map/ppermute | solution.py:26
  80.4 0.0 collective-permute-done.21
  80.4 0.1 add_add_fusion
  80.5 0.7 fusion.8
  81.1 1.2 %collective-permute-start.26 = (f32[4,64,128]{2,1,0:T(8,128)S(1)}, f32[4,64,128]{2,1,0:T(8,128)S(1)}, u32[]{:S(2)}, u32[]{:S(2)}) collective-permute-start(f32[4,64,128]{2,1,0:T(8,128)S(1)} %get-tuple-element.57), channel_id=1, source_target_pairs={{0,16},{2,18},{4,20},{6,22},{8,24},{10,26},{12,28},{14,30},{16,0},... | collective-permute-start | bytes 393224 | tf_op jit(solution)/shard_map/ppermute | solution.py:16
  82.3 0.0 collective-permute-done.19
  82.3 0.1 add.207
  82.5 1.6 %collective-permute-start.24 = (f32[4,64,128]{2,1,0:T(8,128)S(1)}, f32[4,64,128]{2,1,0:T(8,128)S(1)}, u32[]{:S(2)}, u32[]{:S(2)}) collective-permute-start(f32[4,64,128]{2,1,0:T(8,128)S(1)} %get-tuple-element.61), channel_id=1, source_target_pairs={{0,5},{1,4},{2,7},{3,6},{4,1},{5,0},{6,3},{7,2},{8,13},{9,12},{10,... | collective-permute-start | bytes 393224 | tf_op jit(solution)/shard_map/ppermute | solution.py:26
  84.0 0.7 dynamic-slice_bitcast_fusion.12
  84.7 0.0 collective-permute-done.15.refs_2_
  84.7 0.5 collective-permute-start.23
  85.2 1.5 %collective-permute-start.25 = (f32[4,64,128]{2,1,0:T(8,128)S(1)}, f32[4,64,128]{2,1,0:T(8,128)S(1)}, u32[]{:S(2)}, u32[]{:S(2)}) collective-permute-start(f32[4,64,128]{2,1,0:T(8,128)S(1)} %get-tuple-element.59), channel_id=1, source_target_pairs={{0,1},{1,0},{2,3},{3,2},{4,5},{5,4},{6,7},{7,6},{8,9},{9,8},{10,11... | collective-permute-start | bytes 393224 | tf_op jit(solution)/shard_map/ppermute | solution.py:26
  86.7 0.5 xor_add_fusion.where_ref
  87.2 2.9 %collective-permute-done.26.refs_9_ = f32[4,64,128]{2,1,0:T(8,128)S(1)} collective-permute-done((f32[4,64,128]{2,1,0:T(8,128)S(1)}, f32[4,64,128]{2,1,0:T(8,128)S(1)}, u32[]{:S(2)}, u32[]{:S(2)}) %collective-permute-start.26) | collective-permute-done | bytes 131104 | tf_op jit(solution)/shard_map/ppermute | solution.py:16
  90.2 1.1 %collective-permute-done.23.refs_5_ = f32[4,64,128]{2,1,0:T(8,128)S(1)} collective-permute-done((f32[4,64,128]{2,1,0:T(8,128)S(1)}, f32[4,64,128]{2,1,0:T(8,128)S(1)}, u32[]{:S(2)}, u32[]{:S(2)}) %collective-permute-start.23) | collective-permute-done | bytes 131104 | tf_op jit(solution)/shard_map/ppermute | solution.py:26
  91.3 0.1 collective-permute-done.25.refs_7_
  91.4 0.5 copy-done.11
  91.9 0.1 copy-done.12
  92.1 2.2 %shard_map.21 = f32[9,64,128]{2,1,0:T(8,128)} custom-call(s32[9]{0:T(128)} %xor_add_fusion.where_ref, f32[4,64,128]{2,1,0:T(8,128)} %get-tuple-element.64.refs_0_, f32[4,64,128]{2,1,0:T(8,128)} %copy-done.7, f32[4,64,128]{2,1,0:T(8,128)} %copy-done.6, f32[4,64,128]{2,1,0:T(8,128)} %copy-done.8, f32[4,64,128]{2,1,0:T(8,128)} %get-tuple-element.60.refs_4_, ...), custom_call_target="tpu_custom_call" | custom-call | tf_op jit(solution)/shard_map/pallas_call | solution.py:261
  (52 shorter events, 0.4 us)
Async XLA Ops:
  0.0 1.8 %copy-start.5 = (f32[128,3072]{1,0:T(8,128)S(1)}, f32[128,3072]{1,0:T(8,128)}, u32[]{:S(2)}) copy-start(f32[128,3072]{1,0:T(8,128)} %param.1) | copy-start | bytes 4718596
  1.3 6.3 %collective-permute-start = (f32[128,1536]{1,0:T(8,128)S(1)}, f32[128,1536]{1,0:T(8,128)S(1)}, u32[]{:S(2)}, u32[]{:S(2)}) collective-permute-start(f32[128,1536]{1,0:T(8,128)S(1)} %constant_dynamic-slice_fusion.6), channel_id=1, source_target_pairs={{0,2},{2,0},{4,6},{6,4},{8,10},{10,8},{12,14},{14,12},{16,18},{18,... | collective-permute-start | bytes 2359304 | tf_op jit(solution)/shard_map/ppermute | solution.py:11
  1.9 11.2 %collective-permute-start.5 = (f32[1,3072]{1,0:T(1,128)S(1)}, f32[1,3072]{1,0:T(1,128)S(1)}, u32[]{:S(2)}, u32[]{:S(2)}) collective-permute-start(f32[1,3072]{1,0:T(1,128)S(1)} %bitcast.48), channel_id=1, source_target_pairs={{0,24},{2,26},{4,28},{6,30},{8,16},{10,18},{12,20},{14,22},{16,8},... | collective-permute-start | bytes 36872 | tf_op jit(solution)/shard_map/ppermute | solution.py:11
  6.8 6.3 %collective-permute-start.4 = (f32[1,3072]{1,0:T(1,128)S(1)}, f32[1,3072]{1,0:T(1,128)S(1)}, u32[]{:S(2)}, u32[]{:S(2)}) collective-permute-start(f32[1,3072]{1,0:T(1,128)S(1)} %bitcast.49), channel_id=1, source_target_pairs={{0,16},{2,18},{4,20},{6,22},{8,24},{10,26},{12,28},{14,30},{16,0},... | collective-permute-start | bytes 36872 | tf_op jit(solution)/shard_map/ppermute | solution.py:11
  6.8 6.3 %collective-permute-start.3 = (f32[1,3072]{1,0:T(1,128)S(1)}, f32[1,3072]{1,0:T(1,128)S(1)}, u32[]{:S(2)}, u32[]{:S(2)}) collective-permute-start(f32[1,3072]{1,0:T(1,128)S(1)} %bitcast.50), channel_id=1, source_target_pairs={{0,8},{2,10},{4,12},{6,14},{8,0},{10,2},{12,4},{14,6},{16,24},{18,... | collective-permute-start | bytes 36872 | tf_op jit(solution)/shard_map/ppermute | solution.py:11
  7.7 10.8 %collective-permute-start.1 = (f32[2,128,384]{2,1,0:T(8,128)S(1)}, f32[2,128,384]{2,1,0:T(8,128)S(1)}, u32[]{:S(2)}, u32[]{:S(2)}) collective-permute-start(f32[2,128,384]{2,1,0:T(8,128)S(1)} %pad_maximum_fusion.1), channel_id=1, source_target_pairs={{0,4},{2,6},{4,0},{6,2},{8,12},{10,14},{12,8},{14,10},{16,20},{18,... | collective-permute-start | bytes 1179656 | tf_op jit(solution)/shard_map/ppermute | solution.py:11
  9.5 14.1 %collective-permute-start.8 = (f32[2,128,384]{2,1,0:T(8,128)S(1)}, f32[2,128,384]{2,1,0:T(8,128)S(1)}, u32[]{:S(2)}, u32[]{:S(2)}) collective-permute-start(f32[2,128,384]{2,1,0:T(8,128)S(1)} %pad_maximum_fusion.near0), channel_id=1, source_target_pairs={{0,24},{2,26},{4,28},{6,30},{8,0},{10,2},{12,4},{14,6},{16,8},{18,... | collective-permute-start | bytes 1179656 | tf_op jit(solution)/shard_map/ppermute | solution.py:16
  18.5 6.6 %collective-permute-start.6 = (f32[1,1536]{1,0:T(1,128)S(1)}, f32[1,1536]{1,0:T(1,128)S(1)}, u32[]{:S(2)}, u32[]{:S(2)}) collective-permute-start(f32[1,1536]{1,0:T(1,128)S(1)} %constant_dynamic-slice_fusion.4), channel_id=1, source_target_pairs={{0,2},{2,0},{4,6},{6,4},{8,10},{10,8},{12,14},{14,12},{16,18},{18,... | collective-permute-start | bytes 18440 | tf_op jit(solution)/shard_map/ppermute | solution.py:11
  18.5 30.7 %collective-permute-start.2 = (f32[2,128,384]{2,1,0:T(8,128)S(1)}, f32[2,128,384]{2,1,0:T(8,128)S(1)}, u32[]{:S(2)}, u32[]{:S(2)}) collective-permute-start(f32[2,128,384]{2,1,0:T(8,128)S(1)} %pad_maximum_fusion.3), channel_id=1, source_target_pairs={{0,4},{2,6},{4,0},{6,2},{8,12},{10,14},{12,8},{14,10},{16,20},{18,... | collective-permute-start | bytes 1179656 | tf_op jit(solution)/shard_map/ppermute | solution.py:11
  20.1 12.9 %collective-permute-start.10 = (f32[2,128,384]{2,1,0:T(8,128)S(1)}, f32[2,128,384]{2,1,0:T(8,128)S(1)}, u32[]{:S(2)}, u32[]{:S(2)}) collective-permute-start(f32[2,128,384]{2,1,0:T(8,128)S(1)} %collective-permute-done.1.far0), channel_id=1, source_target_pairs={{0,24},{2,26},{4,28},{6,30},{8,0},{10,2},{12,4},{14,6},{16,8},{18,... | collective-permute-start | bytes 1179656 | tf_op jit(solution)/shard_map/ppermute | solution.py:16
  23.6 25.6 %copy-start.3 = (f32[2,128,384]{2,1,0:T(8,128)}, f32[2,128,384]{2,1,0:T(8,128)S(1)}, u32[]{:S(2)}) copy-start(f32[2,128,384]{2,1,0:T(8,128)S(1)} %collective-permute-done.8.refs_0_) | copy-start | bytes 1179652
  23.6 17.9 %collective-permute-start.9 = (f32[2,128,384]{2,1,0:T(8,128)S(1)}, f32[2,128,384]{2,1,0:T(8,128)S(1)}, u32[]{:S(2)}, u32[]{:S(2)}) collective-permute-start(f32[2,128,384]{2,1,0:T(8,128)S(1)} %collective-permute-done.8.refs_0_), channel_id=1, source_target_pairs={{0,24},{2,26},{4,28},{6,30},{8,0},{10,2},{12,4},{14,6},{16,8},{18,... | collective-permute-start | bytes 1179656 | tf_op jit(solution)/shard_map/ppermute | solution.py:16
  33.0 16.2 %copy-start = (f32[2,128,384]{2,1,0:T(8,128)}, f32[2,128,384]{2,1,0:T(8,128)S(1)}, u32[]{:S(2)}) copy-start(f32[2,128,384]{2,1,0:T(8,128)S(1)} %collective-permute-done.10.refs_0_) | copy-start | bytes 1179652
  33.0 16.1 %collective-permute-start.11 = (f32[2,128,384]{2,1,0:T(8,128)S(1)}, f32[2,128,384]{2,1,0:T(8,128)S(1)}, u32[]{:S(2)}, u32[]{:S(2)}) collective-permute-start(f32[2,128,384]{2,1,0:T(8,128)S(1)} %collective-permute-done.10.refs_0_), channel_id=1, source_target_pairs={{0,24},{2,26},{4,28},{6,30},{8,0},{10,2},{12,4},{14,6},{16,8},{18,... | collective-permute-start | bytes 1179656 | tf_op jit(solution)/shard_map/ppermute | solution.py:16
  37.3 3.6 %collective-permute-start.7 = (f32[1,768]{1,0:T(1,128)S(1)}, f32[1,768]{1,0:T(1,128)S(1)}, u32[]{:S(2)}, u32[]{:S(2)}) collective-permute-start(f32[1,768]{1,0:T(1,128)S(1)} %constant_dynamic-slice_fusion.2), channel_id=1, source_target_pairs={{0,4},{2,6},{4,0},{6,2},{8,12},{10,14},{12,8},{14,10},{16,20},{18,... | collective-permute-start | bytes 9224 | tf_op jit(solution)/shard_map/ppermute | solution.py:11
  49.2 5.5 %copy-start.2 = (f32[2,128,384]{2,1,0:T(8,128)}, f32[2,128,384]{2,1,0:T(8,128)S(1)}, u32[]{:S(2)}) copy-start(f32[2,128,384]{2,1,0:T(8,128)S(1)} %collective-permute-done.2.far1) | copy-start | bytes 1179652
  54.8 4.8 %collective-permute-start.12 = (f32[2,2,8,64,128]{4,3,2,1,0:T(8,128)}, f32[2,2,8,64,128]{4,3,2,1,0:T(8,128)}, u32[]{:S(2)}, u32[]{:S(2)}) collective-permute-start(f32[2,2,8,64,128]{4,3,2,1,0:T(8,128)} %get-tuple-element.28), channel_id=1, source_target_pairs={{0,2},{2,0},{4,6},{6,4},{8,10},{10,8},{12,14},{14,12},{16,18},{18,... | collective-permute-start | bytes 3145736 | tf_op jit(solution)/shard_map/ppermute | solution.py:11
  54.8 8.5 %collective-permute-start.13 = (f32[2,2,4,64,128]{4,3,2,1,0:T(8,128)}, f32[2,2,4,64,128]{4,3,2,1,0:T(8,128)}, u32[]{:S(2)}, u32[]{:S(2)}) collective-permute-start(f32[2,2,4,64,128]{4,3,2,1,0:T(8,128)} %get-tuple-element.30), channel_id=1, source_target_pairs={{0,2},{2,0},{4,6},{6,4},{8,10},{10,8},{12,14},{14,12},{16,18},{18,... | collective-permute-start | bytes 1572872 | tf_op jit(solution)/shard_map/ppermute | solution.py:11
  55.3 13.8 %collective-permute-start.18 = (f32[2,128,384]{2,1,0:T(8,128)S(1)}, f32[2,128,384]{2,1,0:T(8,128)S(1)}, u32[]{:S(2)}, u32[]{:S(2)}) collective-permute-start(f32[2,128,384]{2,1,0:T(8,128)S(1)} %pad_maximum_fusion.2.near1), channel_id=1, source_target_pairs={{0,24},{2,26},{4,28},{6,30},{8,0},{10,2},{12,4},{14,6},{16,8},{18,... | collective-permute-start | bytes 1179656 | tf_op jit(solution)/shard_map/ppermute | solution.py:16
  59.5 17.1 %collective-permute-start.17 = (f32[2,128,384]{2,1,0:T(8,128)}, f32[2,128,384]{2,1,0:T(8,128)S(1)}, u32[]{:S(2)}, u32[]{:S(2)}) collective-permute-start(f32[2,128,384]{2,1,0:T(8,128)} %copy-done.2), channel_id=1, source_target_pairs={{0,24},{2,26},{4,28},{6,30},{8,0},{10,2},{12,4},{14,6},{16,8},{18,... | collective-permute-start | bytes 1179656 | tf_op jit(solution)/shard_map/ppermute | solution.py:16
  61.1 17.3 %collective-permute-start.22 = (f32[8,64,128]{2,1,0:T(8,128)S(1)}, f32[8,64,128]{2,1,0:T(8,128)S(1)}, u32[]{:S(2)}, u32[]{:S(2)}) collective-permute-start(f32[8,64,128]{2,1,0:T(8,128)S(1)} %dynamic-slice_bitcast_fusion), channel_id=1, source_target_pairs={{0,1},{1,0},{2,3},{3,2},{4,5},{5,4},{6,7},{7,6},{8,9},{9,8},{10,11... | collective-permute-start | bytes 786440 | tf_op jit(solution)/shard_map/ppermute | solution.py:26
  62.7 16.2 %collective-permute-start.20 = (f32[8,64,128]{2,1,0:T(8,128)S(1)}, f32[8,64,128]{2,1,0:T(8,128)S(1)}, u32[]{:S(2)}, u32[]{:S(2)}) collective-permute-start(f32[8,64,128]{2,1,0:T(8,128)S(1)} %get-tuple-element.53), channel_id=1, source_target_pairs={{0,4},{1,5},{2,6},{3,7},{4,0},{5,1},{6,2},{7,3},{8,12},{9,13},{10,... | collective-permute-start | bytes 786440 | tf_op jit(solution)/shard_map/ppermute | solution.py:26
  63.2 7.3 %copy-start.4 = (f32[2,128,384]{2,1,0:T(8,128)S(1)}, f32[2,128,384]{2,1,0:T(8,128)}, u32[]{:S(2)}) copy-start(f32[2,128,384]{2,1,0:T(8,128)} %copy-done.3) | copy-start | bytes 1179652
  63.2 17.2 %collective-permute-start.21 = (f32[8,64,128]{2,1,0:T(8,128)S(1)}, f32[8,64,128]{2,1,0:T(8,128)S(1)}, u32[]{:S(2)}, u32[]{:S(2)}) collective-permute-start(f32[8,64,128]{2,1,0:T(8,128)S(1)} %get-tuple-element.54), channel_id=1, source_target_pairs={{0,5},{1,4},{2,7},{3,6},{4,1},{5,0},{6,3},{7,2},{8,13},{9,12},{10,... | collective-permute-start | bytes 786440 | tf_op jit(solution)/shard_map/ppermute | solution.py:26
  65.9 10.7 %copy-start.1 = (f32[2,128,384]{2,1,0:T(8,128)S(1)}, f32[2,128,384]{2,1,0:T(8,128)}, u32[]{:S(2)}) copy-start(f32[2,128,384]{2,1,0:T(8,128)} %copy-done) | copy-start | bytes 1179652
  69.0 15.7 %collective-permute-start.15 = (f32[4,64,128]{2,1,0:T(8,128)S(1)}, f32[4,64,128]{2,1,0:T(8,128)S(1)}, u32[]{:S(2)}, u32[]{:S(2)}) collective-permute-start(f32[4,64,128]{2,1,0:T(8,128)S(1)} %get-tuple-element.65), channel_id=1, source_target_pairs={{0,5},{1,4},{2,7},{3,6},{4,1},{5,0},{6,3},{7,2},{8,13},{9,12},{10,... | collective-permute-start | bytes 393224 | tf_op jit(solution)/shard_map/ppermute | solution.py:26
  77.6 4.7 %collective-permute-start.19 = (f32[2,2,4,64,128]{4,3,2,1,0:T(8,128)S(1)}, f32[2,2,4,64,128]{4,3,2,1,0:T(8,128)S(1)}, u32[]{:S(2)}, u32[]{:S(2)}) collective-permute-start(f32[2,2,4,64,128]{4,3,2,1,0:T(8,128)S(1)} %get-tuple-element.37), channel_id=1, source_target_pairs={{0,2},{2,0},{4,6},{6,4},{8,10},{10,8},{12,14},{14,12},{16,18},{18,... | collective-permute-start | bytes 1572872 | tf_op jit(solution)/shard_map/ppermute | solution.py:11
  78.4 6.8 %collective-permute-start.14 = (f32[4,64,128]{2,1,0:T(8,128)S(1)}, f32[4,64,128]{2,1,0:T(8,128)S(1)}, u32[]{:S(2)}, u32[]{:S(2)}) collective-permute-start(f32[4,64,128]{2,1,0:T(8,128)S(1)} %get-tuple-element.66), channel_id=1, source_target_pairs={{0,4},{1,5},{2,6},{3,7},{4,0},{5,1},{6,2},{7,3},{8,12},{9,13},{10,... | collective-permute-start | bytes 393224 | tf_op jit(solution)/shard_map/ppermute | solution.py:26
  78.9 8.3 %collective-permute-start.16 = (f32[4,64,128]{2,1,0:T(8,128)S(1)}, f32[4,64,128]{2,1,0:T(8,128)S(1)}, u32[]{:S(2)}, u32[]{:S(2)}) collective-permute-start(f32[4,64,128]{2,1,0:T(8,128)S(1)} %get-tuple-element.63), channel_id=1, source_target_pairs={{0,1},{1,0},{2,3},{3,2},{4,5},{5,4},{6,7},{7,6},{8,9},{9,8},{10,11... | collective-permute-start | bytes 393224 | tf_op jit(solution)/shard_map/ppermute | solution.py:26
  81.1 9.0 %collective-permute-start.26 = (f32[4,64,128]{2,1,0:T(8,128)S(1)}, f32[4,64,128]{2,1,0:T(8,128)S(1)}, u32[]{:S(2)}, u32[]{:S(2)}) collective-permute-start(f32[4,64,128]{2,1,0:T(8,128)S(1)} %get-tuple-element.57), channel_id=1, source_target_pairs={{0,16},{2,18},{4,20},{6,22},{8,24},{10,26},{12,28},{14,30},{16,0},... | collective-permute-start | bytes 393224 | tf_op jit(solution)/shard_map/ppermute | solution.py:16
  82.5 7.7 %collective-permute-start.24 = (f32[4,64,128]{2,1,0:T(8,128)S(1)}, f32[4,64,128]{2,1,0:T(8,128)S(1)}, u32[]{:S(2)}, u32[]{:S(2)}) collective-permute-start(f32[4,64,128]{2,1,0:T(8,128)S(1)} %get-tuple-element.61), channel_id=1, source_target_pairs={{0,5},{1,4},{2,7},{3,6},{4,1},{5,0},{6,3},{7,2},{8,13},{9,12},{10,... | collective-permute-start | bytes 393224 | tf_op jit(solution)/shard_map/ppermute | solution.py:26
  84.7 6.7 %copy-start.6 = (f32[4,64,128]{2,1,0:T(8,128)}, f32[4,64,128]{2,1,0:T(8,128)S(1)}, u32[]{:S(2)}) copy-start(f32[4,64,128]{2,1,0:T(8,128)S(1)} %collective-permute-done.15.refs_2_) | copy-start | bytes 393220
  84.7 6.6 %collective-permute-start.23 = (f32[4,64,128]{2,1,0:T(8,128)S(1)}, f32[4,64,128]{2,1,0:T(8,128)S(1)}, u32[]{:S(2)}, u32[]{:S(2)}) collective-permute-start(f32[4,64,128]{2,1,0:T(8,128)S(1)} %get-tuple-element.62), channel_id=1, source_target_pairs={{0,4},{1,5},{2,6},{3,7},{4,0},{5,1},{6,2},{7,3},{8,12},{9,13},{10,... | collective-permute-start | bytes 393224 | tf_op jit(solution)/shard_map/ppermute | solution.py:26
  85.2 6.2 %copy-start.7 = (f32[4,64,128]{2,1,0:T(8,128)}, f32[4,64,128]{2,1,0:T(8,128)S(1)}, u32[]{:S(2)}) copy-start(f32[4,64,128]{2,1,0:T(8,128)S(1)} %collective-permute-done.14.refs_1_) | copy-start | bytes 393220
  85.2 6.2 %collective-permute-start.25 = (f32[4,64,128]{2,1,0:T(8,128)S(1)}, f32[4,64,128]{2,1,0:T(8,128)S(1)}, u32[]{:S(2)}, u32[]{:S(2)}) collective-permute-start(f32[4,64,128]{2,1,0:T(8,128)S(1)} %get-tuple-element.59), channel_id=1, source_target_pairs={{0,1},{1,0},{2,3},{3,2},{4,5},{5,4},{6,7},{7,6},{8,9},{9,8},{10,11... | collective-permute-start | bytes 393224 | tf_op jit(solution)/shard_map/ppermute | solution.py:26
  87.2 4.2 %copy-start.8 = (f32[4,64,128]{2,1,0:T(8,128)}, f32[4,64,128]{2,1,0:T(8,128)S(1)}, u32[]{:S(2)}) copy-start(f32[4,64,128]{2,1,0:T(8,128)S(1)} %collective-permute-done.16.refs_3_) | copy-start | bytes 393220
  90.2 1.3 %copy-start.9 = (f32[4,64,128]{2,1,0:T(8,128)}, f32[4,64,128]{2,1,0:T(8,128)S(1)}, u32[]{:S(2)}) copy-start(f32[4,64,128]{2,1,0:T(8,128)S(1)} %collective-permute-done.26.refs_9_) | copy-start | bytes 393220
  90.2 1.3 %copy-start.10 = (f32[4,64,128]{2,1,0:T(8,128)}, f32[4,64,128]{2,1,0:T(8,128)S(1)}, u32[]{:S(2)}) copy-start(f32[4,64,128]{2,1,0:T(8,128)S(1)} %collective-permute-done.24.refs_6_) | copy-start | bytes 393220
  91.3 0.6 copy-start.11
  91.4 0.6 copy-start.12

commit v5 on v4

--- a/solution.py
+++ b/solution.py
@@ -197,7 +197,7 @@
     sums = lax.dynamic_slice_in_dim(sums, side * quarter, quarter, 1) + swap(
         lax.dynamic_slice_in_dim(sums, (1 - side) * quarter, quarter, 1), 2
     )
-    mean = after(sums, *first[steps]) / (rows * nblocks)
+    mean = after(sums, first[1][1]) / (rows * nblocks)
     mean = jnp.stack(
         [lax.dynamic_slice_in_dim(mean, part * eighth, eighth, 1) for part in (lead, 1 - lead)]
     )
@@ -223,9 +223,10 @@
         (mean, high, low, *first[steps]),
         4 * flops,
     )
-    total = exchange(keep, send)
+    first_total = exchange(*own)
+    shares = [messages(first_total, shard)]
+    total = after(exchange(keep, send), first_total)
     last = messages(total, shard)
-    shares = [messages(exchange(after(own[0], total), own[1]), shard)]
     pending = last
 
     mean = after(mean, total)

time: 95.1 us -> 92.3 us (0.971)
  starting transfers between devices: 39.5 us -> 35.9 us
    ppermute x7, waiting for transfers between devices: 27.4 us -> 23.2 us  [shift(): lax.ppermute(value, 'blk', [(k, (k + steps) % count) for k in range(count)])]
    ppermute x11, waiting for transfers between devices: 8.4 us -> 12.4 us  [swap(): lax.ppermute(value, 'blk', [(k, k ^ mask) for k in range(lax.axis_size('b...]
    ppermute x7, starting transfers between devices: 18.4 us -> 15.7 us  [shift(): lax.ppermute(value, 'blk', [(k, (k + steps) % count) for k in range(count)])]
    ppermute x9, waiting for transfers between devices: 1.25 us -> 2.27 us  [hop(): return lax.ppermute(value, ('blk', 'par'), pairs)]
    ppermute x9, starting transfers between devices: 10.6 us -> 9.65 us  [hop(): return lax.ppermute(value, ('blk', 'par'), pairs)]
  transfers between devices with their start and end apart: 27 -> 27, of which waited for: 10 -> 12; matrix products, arithmetic and copies ran while one was open for 6% -> 6% of each run, Pallas kernels for 2% -> 5%
where the time goes in v5:
time: 92.3 us; the launch traced here: 91.5 us
  waiting for transfers between devices  37.8 us (41%)
  starting transfers between devices  35.9 us (39%)
  Pallas kernels  9.68 us (10%)
  local copies, waits for them, and re-layouts  4.44 us (5%)
  other arithmetic  3.34 us (4%)
    ppermute x7, waiting for transfers between devices, shift(): lax.ppermute(value, 'blk', [(k, (k + steps) % count) for k in range(count)])  23.2 us
    ppermute x7, starting transfers between devices, shift(): lax.ppermute(value, 'blk', [(k, (k + steps) % count) for k in range(count)])  15.7 us
    ppermute x11, waiting for transfers between devices, swap(): lax.ppermute(value, 'blk', [(k, k ^ mask) for k in range(lax.axis_size('b...  12.4 us
    ppermute x11, starting transfers between devices, swap(): lax.ppermute(value, 'blk', [(k, k ^ mask) for k in range(lax.axis_size('b...  10.6 us
    ppermute x9, starting transfers between devices, hop(): return lax.ppermute(value, ('blk', 'par'), pairs)  9.65 us
    pallas_call x4, Pallas kernels, call(): pl.pallas_call(kernel, out_shape=outs, in_specs=[SMEM] * len(scalars) + [...  7.5 us
    add x3, other arithmetic, exchange(): return keep + swap(send, 1)  2.52 us
    ppermute x9, waiting for transfers between devices, hop(): return lax.ppermute(value, ('blk', 'par'), pairs)  2.27 us
  transfers between devices with their start and end apart: 27, of which 12 were waited for; matrix products, arithmetic and copies ran while one was open for 6% of the time, Pallas kernels for 5%

profile of v5, /device:TPU:0, one launch (start us, length us, event | category | flops | bytes accessed | tf_op | source)
XLA Modules:
  0.0 91.5 jit_solution(16590924285897248691)
XLA Ops:
  0.0 1.3 %constant_dynamic-slice_fusion.6 = f32[128,1536]{1,0:T(8,128)S(1)} fusion(f32[128,3072]{1,0:T(8,128)} %param.1, s32[]{:T(128)S(6)} %select_n.113), kind=kLoop, calls=%fused_computation.32 | loop fusion | bytes 1572868 | tf_op jit(solution)/shard_map/dynamic_slice | solution.py:170
  1.3 0.5 collective-permute-start
  1.8 0.1 reduce_sum.9
  1.9 4.9 %collective-permute-start.5 = (f32[1,3072]{1,0:T(1,128)S(1)}, f32[1,3072]{1,0:T(1,128)S(1)}, u32[]{:S(2)}, u32[]{:S(2)}) collective-permute-start(f32[1,3072]{1,0:T(1,128)S(1)} %bitcast.48), channel_id=1, source_target_pairs={{0,24},{2,26},{4,28},{6,30},{8,16},{10,18},{12,20},{14,22},{16,8},... | collective-permute-start | bytes 36872 | tf_op jit(solution)/shard_map/ppermute | solution.py:11
  6.8 0.0 collective-permute-start.4
  6.8 0.6 collective-permute-start.3
  7.5 0.1 dynamic-slice_bitcast_fusion.5
  7.6 0.0 collective-permute-done
  7.6 0.1 dynamic-slice_bitcast_fusion.4
  7.7 1.7 %collective-permute-start.1 = (f32[2,128,384]{2,1,0:T(8,128)S(1)}, f32[2,128,384]{2,1,0:T(8,128)S(1)}, u32[]{:S(2)}, u32[]{:S(2)}) collective-permute-start(f32[2,128,384]{2,1,0:T(8,128)S(1)} %pad_maximum_fusion.1), channel_id=1, source_target_pairs={{0,4},{2,6},{4,0},{6,2},{8,12},{10,14},{12,8},{14,10},{16,20},{18,... | collective-permute-start | bytes 1179656 | tf_op jit(solution)/shard_map/ppermute | solution.py:11
  9.4 0.0 collective-permute-done.5
  9.4 2.0 %collective-permute-done.4 = f32[1,3072]{1,0:T(1,128)S(1)} collective-permute-done((f32[1,3072]{1,0:T(1,128)S(1)}, f32[1,3072]{1,0:T(1,128)S(1)}, u32[]{:S(2)}, u32[]{:S(2)}) %collective-permute-start.4) | collective-permute-done | bytes 12320 | tf_op jit(solution)/shard_map/ppermute | solution.py:11
  11.4 0.0 collective-permute-done.3
  11.5 1.7 %collective-permute-start.13 = (f32[2,128,384]{2,1,0:T(8,128)S(1)}, f32[2,128,384]{2,1,0:T(8,128)S(1)}, u32[]{:S(2)}, u32[]{:S(2)}) collective-permute-start(f32[2,128,384]{2,1,0:T(8,128)S(1)} %pad_maximum_fusion.near0), channel_id=1, source_target_pairs={{0,24},{2,26},{4,28},{6,30},{8,0},{10,2},{12,4},{14,6},{16,8},{18,... | collective-permute-start | bytes 1179656 | tf_op jit(solution)/shard_map/ppermute | solution.py:16
  13.2 5.3 %collective-permute-done.1.far0 = f32[2,128,384]{2,1,0:T(8,128)S(1)} collective-permute-done((f32[2,128,384]{2,1,0:T(8,128)S(1)}, f32[2,128,384]{2,1,0:T(8,128)S(1)}, u32[]{:S(2)}, u32[]{:S(2)}) %collective-permute-start.1) | collective-permute-done | bytes 393248 | tf_op jit(solution)/shard_map/ppermute | solution.py:11
  18.5 1.6 %collective-permute-start.2 = (f32[2,128,384]{2,1,0:T(8,128)S(1)}, f32[2,128,384]{2,1,0:T(8,128)S(1)}, u32[]{:S(2)}, u32[]{:S(2)}) collective-permute-start(f32[2,128,384]{2,1,0:T(8,128)S(1)} %pad_maximum_fusion.3), channel_id=1, source_target_pairs={{0,4},{2,6},{4,0},{6,2},{8,12},{10,14},{12,8},{14,10},{16,20},{18,... | collective-permute-start | bytes 1179656 | tf_op jit(solution)/shard_map/ppermute | solution.py:11
  20.1 3.5 %collective-permute-start.8 = (f32[2,128,384]{2,1,0:T(8,128)S(1)}, f32[2,128,384]{2,1,0:T(8,128)S(1)}, u32[]{:S(2)}, u32[]{:S(2)}) collective-permute-start(f32[2,128,384]{2,1,0:T(8,128)S(1)} %collective-permute-done.1.far0), channel_id=1, source_target_pairs={{0,24},{2,26},{4,28},{6,30},{8,0},{10,2},{12,4},{14,6},{16,8},{18,... | collective-permute-start | bytes 1179656 | tf_op jit(solution)/shard_map/ppermute | solution.py:16
  23.6 0.6 collective-permute-start.7
  24.2 0.0 collective-permute-done.13.refs_0_
  24.2 0.9 collective-permute-start.14
  25.1 5.1 %collective-permute-done.7 = f32[1,768]{1,0:T(1,128)S(1)} collective-permute-done((f32[1,768]{1,0:T(1,128)S(1)}, f32[1,768]{1,0:T(1,128)S(1)}, u32[]{:S(2)}, u32[]{:S(2)}) %collective-permute-start.7) | collective-permute-done | bytes 3104 | tf_op jit(solution)/shard_map/ppermute | solution.py:11
  30.2 2.9 %collective-permute-done.8.refs_0_ = f32[2,128,384]{2,1,0:T(8,128)S(1)} collective-permute-done((f32[2,128,384]{2,1,0:T(8,128)S(1)}, f32[2,128,384]{2,1,0:T(8,128)S(1)}, u32[]{:S(2)}, u32[]{:S(2)}) %collective-permute-start.8) | collective-permute-done | bytes 393248 | tf_op jit(solution)/shard_map/ppermute | solution.py:16
  33.0 4.3 %collective-permute-start.15 = (f32[2,128,384]{2,1,0:T(8,128)S(1)}, f32[2,128,384]{2,1,0:T(8,128)S(1)}, u32[]{:S(2)}, u32[]{:S(2)}) collective-permute-start(f32[2,128,384]{2,1,0:T(8,128)S(1)} %collective-permute-done.8.refs_0_), channel_id=1, source_target_pairs={{0,24},{2,26},{4,28},{6,30},{8,0},{10,2},{12,4},{14,6},{16,8},{18,... | collective-permute-start | bytes 1179656 | tf_op jit(solution)/shard_map/ppermute | solution.py:16
  37.3 0.0 collective-permute-done.2.far1
  37.4 2.7 %shard_map.17 = (f32[2,2,4,64,128]{4,3,2,1,0:T(8,128)S(1)}, f32[2,2,4,64,128]{4,3,2,1,0:T(8,128)}, bf16[2,2,256,384]{3,2,1,0:T(8,128)(2,1)S(1)}, bf16[2,2,256,384]{3,2,1,0:T(8,128)(2,1)S(1)}) custom-call(f32[2,128,384]{2,1,0:T(8,128)S(1)} %pad_maximum_fusion.near0, f32[2,128,384]{2,1,0:T(8,128)S(1)} %collective-permute-done.1.far0, ...), custom_call_target="tpu_custom_call" | custom-call | tf_op jit(solution)/shard_map/pallas_call | solution.py:113
  40.0 1.4 %collective-permute-done.14.near_ref = f32[2,128,384]{2,1,0:T(8,128)S(1)} collective-permute-done((f32[2,128,384]{2,1,0:T(8,128)S(1)}, f32[2,128,384]{2,1,0:T(8,128)S(1)}, u32[]{:S(2)}, u32[]{:S(2)}) %collective-permute-start.14) | collective-permute-done | bytes 393248 | tf_op jit(solution)/shard_map/ppermute | solution.py:16
  41.5 7.7 %collective-permute-done.15.far_ref = f32[2,128,384]{2,1,0:T(8,128)S(1)} collective-permute-done((f32[2,128,384]{2,1,0:T(8,128)S(1)}, f32[2,128,384]{2,1,0:T(8,128)S(1)}, u32[]{:S(2)}, u32[]{:S(2)}) %collective-permute-start.15) | collective-permute-done | bytes 393248 | tf_op jit(solution)/shard_map/ppermute | solution.py:16
  49.2 2.8 %shard_map.18 = (f32[2,2,8,64,128]{4,3,2,1,0:T(8,128)S(1)}, f32[2,2,8,64,128]{4,3,2,1,0:T(8,128)}) custom-call(f32[2,1,384]{2,1,0:T(1,128)S(1)} %pad_maximum_fusion.4.mean_ref, bf16[2,2,256,384]{3,2,1,0:T(8,128)(2,1)S(1)} %get-tuple-element.26.high_ref, bf16[2,2,256,384]{3,2,1,0:T(8,128)(2,1)S(1)} %get-tuple-element.27.low_ref, ...), custom_call_target="tpu_custom_call" | custom-call | tf_op jit(solution)/shard_map/pallas_call | solution.py:113
  52.0 0.5 collective-permute-start.9
  52.5 4.3 %collective-permute-start.18 = (f32[2,128,384]{2,1,0:T(8,128)S(1)}, f32[2,128,384]{2,1,0:T(8,128)S(1)}, u32[]{:S(2)}, u32[]{:S(2)}) collective-permute-start(f32[2,128,384]{2,1,0:T(8,128)S(1)} %pad_maximum_fusion.2.near1), channel_id=1, source_target_pairs={{0,24},{2,26},{4,28},{6,30},{8,0},{10,2},{12,4},{14,6},{16,8},{18,... | collective-permute-start | bytes 1179656 | tf_op jit(solution)/shard_map/ppermute | solution.py:16
  56.8 0.0 collective-permute-start.17
  56.8 0.0 collective-permute-done.9
  56.8 1.1 %add.197 = f32[2,2,4,64,128]{4,3,2,1,0:T(8,128)S(1)} add(f32[2,2,4,64,128]{4,3,2,1,0:T(8,128)S(1)} %get-tuple-element.24, f32[2,2,4,64,128]{4,3,2,1,0:T(8,128)} %collective-permute-done.9) | non-fusion elementwise | flops 131072 | bytes 1572864 | tf_op jit(solution)/shard_map/add | solution.py:124
  58.0 1.4 %add.206 = f32[2,2,8,64,128]{4,3,2,1,0:T(8,128)S(1)} add(f32[2,2,8,64,128]{4,3,2,1,0:T(8,128)S(1)} %get-tuple-element.28, f32[2,2,8,64,128]{4,3,2,1,0:T(8,128)} %collective-permute-done.16) | non-fusion elementwise | flops 262144 | bytes 3145728 | tf_op jit(solution)/shard_map/add | solution.py:124
  59.3 0.1 fusion.5
  59.4 1.6 %collective-permute-start.22 = (f32[8,64,128]{2,1,0:T(8,128)S(1)}, f32[8,64,128]{2,1,0:T(8,128)S(1)}, u32[]{:S(2)}, u32[]{:S(2)}) collective-permute-start(f32[8,64,128]{2,1,0:T(8,128)S(1)} %dynamic-slice_bitcast_fusion), channel_id=1, source_target_pairs={{0,1},{1,0},{2,3},{3,2},{4,5},{5,4},{6,7},{7,6},{8,9},{9,8},{10,11... | collective-permute-start | bytes 786440 | tf_op jit(solution)/shard_map/ppermute | solution.py:26
  61.0 0.6 collective-permute-start.20
  61.6 1.5 %collective-permute-start.21 = (f32[8,64,128]{2,1,0:T(8,128)S(1)}, f32[8,64,128]{2,1,0:T(8,128)S(1)}, u32[]{:S(2)}, u32[]{:S(2)}) collective-permute-start(f32[8,64,128]{2,1,0:T(8,128)S(1)} %get-tuple-element.54), channel_id=1, source_target_pairs={{0,5},{1,4},{2,7},{3,6},{4,1},{5,0},{6,3},{7,2},{8,13},{9,12},{10,... | collective-permute-start | bytes 786440 | tf_op jit(solution)/shard_map/ppermute | solution.py:26
  63.2 3.1 %collective-permute-done.18.refs_1_ = f32[2,128,384]{2,1,0:T(8,128)S(1)} collective-permute-done((f32[2,128,384]{2,1,0:T(8,128)S(1)}, f32[2,128,384]{2,1,0:T(8,128)S(1)}, u32[]{:S(2)}, u32[]{:S(2)}) %collective-permute-start.18) | collective-permute-done | bytes 393248 | tf_op jit(solution)/shard_map/ppermute | solution.py:16
  66.3 1.4 %collective-permute-start.11 = (f32[4,64,128]{2,1,0:T(8,128)S(1)}, f32[4,64,128]{2,1,0:T(8,128)S(1)}, u32[]{:S(2)}, u32[]{:S(2)}) collective-permute-start(f32[4,64,128]{2,1,0:T(8,128)S(1)} %get-tuple-element.65), channel_id=1, source_target_pairs={{0,5},{1,4},{2,7},{3,6},{4,1},{5,0},{6,3},{7,2},{8,13},{9,12},{10,... | collective-permute-start | bytes 393224 | tf_op jit(solution)/shard_map/ppermute | solution.py:26
  67.7 1.0 %shard_map.19 = (f32[2,2,4,64,128]{4,3,2,1,0:T(8,128)S(1)}, f32[2,2,4,64,128]{4,3,2,1,0:T(8,128)S(1)}) custom-call(s32[1]{0:T(128)} %bitcast.15.flag_ref, f32[2,1,384]{2,1,0:T(1,128)S(1)} %pad_maximum_fusion.4.mean_ref, bf16[2,2,256,384]{3,2,1,0:T(8,128)(2,1)S(1)} %get-tuple-element.26.high_ref, bf16[2,2,256,384]{3,2,1,0:T(8,128)(2,1)S(1)} %get-tuple-element.27.low_ref, ...), custom_call_target="tpu_custom_call" | custom-call | tf_op jit(solution)/shard_map/pallas_call | solution.py:113
  68.8 5.1 %collective-permute-done.17.refs_1_ = f32[2,128,384]{2,1,0:T(8,128)S(1)} collective-permute-done((f32[2,128,384]{2,1,0:T(8,128)}, f32[2,128,384]{2,1,0:T(8,128)S(1)}, u32[]{:S(2)}, u32[]{:S(2)}) %collective-permute-start.17) | collective-permute-done | bytes 393248 | tf_op jit(solution)/shard_map/ppermute | solution.py:16
  73.9 1.0 %shard_map.20 = (f32[2,2,4,64,128]{4,3,2,1,0:T(8,128)S(1)}, f32[2,2,4,64,128]{4,3,2,1,0:T(8,128)S(1)}) custom-call(s32[1]{0:T(128)} %bitcast.15.flag_ref, f32[2,1,384]{2,1,0:T(1,128)S(1)} %pad_maximum_fusion.4.mean_ref, bf16[2,2,256,384]{3,2,1,0:T(8,128)(2,1)S(1)} %get-tuple-element.26.high_ref, bf16[2,2,256,384]{3,2,1,0:T(8,128)(2,1)S(1)} %get-tuple-element.27.low_ref, ...), custom_call_target="tpu_custom_call" | custom-call | tf_op jit(solution)/shard_map/pallas_call | solution.py:113
  74.9 0.1 collective-permute-start.19
  75.0 0.7 dynamic-slice_bitcast_fusion.16
  75.7 0.0 collective-permute-done.22
  75.7 0.5 collective-permute-start.10
  76.2 1.0 %collective-permute-done.20 = f32[8,64,128]{2,1,0:T(8,128)S(1)} collective-permute-done((f32[8,64,128]{2,1,0:T(8,128)S(1)}, f32[8,64,128]{2,1,0:T(8,128)S(1)}, u32[]{:S(2)}, u32[]{:S(2)}) %collective-permute-start.20) | collective-permute-done | bytes 262176 | tf_op jit(solution)/shard_map/ppermute | solution.py:26
  77.2 0.5 collective-permute-start.12
  77.7 0.1 add_add_fusion
  77.8 0.7 fusion.8
  78.5 1.1 %collective-permute-start.26 = (f32[4,64,128]{2,1,0:T(8,128)S(1)}, f32[4,64,128]{2,1,0:T(8,128)S(1)}, u32[]{:S(2)}, u32[]{:S(2)}) collective-permute-start(f32[4,64,128]{2,1,0:T(8,128)S(1)} %get-tuple-element.57), channel_id=1, source_target_pairs={{0,16},{2,18},{4,20},{6,22},{8,24},{10,26},{12,28},{14,30},{16,0},... | collective-permute-start | bytes 393224 | tf_op jit(solution)/shard_map/ppermute | solution.py:16
  79.6 0.1 add.207
  79.7 1.6 %collective-permute-start.24 = (f32[4,64,128]{2,1,0:T(8,128)S(1)}, f32[4,64,128]{2,1,0:T(8,128)S(1)}, u32[]{:S(2)}, u32[]{:S(2)}) collective-permute-start(f32[4,64,128]{2,1,0:T(8,128)S(1)} %get-tuple-element.61), channel_id=1, source_target_pairs={{0,5},{1,4},{2,7},{3,6},{4,1},{5,0},{6,3},{7,2},{8,13},{9,12},{10,... | collective-permute-start | bytes 393224 | tf_op jit(solution)/shard_map/ppermute | solution.py:26
  81.3 0.7 dynamic-slice_bitcast_fusion.12
  82.0 1.0 %collective-permute-start.23 = (f32[4,64,128]{2,1,0:T(8,128)S(1)}, f32[4,64,128]{2,1,0:T(8,128)S(1)}, u32[]{:S(2)}, u32[]{:S(2)}) collective-permute-start(f32[4,64,128]{2,1,0:T(8,128)S(1)} %get-tuple-element.62), channel_id=1, source_target_pairs={{0,4},{1,5},{2,6},{3,7},{4,0},{5,1},{6,2},{7,3},{8,12},{9,13},{10,... | collective-permute-start | bytes 393224 | tf_op jit(solution)/shard_map/ppermute | solution.py:26
  83.0 1.0 %collective-permute-start.25 = (f32[4,64,128]{2,1,0:T(8,128)S(1)}, f32[4,64,128]{2,1,0:T(8,128)S(1)}, u32[]{:S(2)}, u32[]{:S(2)}) collective-permute-start(f32[4,64,128]{2,1,0:T(8,128)S(1)} %get-tuple-element.59), channel_id=1, source_target_pairs={{0,1},{1,0},{2,3},{3,2},{4,5},{5,4},{6,7},{7,6},{8,9},{9,8},{10,11... | collective-permute-start | bytes 393224 | tf_op jit(solution)/shard_map/ppermute | solution.py:26
  84.0 0.5 xor_add_fusion.where_ref
  84.5 2.9 %collective-permute-done.26.refs_9_ = f32[4,64,128]{2,1,0:T(8,128)S(1)} collective-permute-done((f32[4,64,128]{2,1,0:T(8,128)S(1)}, f32[4,64,128]{2,1,0:T(8,128)S(1)}, u32[]{:S(2)}, u32[]{:S(2)}) %collective-permute-start.26) | collective-permute-done | bytes 131104 | tf_op jit(solution)/shard_map/ppermute | solution.py:16
  87.4 1.1 %collective-permute-done.23.refs_5_ = f32[4,64,128]{2,1,0:T(8,128)S(1)} collective-permute-done((f32[4,64,128]{2,1,0:T(8,128)S(1)}, f32[4,64,128]{2,1,0:T(8,128)S(1)}, u32[]{:S(2)}, u32[]{:S(2)}) %collective-permute-start.23) | collective-permute-done | bytes 131104 | tf_op jit(solution)/shard_map/ppermute | solution.py:26
  88.6 0.1 collective-permute-done.25.refs_7_
  88.7 0.5 copy-done.11
  89.2 0.1 copy-done.12
  89.3 2.2 %shard_map.21 = f32[9,64,128]{2,1,0:T(8,128)} custom-call(s32[9]{0:T(128)} %xor_add_fusion.where_ref, f32[4,64,128]{2,1,0:T(8,128)} %get-tuple-element.64.refs_0_, f32[4,64,128]{2,1,0:T(8,128)} %copy-done.7, f32[4,64,128]{2,1,0:T(8,128)} %copy-done.6, f32[4,64,128]{2,1,0:T(8,128)} %copy-done.8, f32[4,64,128]{2,1,0:T(8,128)} %get-tuple-element.60.refs_4_, ...), custom_call_target="tpu_custom_call" | custom-call | tf_op jit(solution)/shard_map/pallas_call | solution.py:262
  (52 shorter events, 0.4 us)
Async XLA Ops:
  0.0 1.8 %copy-start.5 = (f32[128,3072]{1,0:T(8,128)S(1)}, f32[128,3072]{1,0:T(8,128)}, u32[]{:S(2)}) copy-start(f32[128,3072]{1,0:T(8,128)} %param.1) | copy-start | bytes 4718596
  1.3 6.3 %collective-permute-start = (f32[128,1536]{1,0:T(8,128)S(1)}, f32[128,1536]{1,0:T(8,128)S(1)}, u32[]{:S(2)}, u32[]{:S(2)}) collective-permute-start(f32[128,1536]{1,0:T(8,128)S(1)} %constant_dynamic-slice_fusion.6), channel_id=1, source_target_pairs={{0,2},{2,0},{4,6},{6,4},{8,10},{10,8},{12,14},{14,12},{16,18},{18,... | collective-permute-start | bytes 2359304 | tf_op jit(solution)/shard_map/ppermute | solution.py:11
  1.9 7.5 %collective-permute-start.5 = (f32[1,3072]{1,0:T(1,128)S(1)}, f32[1,3072]{1,0:T(1,128)S(1)}, u32[]{:S(2)}, u32[]{:S(2)}) collective-permute-start(f32[1,3072]{1,0:T(1,128)S(1)} %bitcast.48), channel_id=1, source_target_pairs={{0,24},{2,26},{4,28},{6,30},{8,16},{10,18},{12,20},{14,22},{16,8},... | collective-permute-start | bytes 36872 | tf_op jit(solution)/shard_map/ppermute | solution.py:11
  6.8 4.6 %collective-permute-start.4 = (f32[1,3072]{1,0:T(1,128)S(1)}, f32[1,3072]{1,0:T(1,128)S(1)}, u32[]{:S(2)}, u32[]{:S(2)}) collective-permute-start(f32[1,3072]{1,0:T(1,128)S(1)} %bitcast.49), channel_id=1, source_target_pairs={{0,16},{2,18},{4,20},{6,22},{8,24},{10,26},{12,28},{14,30},{16,0},... | collective-permute-start | bytes 36872 | tf_op jit(solution)/shard_map/ppermute | solution.py:11
  6.8 4.6 %collective-permute-start.3 = (f32[1,3072]{1,0:T(1,128)S(1)}, f32[1,3072]{1,0:T(1,128)S(1)}, u32[]{:S(2)}, u32[]{:S(2)}) collective-permute-start(f32[1,3072]{1,0:T(1,128)S(1)} %bitcast.50), channel_id=1, source_target_pairs={{0,8},{2,10},{4,12},{6,14},{8,0},{10,2},{12,4},{14,6},{16,24},{18,... | collective-permute-start | bytes 36872 | tf_op jit(solution)/shard_map/ppermute | solution.py:11
  7.7 10.8 %collective-permute-start.1 = (f32[2,128,384]{2,1,0:T(8,128)S(1)}, f32[2,128,384]{2,1,0:T(8,128)S(1)}, u32[]{:S(2)}, u32[]{:S(2)}) collective-permute-start(f32[2,128,384]{2,1,0:T(8,128)S(1)} %pad_maximum_fusion.1), channel_id=1, source_target_pairs={{0,4},{2,6},{4,0},{6,2},{8,12},{10,14},{12,8},{14,10},{16,20},{18,... | collective-permute-start | bytes 1179656 | tf_op jit(solution)/shard_map/ppermute | solution.py:11
  11.5 12.7 %collective-permute-start.13 = (f32[2,128,384]{2,1,0:T(8,128)S(1)}, f32[2,128,384]{2,1,0:T(8,128)S(1)}, u32[]{:S(2)}, u32[]{:S(2)}) collective-permute-start(f32[2,128,384]{2,1,0:T(8,128)S(1)} %pad_maximum_fusion.near0), channel_id=1, source_target_pairs={{0,24},{2,26},{4,28},{6,30},{8,0},{10,2},{12,4},{14,6},{16,8},{18,... | collective-permute-start | bytes 1179656 | tf_op jit(solution)/shard_map/ppermute | solution.py:16
  18.5 5.1 %collective-permute-start.6 = (f32[1,1536]{1,0:T(1,128)S(1)}, f32[1,1536]{1,0:T(1,128)S(1)}, u32[]{:S(2)}, u32[]{:S(2)}) collective-permute-start(f32[1,1536]{1,0:T(1,128)S(1)} %constant_dynamic-slice_fusion.4), channel_id=1, source_target_pairs={{0,2},{2,0},{4,6},{6,4},{8,10},{10,8},{12,14},{14,12},{16,18},{18,... | collective-permute-start | bytes 18440 | tf_op jit(solution)/shard_map/ppermute | solution.py:11
  18.5 18.8 %collective-permute-start.2 = (f32[2,128,384]{2,1,0:T(8,128)S(1)}, f32[2,128,384]{2,1,0:T(8,128)S(1)}, u32[]{:S(2)}, u32[]{:S(2)}) collective-permute-start(f32[2,128,384]{2,1,0:T(8,128)S(1)} %pad_maximum_fusion.3), channel_id=1, source_target_pairs={{0,4},{2,6},{4,0},{6,2},{8,12},{10,14},{12,8},{14,10},{16,20},{18,... | collective-permute-start | bytes 1179656 | tf_op jit(solution)/shard_map/ppermute | solution.py:11
  20.1 12.9 %collective-permute-start.8 = (f32[2,128,384]{2,1,0:T(8,128)S(1)}, f32[2,128,384]{2,1,0:T(8,128)S(1)}, u32[]{:S(2)}, u32[]{:S(2)}) collective-permute-start(f32[2,128,384]{2,1,0:T(8,128)S(1)} %collective-permute-done.1.far0), channel_id=1, source_target_pairs={{0,24},{2,26},{4,28},{6,30},{8,0},{10,2},{12,4},{14,6},{16,8},{18,... | collective-permute-start | bytes 1179656 | tf_op jit(solution)/shard_map/ppermute | solution.py:16
  23.6 6.6 %collective-permute-start.7 = (f32[1,768]{1,0:T(1,128)S(1)}, f32[1,768]{1,0:T(1,128)S(1)}, u32[]{:S(2)}, u32[]{:S(2)}) collective-permute-start(f32[1,768]{1,0:T(1,128)S(1)} %constant_dynamic-slice_fusion.2), channel_id=1, source_target_pairs={{0,4},{2,6},{4,0},{6,2},{8,12},{10,14},{12,8},{14,10},{16,20},{18,... | collective-permute-start | bytes 9224 | tf_op jit(solution)/shard_map/ppermute | solution.py:11
  24.2 25.0 %copy-start.3 = (f32[2,128,384]{2,1,0:T(8,128)}, f32[2,128,384]{2,1,0:T(8,128)S(1)}, u32[]{:S(2)}) copy-start(f32[2,128,384]{2,1,0:T(8,128)S(1)} %collective-permute-done.13.refs_0_) | copy-start | bytes 1179652
  24.2 17.2 %collective-permute-start.14 = (f32[2,128,384]{2,1,0:T(8,128)S(1)}, f32[2,128,384]{2,1,0:T(8,128)S(1)}, u32[]{:S(2)}, u32[]{:S(2)}) collective-permute-start(f32[2,128,384]{2,1,0:T(8,128)S(1)} %collective-permute-done.13.refs_0_), channel_id=1, source_target_pairs={{0,24},{2,26},{4,28},{6,30},{8,0},{10,2},{12,4},{14,6},{16,8},{18,... | collective-permute-start | bytes 1179656 | tf_op jit(solution)/shard_map/ppermute | solution.py:16
  33.0 16.2 %copy-start = (f32[2,128,384]{2,1,0:T(8,128)}, f32[2,128,384]{2,1,0:T(8,128)S(1)}, u32[]{:S(2)}) copy-start(f32[2,128,384]{2,1,0:T(8,128)S(1)} %collective-permute-done.8.refs_0_) | copy-start | bytes 1179652
  33.0 16.1 %collective-permute-start.15 = (f32[2,128,384]{2,1,0:T(8,128)S(1)}, f32[2,128,384]{2,1,0:T(8,128)S(1)}, u32[]{:S(2)}, u32[]{:S(2)}) collective-permute-start(f32[2,128,384]{2,1,0:T(8,128)S(1)} %collective-permute-done.8.refs_0_), channel_id=1, source_target_pairs={{0,24},{2,26},{4,28},{6,30},{8,0},{10,2},{12,4},{14,6},{16,8},{18,... | collective-permute-start | bytes 1179656 | tf_op jit(solution)/shard_map/ppermute | solution.py:16
  37.3 14.7 %copy-start.2 = (f32[2,128,384]{2,1,0:T(8,128)}, f32[2,128,384]{2,1,0:T(8,128)S(1)}, u32[]{:S(2)}) copy-start(f32[2,128,384]{2,1,0:T(8,128)S(1)} %collective-permute-done.2.far1) | copy-start | bytes 1179652
  52.0 5.9 %collective-permute-start.16 = (f32[2,2,8,64,128]{4,3,2,1,0:T(8,128)}, f32[2,2,8,64,128]{4,3,2,1,0:T(8,128)}, u32[]{:S(2)}, u32[]{:S(2)}) collective-permute-start(f32[2,2,8,64,128]{4,3,2,1,0:T(8,128)} %get-tuple-element.29), channel_id=1, source_target_pairs={{0,2},{2,0},{4,6},{6,4},{8,10},{10,8},{12,14},{14,12},{16,18},{18,... | collective-permute-start | bytes 3145736 | tf_op jit(solution)/shard_map/ppermute | solution.py:11
  52.0 4.8 %collective-permute-start.9 = (f32[2,2,4,64,128]{4,3,2,1,0:T(8,128)}, f32[2,2,4,64,128]{4,3,2,1,0:T(8,128)}, u32[]{:S(2)}, u32[]{:S(2)}) collective-permute-start(f32[2,2,4,64,128]{4,3,2,1,0:T(8,128)} %get-tuple-element.25), channel_id=1, source_target_pairs={{0,2},{2,0},{4,6},{6,4},{8,10},{10,8},{12,14},{14,12},{16,18},{18,... | collective-permute-start | bytes 1572872 | tf_op jit(solution)/shard_map/ppermute | solution.py:11
  52.5 13.8 %collective-permute-start.18 = (f32[2,128,384]{2,1,0:T(8,128)S(1)}, f32[2,128,384]{2,1,0:T(8,128)S(1)}, u32[]{:S(2)}, u32[]{:S(2)}) collective-permute-start(f32[2,128,384]{2,1,0:T(8,128)S(1)} %pad_maximum_fusion.2.near1), channel_id=1, source_target_pairs={{0,24},{2,26},{4,28},{6,30},{8,0},{10,2},{12,4},{14,6},{16,8},{18,... | collective-permute-start | bytes 1179656 | tf_op jit(solution)/shard_map/ppermute | solution.py:16
  56.8 17.1 %collective-permute-start.17 = (f32[2,128,384]{2,1,0:T(8,128)}, f32[2,128,384]{2,1,0:T(8,128)S(1)}, u32[]{:S(2)}, u32[]{:S(2)}) collective-permute-start(f32[2,128,384]{2,1,0:T(8,128)} %copy-done.2), channel_id=1, source_target_pairs={{0,24},{2,26},{4,28},{6,30},{8,0},{10,2},{12,4},{14,6},{16,8},{18,... | collective-permute-start | bytes 1179656 | tf_op jit(solution)/shard_map/ppermute | solution.py:16
  59.4 8.3 %copy-start.4 = (f32[2,128,384]{2,1,0:T(8,128)S(1)}, f32[2,128,384]{2,1,0:T(8,128)}, u32[]{:S(2)}) copy-start(f32[2,128,384]{2,1,0:T(8,128)} %copy-done.3) | copy-start | bytes 1179652
  59.4 16.2 %collective-permute-start.22 = (f32[8,64,128]{2,1,0:T(8,128)S(1)}, f32[8,64,128]{2,1,0:T(8,128)S(1)}, u32[]{:S(2)}, u32[]{:S(2)}) collective-permute-start(f32[8,64,128]{2,1,0:T(8,128)S(1)} %dynamic-slice_bitcast_fusion), channel_id=1, source_target_pairs={{0,1},{1,0},{2,3},{3,2},{4,5},{5,4},{6,7},{7,6},{8,9},{9,8},{10,11... | collective-permute-start | bytes 786440 | tf_op jit(solution)/shard_map/ppermute | solution.py:26
  61.0 16.1 %collective-permute-start.20 = (f32[8,64,128]{2,1,0:T(8,128)S(1)}, f32[8,64,128]{2,1,0:T(8,128)S(1)}, u32[]{:S(2)}, u32[]{:S(2)}) collective-permute-start(f32[8,64,128]{2,1,0:T(8,128)S(1)} %get-tuple-element.53), channel_id=1, source_target_pairs={{0,4},{1,5},{2,6},{3,7},{4,0},{5,1},{6,2},{7,3},{8,12},{9,13},{10,... | collective-permute-start | bytes 786440 | tf_op jit(solution)/shard_map/ppermute | solution.py:26
  61.6 16.1 %collective-permute-start.21 = (f32[8,64,128]{2,1,0:T(8,128)S(1)}, f32[8,64,128]{2,1,0:T(8,128)S(1)}, u32[]{:S(2)}, u32[]{:S(2)}) collective-permute-start(f32[8,64,128]{2,1,0:T(8,128)S(1)} %get-tuple-element.54), channel_id=1, source_target_pairs={{0,5},{1,4},{2,7},{3,6},{4,1},{5,0},{6,3},{7,2},{8,13},{9,12},{10,... | collective-permute-start | bytes 786440 | tf_op jit(solution)/shard_map/ppermute | solution.py:26
  63.2 10.7 %copy-start.1 = (f32[2,128,384]{2,1,0:T(8,128)S(1)}, f32[2,128,384]{2,1,0:T(8,128)}, u32[]{:S(2)}) copy-start(f32[2,128,384]{2,1,0:T(8,128)} %copy-done) | copy-start | bytes 1179652
  66.3 15.7 %collective-permute-start.11 = (f32[4,64,128]{2,1,0:T(8,128)S(1)}, f32[4,64,128]{2,1,0:T(8,128)S(1)}, u32[]{:S(2)}, u32[]{:S(2)}) collective-permute-start(f32[4,64,128]{2,1,0:T(8,128)S(1)} %get-tuple-element.65), channel_id=1, source_target_pairs={{0,5},{1,4},{2,7},{3,6},{4,1},{5,0},{6,3},{7,2},{8,13},{9,12},{10,... | collective-permute-start | bytes 393224 | tf_op jit(solution)/shard_map/ppermute | solution.py:26
  74.9 4.7 %collective-permute-start.19 = (f32[2,2,4,64,128]{4,3,2,1,0:T(8,128)S(1)}, f32[2,2,4,64,128]{4,3,2,1,0:T(8,128)S(1)}, u32[]{:S(2)}, u32[]{:S(2)}) collective-permute-start(f32[2,2,4,64,128]{4,3,2,1,0:T(8,128)S(1)} %get-tuple-element.37), channel_id=1, source_target_pairs={{0,2},{2,0},{4,6},{6,4},{8,10},{10,8},{12,14},{14,12},{16,18},{18,... | collective-permute-start | bytes 1572872 | tf_op jit(solution)/shard_map/ppermute | solution.py:11
  75.7 7.3 %collective-permute-start.10 = (f32[4,64,128]{2,1,0:T(8,128)S(1)}, f32[4,64,128]{2,1,0:T(8,128)S(1)}, u32[]{:S(2)}, u32[]{:S(2)}) collective-permute-start(f32[4,64,128]{2,1,0:T(8,128)S(1)} %get-tuple-element.66), channel_id=1, source_target_pairs={{0,4},{1,5},{2,6},{3,7},{4,0},{5,1},{6,2},{7,3},{8,12},{9,13},{10,... | collective-permute-start | bytes 393224 | tf_op jit(solution)/shard_map/ppermute | solution.py:26
  77.2 7.3 %collective-permute-start.12 = (f32[4,64,128]{2,1,0:T(8,128)S(1)}, f32[4,64,128]{2,1,0:T(8,128)S(1)}, u32[]{:S(2)}, u32[]{:S(2)}) collective-permute-start(f32[4,64,128]{2,1,0:T(8,128)S(1)} %get-tuple-element.63), channel_id=1, source_target_pairs={{0,1},{1,0},{2,3},{3,2},{4,5},{5,4},{6,7},{7,6},{8,9},{9,8},{10,11... | collective-permute-start | bytes 393224 | tf_op jit(solution)/shard_map/ppermute | solution.py:26
  78.5 9.0 %collective-permute-start.26 = (f32[4,64,128]{2,1,0:T(8,128)S(1)}, f32[4,64,128]{2,1,0:T(8,128)S(1)}, u32[]{:S(2)}, u32[]{:S(2)}) collective-permute-start(f32[4,64,128]{2,1,0:T(8,128)S(1)} %get-tuple-element.57), channel_id=1, source_target_pairs={{0,16},{2,18},{4,20},{6,22},{8,24},{10,26},{12,28},{14,30},{16,0},... | collective-permute-start | bytes 393224 | tf_op jit(solution)/shard_map/ppermute | solution.py:16
  79.7 7.7 %collective-permute-start.24 = (f32[4,64,128]{2,1,0:T(8,128)S(1)}, f32[4,64,128]{2,1,0:T(8,128)S(1)}, u32[]{:S(2)}, u32[]{:S(2)}) collective-permute-start(f32[4,64,128]{2,1,0:T(8,128)S(1)} %get-tuple-element.61), channel_id=1, source_target_pairs={{0,5},{1,4},{2,7},{3,6},{4,1},{5,0},{6,3},{7,2},{8,13},{9,12},{10,... | collective-permute-start | bytes 393224 | tf_op jit(solution)/shard_map/ppermute | solution.py:26
  82.0 6.7 %copy-start.6 = (f32[4,64,128]{2,1,0:T(8,128)}, f32[4,64,128]{2,1,0:T(8,128)S(1)}, u32[]{:S(2)}) copy-start(f32[4,64,128]{2,1,0:T(8,128)S(1)} %collective-permute-done.11.refs_2_) | copy-start | bytes 393220
  82.0 6.6 %collective-permute-start.23 = (f32[4,64,128]{2,1,0:T(8,128)S(1)}, f32[4,64,128]{2,1,0:T(8,128)S(1)}, u32[]{:S(2)}, u32[]{:S(2)}) collective-permute-start(f32[4,64,128]{2,1,0:T(8,128)S(1)} %get-tuple-element.62), channel_id=1, source_target_pairs={{0,4},{1,5},{2,6},{3,7},{4,0},{5,1},{6,2},{7,3},{8,12},{9,13},{10,... | collective-permute-start | bytes 393224 | tf_op jit(solution)/shard_map/ppermute | solution.py:26
  83.0 5.7 %copy-start.7 = (f32[4,64,128]{2,1,0:T(8,128)}, f32[4,64,128]{2,1,0:T(8,128)S(1)}, u32[]{:S(2)}) copy-start(f32[4,64,128]{2,1,0:T(8,128)S(1)} %collective-permute-done.10.refs_1_) | copy-start | bytes 393220
  83.0 5.7 %collective-permute-start.25 = (f32[4,64,128]{2,1,0:T(8,128)S(1)}, f32[4,64,128]{2,1,0:T(8,128)S(1)}, u32[]{:S(2)}, u32[]{:S(2)}) collective-permute-start(f32[4,64,128]{2,1,0:T(8,128)S(1)} %get-tuple-element.59), channel_id=1, source_target_pairs={{0,1},{1,0},{2,3},{3,2},{4,5},{5,4},{6,7},{7,6},{8,9},{9,8},{10,11... | collective-permute-start | bytes 393224 | tf_op jit(solution)/shard_map/ppermute | solution.py:26
  84.5 4.2 %copy-start.8 = (f32[4,64,128]{2,1,0:T(8,128)}, f32[4,64,128]{2,1,0:T(8,128)S(1)}, u32[]{:S(2)}) copy-start(f32[4,64,128]{2,1,0:T(8,128)S(1)} %collective-permute-done.12.refs_3_) | copy-start | bytes 393220
  87.4 1.3 %copy-start.9 = (f32[4,64,128]{2,1,0:T(8,128)}, f32[4,64,128]{2,1,0:T(8,128)S(1)}, u32[]{:S(2)}) copy-start(f32[4,64,128]{2,1,0:T(8,128)S(1)} %collective-permute-done.26.refs_9_) | copy-start | bytes 393220
  87.4 1.3 %copy-start.10 = (f32[4,64,128]{2,1,0:T(8,128)}, f32[4,64,128]{2,1,0:T(8,128)S(1)}, u32[]{:S(2)}) copy-start(f32[4,64,128]{2,1,0:T(8,128)S(1)} %collective-permute-done.24.refs_6_) | copy-start | bytes 393220
  88.6 0.6 copy-start.11
  88.7 0.6 copy-start.12

commit v6 on v5

--- a/solution.py
+++ b/solution.py
@@ -95,13 +95,19 @@
             store(block, out_refs, a, b, 0)
 
 
-def half_kernel(mean_ref, high_ref, low_ref, near_ref, far_ref, keep_ref, send_ref):
+def half_kernel(column, mean_ref, high_ref, low_ref, right_ref, *refs):
+    out_refs = refs[-2:]
+    for old, new in zip(refs[:-2], out_refs):
+        new[1 - column, :, 4:] = old[1 - column, :, 4:]
+        for a in range(2):
+            for place in range(4):
+                if (place ^ (2 * a)) // 2 != column:
+                    new[a, :, place] = old[a, :, place]
     lefts = [(high_ref[1, a], low_ref[1, a]) for a in range(2)]
-    rights = [centered(ref, mean_ref[1]) for ref in (near_ref, far_ref)]
+    right = centered(right_ref, mean_ref[1])
     for a in range(2):
-        for b in range(2):
-            store(product(lefts[a], rights[b]), (keep_ref, send_ref), a, b, 0)
-            store(product(rights[a], lefts[b]), (keep_ref, send_ref), a, b, 4)
+        store(product(lefts[a], right), out_refs, a, column, 0)
+        store(product(right, lefts[a]), out_refs, column, a, 4)
 
 
 VMEM = pl.BlockSpec(memory_space=pltpu.VMEM)
@@ -216,13 +222,16 @@
     )
     own = keep, send
 
-    keep, send = call(
-        half_kernel,
-        (tile_shape(8), tile_shape(8)),
-        (),
-        (mean, high, low, *first[steps]),
-        4 * flops,
-    )
+    outs = ()
+    for column in range(2):
+        outs = call(
+            functools.partial(half_kernel, column),
+            (tile_shape(8), tile_shape(8)),
+            (),
+            (mean, high, low, first[steps][column], *outs),
+            2 * flops,
+        )
+    keep, send = outs
     first_total = exchange(*own)
     shares = [messages(first_total, shard)]
     total = after(exchange(keep, send), first_total)

time: 92.3 us -> 91.5 us (level)
  waiting for transfers between devices: 37.8 us -> 36.7 us
    ppermute x7, waiting for transfers between devices: 23.2 us -> 22.1 us  [shift(): lax.ppermute(value, 'blk', [(k, (k + steps) % count) for k in range(count)])]
    pallas_call x4 -> x5, Pallas kernels: 7.5 us -> 7.74 us  [call(): pl.pallas_call(kernel, out_shape=outs, in_specs=[SMEM] * len(scalars) + [...]
  transfers between devices with their start and end apart: 27 -> 27, of which waited for: 12 -> 12; matrix products, arithmetic and copies ran while one was open for 6% -> 7% of each run, Pallas kernels for 5% -> 6%
where the time goes in v6:
time: 91.5 us; the launch traced here: 90.7 us
  waiting for transfers between devices  36.7 us (40%)
  starting transfers between devices  35.9 us (39%)
  Pallas kernels  9.92 us (11%)
  local copies, waits for them, and re-layouts  4.46 us (5%)
  other arithmetic  3.41 us (4%)
    ppermute x7, waiting for transfers between devices, shift(): lax.ppermute(value, 'blk', [(k, (k + steps) % count) for k in range(count)])  22.1 us
    ppermute x7, starting transfers between devices, shift(): lax.ppermute(value, 'blk', [(k, (k + steps) % count) for k in range(count)])  15.7 us
    ppermute x11, waiting for transfers between devices, swap(): lax.ppermute(value, 'blk', [(k, k ^ mask) for k in range(lax.axis_size('b...  12.4 us
    ppermute x11, starting transfers between devices, swap(): lax.ppermute(value, 'blk', [(k, k ^ mask) for k in range(lax.axis_size('b...  10.6 us
    ppermute x9, starting transfers between devices, hop(): return lax.ppermute(value, ('blk', 'par'), pairs)  9.64 us
    pallas_call x5, Pallas kernels, call(): pl.pallas_call(kernel, out_shape=outs, in_specs=[SMEM] * len(scalars) + [...  7.74 us
    add x3, other arithmetic, exchange(): return keep + swap(send, 1)  2.52 us
    ppermute x9, waiting for transfers between devices, hop(): return lax.ppermute(value, ('blk', 'par'), pairs)  2.27 us
  transfers between devices with their start and end apart: 27, of which 12 were waited for; matrix products, arithmetic and copies ran while one was open for 7% of the time, Pallas kernels for 6%

profile of v6, /device:TPU:0, one launch (start us, length us, event | category | flops | bytes accessed | tf_op | source)
XLA Modules:
  0.0 90.7 jit_solution(11506947335755972521)
XLA Ops:
  0.0 1.3 %constant_dynamic-slice_fusion.6 = f32[128,1536]{1,0:T(8,128)S(1)} fusion(f32[128,3072]{1,0:T(8,128)} %param.1, s32[]{:T(128)S(6)} %select_n.113), kind=kLoop, calls=%fused_computation.32 | loop fusion | bytes 1572868 | tf_op jit(solution)/shard_map/dynamic_slice | solution.py:176
  1.3 0.5 collective-permute-start
  1.8 0.1 reduce_sum.9
  1.9 4.9 %collective-permute-start.5 = (f32[1,3072]{1,0:T(1,128)S(1)}, f32[1,3072]{1,0:T(1,128)S(1)}, u32[]{:S(2)}, u32[]{:S(2)}) collective-permute-start(f32[1,3072]{1,0:T(1,128)S(1)} %bitcast.48), channel_id=1, source_target_pairs={{0,24},{2,26},{4,28},{6,30},{8,16},{10,18},{12,20},{14,22},{16,8},... | collective-permute-start | bytes 36872 | tf_op jit(solution)/shard_map/ppermute | solution.py:11
  6.8 0.6 collective-permute-start.3
  7.5 0.1 dynamic-slice_bitcast_fusion.5
  7.6 0.1 dynamic-slice_bitcast_fusion.4
  7.7 1.7 %collective-permute-start.1 = (f32[2,128,384]{2,1,0:T(8,128)S(1)}, f32[2,128,384]{2,1,0:T(8,128)S(1)}, u32[]{:S(2)}, u32[]{:S(2)}) collective-permute-start(f32[2,128,384]{2,1,0:T(8,128)S(1)} %pad_maximum_fusion.1), channel_id=1, source_target_pairs={{0,4},{2,6},{4,0},{6,2},{8,12},{10,14},{12,8},{14,10},{16,20},{18,... | collective-permute-start | bytes 1179656 | tf_op jit(solution)/shard_map/ppermute | solution.py:11
  9.4 2.0 %collective-permute-done.4 = f32[1,3072]{1,0:T(1,128)S(1)} collective-permute-done((f32[1,3072]{1,0:T(1,128)S(1)}, f32[1,3072]{1,0:T(1,128)S(1)}, u32[]{:S(2)}, u32[]{:S(2)}) %collective-permute-start.4) | collective-permute-done | bytes 12320 | tf_op jit(solution)/shard_map/ppermute | solution.py:11
  11.5 1.7 %collective-permute-start.14 = (f32[2,128,384]{2,1,0:T(8,128)S(1)}, f32[2,128,384]{2,1,0:T(8,128)S(1)}, u32[]{:S(2)}, u32[]{:S(2)}) collective-permute-start(f32[2,128,384]{2,1,0:T(8,128)S(1)} %pad_maximum_fusion.near0), channel_id=1, source_target_pairs={{0,24},{2,26},{4,28},{6,30},{8,0},{10,2},{12,4},{14,6},{16,8},{18,... | collective-permute-start | bytes 1179656 | tf_op jit(solution)/shard_map/ppermute | solution.py:16
  13.2 5.3 %collective-permute-done.1.far0 = f32[2,128,384]{2,1,0:T(8,128)S(1)} collective-permute-done((f32[2,128,384]{2,1,0:T(8,128)S(1)}, f32[2,128,384]{2,1,0:T(8,128)S(1)}, u32[]{:S(2)}, u32[]{:S(2)}) %collective-permute-start.1) | collective-permute-done | bytes 393248 | tf_op jit(solution)/shard_map/ppermute | solution.py:11
  18.5 0.0 collective-permute-start.6
  18.5 1.6 %collective-permute-start.2 = (f32[2,128,384]{2,1,0:T(8,128)S(1)}, f32[2,128,384]{2,1,0:T(8,128)S(1)}, u32[]{:S(2)}, u32[]{:S(2)}) collective-permute-start(f32[2,128,384]{2,1,0:T(8,128)S(1)} %pad_maximum_fusion.3), channel_id=1, source_target_pairs={{0,4},{2,6},{4,0},{6,2},{8,12},{10,14},{12,8},{14,10},{16,20},{18,... | collective-permute-start | bytes 1179656 | tf_op jit(solution)/shard_map/ppermute | solution.py:11
  20.1 3.5 %collective-permute-start.8 = (f32[2,128,384]{2,1,0:T(8,128)S(1)}, f32[2,128,384]{2,1,0:T(8,128)S(1)}, u32[]{:S(2)}, u32[]{:S(2)}) collective-permute-start(f32[2,128,384]{2,1,0:T(8,128)S(1)} %collective-permute-done.1.far0), channel_id=1, source_target_pairs={{0,24},{2,26},{4,28},{6,30},{8,0},{10,2},{12,4},{14,6},{16,8},{18,... | collective-permute-start | bytes 1179656 | tf_op jit(solution)/shard_map/ppermute | solution.py:16
  23.6 0.0 collective-permute-done.6
  23.6 0.6 collective-permute-start.7
  24.2 0.9 collective-permute-start.15
  25.1 5.1 %collective-permute-done.7 = f32[1,768]{1,0:T(1,128)S(1)} collective-permute-done((f32[1,768]{1,0:T(1,128)S(1)}, f32[1,768]{1,0:T(1,128)S(1)}, u32[]{:S(2)}, u32[]{:S(2)}) %collective-permute-start.7) | collective-permute-done | bytes 3104 | tf_op jit(solution)/shard_map/ppermute | solution.py:11
  30.2 2.9 %collective-permute-done.8.refs_0_ = f32[2,128,384]{2,1,0:T(8,128)S(1)} collective-permute-done((f32[2,128,384]{2,1,0:T(8,128)S(1)}, f32[2,128,384]{2,1,0:T(8,128)S(1)}, u32[]{:S(2)}, u32[]{:S(2)}) %collective-permute-start.8) | collective-permute-done | bytes 393248 | tf_op jit(solution)/shard_map/ppermute | solution.py:16
  33.0 4.3 %collective-permute-start.13 = (f32[2,128,384]{2,1,0:T(8,128)S(1)}, f32[2,128,384]{2,1,0:T(8,128)S(1)}, u32[]{:S(2)}, u32[]{:S(2)}) collective-permute-start(f32[2,128,384]{2,1,0:T(8,128)S(1)} %collective-permute-done.8.refs_0_), channel_id=1, source_target_pairs={{0,24},{2,26},{4,28},{6,30},{8,0},{10,2},{12,4},{14,6},{16,8},{18,... | collective-permute-start | bytes 1179656 | tf_op jit(solution)/shard_map/ppermute | solution.py:16
  37.4 2.7 %shard_map.17 = (f32[2,2,4,64,128]{4,3,2,1,0:T(8,128)S(1)}, f32[2,2,4,64,128]{4,3,2,1,0:T(8,128)}, bf16[2,2,256,384]{3,2,1,0:T(8,128)(2,1)S(1)}, bf16[2,2,256,384]{3,2,1,0:T(8,128)(2,1)S(1)}) custom-call(f32[2,128,384]{2,1,0:T(8,128)S(1)} %pad_maximum_fusion.near0, f32[2,128,384]{2,1,0:T(8,128)S(1)} %collective-permute-done.1.far0, ...), custom_call_target="tpu_custom_call" | custom-call | tf_op jit(solution)/shard_map/pallas_call | solution.py:119
  40.0 1.4 %collective-permute-done.15.right_ref = f32[2,128,384]{2,1,0:T(8,128)S(1)} collective-permute-done((f32[2,128,384]{2,1,0:T(8,128)S(1)}, f32[2,128,384]{2,1,0:T(8,128)S(1)}, u32[]{:S(2)}, u32[]{:S(2)}) %collective-permute-start.15) | collective-permute-done | bytes 393248 | tf_op jit(solution)/shard_map/ppermute | solution.py:16
  41.5 1.0 %shard_map.18 = (f32[2,2,8,64,128]{4,3,2,1,0:T(8,128)S(1)}, f32[2,2,8,64,128]{4,3,2,1,0:T(8,128)S(1)}) custom-call(f32[2,1,384]{2,1,0:T(1,128)S(1)} %pad_maximum_fusion.4.mean_ref, bf16[2,2,256,384]{3,2,1,0:T(8,128)(2,1)S(1)} %get-tuple-element.28.high_ref, bf16[2,2,256,384]{3,2,1,0:T(8,128)(2,1)S(1)} %get-tuple-element.29.low_ref, ...), custom_call_target="tpu_custom_call" | custom-call | tf_op jit(solution)/shard_map/pallas_call | solution.py:119
  42.5 6.7 %collective-permute-done.13.right_ref = f32[2,128,384]{2,1,0:T(8,128)S(1)} collective-permute-done((f32[2,128,384]{2,1,0:T(8,128)S(1)}, f32[2,128,384]{2,1,0:T(8,128)S(1)}, u32[]{:S(2)}, u32[]{:S(2)}) %collective-permute-start.13) | collective-permute-done | bytes 393248 | tf_op jit(solution)/shard_map/ppermute | solution.py:16
  49.2 2.0 %shard_map.19 = (f32[2,2,8,64,128]{4,3,2,1,0:T(8,128)S(1)}, f32[2,2,8,64,128]{4,3,2,1,0:T(8,128)}) custom-call(f32[2,1,384]{2,1,0:T(1,128)S(1)} %pad_maximum_fusion.4.mean_ref, bf16[2,2,256,384]{3,2,1,0:T(8,128)(2,1)S(1)} %get-tuple-element.28.high_ref, bf16[2,2,256,384]{3,2,1,0:T(8,128)(2,1)S(1)} %get-tuple-element.29.low_ref, ...), custom_call_target="tpu_custom_call" | custom-call | tf_op jit(solution)/shard_map/pallas_call | solution.py:119
  51.2 0.0 collective-permute-start.16
  51.2 0.5 collective-permute-start.9
  51.7 4.3 %collective-permute-start.18 = (f32[2,128,384]{2,1,0:T(8,128)S(1)}, f32[2,128,384]{2,1,0:T(8,128)S(1)}, u32[]{:S(2)}, u32[]{:S(2)}) collective-permute-start(f32[2,128,384]{2,1,0:T(8,128)S(1)} %pad_maximum_fusion.2.near1), channel_id=1, source_target_pairs={{0,24},{2,26},{4,28},{6,30},{8,0},{10,2},{12,4},{14,6},{16,8},{18,... | collective-permute-start | bytes 1179656 | tf_op jit(solution)/shard_map/ppermute | solution.py:16
  56.0 0.0 collective-permute-start.17
  56.0 0.0 collective-permute-done.9
  56.1 1.1 %add.197 = f32[2,2,4,64,128]{4,3,2,1,0:T(8,128)S(1)} add(f32[2,2,4,64,128]{4,3,2,1,0:T(8,128)S(1)} %get-tuple-element.26, f32[2,2,4,64,128]{4,3,2,1,0:T(8,128)} %collective-permute-done.9) | non-fusion elementwise | flops 131072 | bytes 1572864 | tf_op jit(solution)/shard_map/add | solution.py:130
  57.2 1.4 %add.206 = f32[2,2,8,64,128]{4,3,2,1,0:T(8,128)S(1)} add(f32[2,2,8,64,128]{4,3,2,1,0:T(8,128)S(1)} %get-tuple-element.32, f32[2,2,8,64,128]{4,3,2,1,0:T(8,128)} %collective-permute-done.16) | non-fusion elementwise | flops 262144 | bytes 3145728 | tf_op jit(solution)/shard_map/add | solution.py:130
  58.5 0.1 fusion.5
  58.7 1.6 %collective-permute-start.22 = (f32[8,64,128]{2,1,0:T(8,128)S(1)}, f32[8,64,128]{2,1,0:T(8,128)S(1)}, u32[]{:S(2)}, u32[]{:S(2)}) collective-permute-start(f32[8,64,128]{2,1,0:T(8,128)S(1)} %dynamic-slice_bitcast_fusion), channel_id=1, source_target_pairs={{0,1},{1,0},{2,3},{3,2},{4,5},{5,4},{6,7},{7,6},{8,9},{9,8},{10,11... | collective-permute-start | bytes 786440 | tf_op jit(solution)/shard_map/ppermute | solution.py:26
  60.3 0.6 collective-permute-start.20
  60.8 1.5 %collective-permute-start.21 = (f32[8,64,128]{2,1,0:T(8,128)S(1)}, f32[8,64,128]{2,1,0:T(8,128)S(1)}, u32[]{:S(2)}, u32[]{:S(2)}) collective-permute-start(f32[8,64,128]{2,1,0:T(8,128)S(1)} %get-tuple-element.58), channel_id=1, source_target_pairs={{0,5},{1,4},{2,7},{3,6},{4,1},{5,0},{6,3},{7,2},{8,13},{9,12},{10,... | collective-permute-start | bytes 786440 | tf_op jit(solution)/shard_map/ppermute | solution.py:26
  62.4 3.1 %collective-permute-done.18.refs_1_ = f32[2,128,384]{2,1,0:T(8,128)S(1)} collective-permute-done((f32[2,128,384]{2,1,0:T(8,128)S(1)}, f32[2,128,384]{2,1,0:T(8,128)S(1)}, u32[]{:S(2)}, u32[]{:S(2)}) %collective-permute-start.18) | collective-permute-done | bytes 393248 | tf_op jit(solution)/shard_map/ppermute | solution.py:16
  65.5 1.4 %collective-permute-start.11 = (f32[4,64,128]{2,1,0:T(8,128)S(1)}, f32[4,64,128]{2,1,0:T(8,128)S(1)}, u32[]{:S(2)}, u32[]{:S(2)}) collective-permute-start(f32[4,64,128]{2,1,0:T(8,128)S(1)} %get-tuple-element.69), channel_id=1, source_target_pairs={{0,5},{1,4},{2,7},{3,6},{4,1},{5,0},{6,3},{7,2},{8,13},{9,12},{10,... | collective-permute-start | bytes 393224 | tf_op jit(solution)/shard_map/ppermute | solution.py:26
  67.0 1.0 %shard_map.20 = (f32[2,2,4,64,128]{4,3,2,1,0:T(8,128)S(1)}, f32[2,2,4,64,128]{4,3,2,1,0:T(8,128)S(1)}) custom-call(s32[1]{0:T(128)} %bitcast.15.flag_ref, f32[2,1,384]{2,1,0:T(1,128)S(1)} %pad_maximum_fusion.4.mean_ref, bf16[2,2,256,384]{3,2,1,0:T(8,128)(2,1)S(1)} %get-tuple-element.28.high_ref, bf16[2,2,256,384]{3,2,1,0:T(8,128)(2,1)S(1)} %get-tuple-element.29.low_ref, ...), custom_call_target="tpu_custom_call" | custom-call | tf_op jit(solution)/shard_map/pallas_call | solution.py:119
  68.0 5.1 %collective-permute-done.17.refs_1_ = f32[2,128,384]{2,1,0:T(8,128)S(1)} collective-permute-done((f32[2,128,384]{2,1,0:T(8,128)}, f32[2,128,384]{2,1,0:T(8,128)S(1)}, u32[]{:S(2)}, u32[]{:S(2)}) %collective-permute-start.17) | collective-permute-done | bytes 393248 | tf_op jit(solution)/shard_map/ppermute | solution.py:16
  73.1 1.0 %shard_map.21 = (f32[2,2,4,64,128]{4,3,2,1,0:T(8,128)S(1)}, f32[2,2,4,64,128]{4,3,2,1,0:T(8,128)S(1)}) custom-call(s32[1]{0:T(128)} %bitcast.15.flag_ref, f32[2,1,384]{2,1,0:T(1,128)S(1)} %pad_maximum_fusion.4.mean_ref, bf16[2,2,256,384]{3,2,1,0:T(8,128)(2,1)S(1)} %get-tuple-element.28.high_ref, bf16[2,2,256,384]{3,2,1,0:T(8,128)(2,1)S(1)} %get-tuple-element.29.low_ref, ...), custom_call_target="tpu_custom_call" | custom-call | tf_op jit(solution)/shard_map/pallas_call | solution.py:119
  74.1 0.1 collective-permute-start.19
  74.2 0.7 dynamic-slice_bitcast_fusion.16
  74.9 0.5 collective-permute-start.10
  75.4 1.0 %collective-permute-done.20 = f32[8,64,128]{2,1,0:T(8,128)S(1)} collective-permute-done((f32[8,64,128]{2,1,0:T(8,128)S(1)}, f32[8,64,128]{2,1,0:T(8,128)S(1)}, u32[]{:S(2)}, u32[]{:S(2)}) %collective-permute-start.20) | collective-permute-done | bytes 262176 | tf_op jit(solution)/shard_map/ppermute | solution.py:26
  76.4 0.5 collective-permute-start.12
  76.9 0.1 add_add_fusion
  77.0 0.7 fusion.8
  77.7 1.1 %collective-permute-start.26 = (f32[4,64,128]{2,1,0:T(8,128)S(1)}, f32[4,64,128]{2,1,0:T(8,128)S(1)}, u32[]{:S(2)}, u32[]{:S(2)}) collective-permute-start(f32[4,64,128]{2,1,0:T(8,128)S(1)} %get-tuple-element.61), channel_id=1, source_target_pairs={{0,16},{2,18},{4,20},{6,22},{8,24},{10,26},{12,28},{14,30},{16,0},... | collective-permute-start | bytes 393224 | tf_op jit(solution)/shard_map/ppermute | solution.py:16
  78.8 0.0 collective-permute-done.19
  78.8 0.1 add.207
  79.0 1.6 %collective-permute-start.24 = (f32[4,64,128]{2,1,0:T(8,128)S(1)}, f32[4,64,128]{2,1,0:T(8,128)S(1)}, u32[]{:S(2)}, u32[]{:S(2)}) collective-permute-start(f32[4,64,128]{2,1,0:T(8,128)S(1)} %get-tuple-element.65), channel_id=1, source_target_pairs={{0,5},{1,4},{2,7},{3,6},{4,1},{5,0},{6,3},{7,2},{8,13},{9,12},{10,... | collective-permute-start | bytes 393224 | tf_op jit(solution)/shard_map/ppermute | solution.py:26
  80.5 0.7 dynamic-slice_bitcast_fusion.12
  81.2 0.0 collective-permute-done.11.refs_2_
  81.2 1.0 %collective-permute-start.23 = (f32[4,64,128]{2,1,0:T(8,128)S(1)}, f32[4,64,128]{2,1,0:T(8,128)S(1)}, u32[]{:S(2)}, u32[]{:S(2)}) collective-permute-start(f32[4,64,128]{2,1,0:T(8,128)S(1)} %get-tuple-element.66), channel_id=1, source_target_pairs={{0,4},{1,5},{2,6},{3,7},{4,0},{5,1},{6,2},{7,3},{8,12},{9,13},{10,... | collective-permute-start | bytes 393224 | tf_op jit(solution)/shard_map/ppermute | solution.py:26
  82.2 1.0 %collective-permute-start.25 = (f32[4,64,128]{2,1,0:T(8,128)S(1)}, f32[4,64,128]{2,1,0:T(8,128)S(1)}, u32[]{:S(2)}, u32[]{:S(2)}) collective-permute-start(f32[4,64,128]{2,1,0:T(8,128)S(1)} %get-tuple-element.63), channel_id=1, source_target_pairs={{0,1},{1,0},{2,3},{3,2},{4,5},{5,4},{6,7},{7,6},{8,9},{9,8},{10,11... | collective-permute-start | bytes 393224 | tf_op jit(solution)/shard_map/ppermute | solution.py:26
  83.2 0.6 xor_add_fusion.where_ref
  83.8 2.9 %collective-permute-done.26.refs_9_ = f32[4,64,128]{2,1,0:T(8,128)S(1)} collective-permute-done((f32[4,64,128]{2,1,0:T(8,128)S(1)}, f32[4,64,128]{2,1,0:T(8,128)S(1)}, u32[]{:S(2)}, u32[]{:S(2)}) %collective-permute-start.26) | collective-permute-done | bytes 131104 | tf_op jit(solution)/shard_map/ppermute | solution.py:16
  86.7 0.0 collective-permute-done.24.refs_6_
  86.7 1.1 %collective-permute-done.23.refs_5_ = f32[4,64,128]{2,1,0:T(8,128)S(1)} collective-permute-done((f32[4,64,128]{2,1,0:T(8,128)S(1)}, f32[4,64,128]{2,1,0:T(8,128)S(1)}, u32[]{:S(2)}, u32[]{:S(2)}) %collective-permute-start.23) | collective-permute-done | bytes 131104 | tf_op jit(solution)/shard_map/ppermute | solution.py:26
  87.8 0.1 collective-permute-done.25.refs_7_
  87.9 0.5 copy-done.11
  88.4 0.1 copy-done.12
  88.5 2.2 %shard_map.22 = f32[9,64,128]{2,1,0:T(8,128)} custom-call(s32[9]{0:T(128)} %xor_add_fusion.where_ref, f32[4,64,128]{2,1,0:T(8,128)} %get-tuple-element.68.refs_0_, f32[4,64,128]{2,1,0:T(8,128)} %copy-done.7, f32[4,64,128]{2,1,0:T(8,128)} %copy-done.6, f32[4,64,128]{2,1,0:T(8,128)} %copy-done.8, f32[4,64,128]{2,1,0:T(8,128)} %get-tuple-element.64.refs_4_, ...), custom_call_target="tpu_custom_call" | custom-call | tf_op jit(solution)/shard_map/pallas_call | solution.py:271
  (53 shorter events, 0.4 us)
Async XLA Ops:
  0.0 1.8 %copy-start.5 = (f32[128,3072]{1,0:T(8,128)S(1)}, f32[128,3072]{1,0:T(8,128)}, u32[]{:S(2)}) copy-start(f32[128,3072]{1,0:T(8,128)} %param.1) | copy-start | bytes 4718596
  1.3 6.3 %collective-permute-start = (f32[128,1536]{1,0:T(8,128)S(1)}, f32[128,1536]{1,0:T(8,128)S(1)}, u32[]{:S(2)}, u32[]{:S(2)}) collective-permute-start(f32[128,1536]{1,0:T(8,128)S(1)} %constant_dynamic-slice_fusion.6), channel_id=1, source_target_pairs={{0,2},{2,0},{4,6},{6,4},{8,10},{10,8},{12,14},{14,12},{16,18},{18,... | collective-permute-start | bytes 2359304 | tf_op jit(solution)/shard_map/ppermute | solution.py:11
  1.9 7.5 %collective-permute-start.5 = (f32[1,3072]{1,0:T(1,128)S(1)}, f32[1,3072]{1,0:T(1,128)S(1)}, u32[]{:S(2)}, u32[]{:S(2)}) collective-permute-start(f32[1,3072]{1,0:T(1,128)S(1)} %bitcast.48), channel_id=1, source_target_pairs={{0,24},{2,26},{4,28},{6,30},{8,16},{10,18},{12,20},{14,22},{16,8},... | collective-permute-start | bytes 36872 | tf_op jit(solution)/shard_map/ppermute | solution.py:11
  6.8 4.6 %collective-permute-start.4 = (f32[1,3072]{1,0:T(1,128)S(1)}, f32[1,3072]{1,0:T(1,128)S(1)}, u32[]{:S(2)}, u32[]{:S(2)}) collective-permute-start(f32[1,3072]{1,0:T(1,128)S(1)} %bitcast.49), channel_id=1, source_target_pairs={{0,16},{2,18},{4,20},{6,22},{8,24},{10,26},{12,28},{14,30},{16,0},... | collective-permute-start | bytes 36872 | tf_op jit(solution)/shard_map/ppermute | solution.py:11
  6.8 4.6 %collective-permute-start.3 = (f32[1,3072]{1,0:T(1,128)S(1)}, f32[1,3072]{1,0:T(1,128)S(1)}, u32[]{:S(2)}, u32[]{:S(2)}) collective-permute-start(f32[1,3072]{1,0:T(1,128)S(1)} %bitcast.50), channel_id=1, source_target_pairs={{0,8},{2,10},{4,12},{6,14},{8,0},{10,2},{12,4},{14,6},{16,24},{18,... | collective-permute-start | bytes 36872 | tf_op jit(solution)/shard_map/ppermute | solution.py:11
  7.7 10.8 %collective-permute-start.1 = (f32[2,128,384]{2,1,0:T(8,128)S(1)}, f32[2,128,384]{2,1,0:T(8,128)S(1)}, u32[]{:S(2)}, u32[]{:S(2)}) collective-permute-start(f32[2,128,384]{2,1,0:T(8,128)S(1)} %pad_maximum_fusion.1), channel_id=1, source_target_pairs={{0,4},{2,6},{4,0},{6,2},{8,12},{10,14},{12,8},{14,10},{16,20},{18,... | collective-permute-start | bytes 1179656 | tf_op jit(solution)/shard_map/ppermute | solution.py:11
  11.5 12.7 %collective-permute-start.14 = (f32[2,128,384]{2,1,0:T(8,128)S(1)}, f32[2,128,384]{2,1,0:T(8,128)S(1)}, u32[]{:S(2)}, u32[]{:S(2)}) collective-permute-start(f32[2,128,384]{2,1,0:T(8,128)S(1)} %pad_maximum_fusion.near0), channel_id=1, source_target_pairs={{0,24},{2,26},{4,28},{6,30},{8,0},{10,2},{12,4},{14,6},{16,8},{18,... | collective-permute-start | bytes 1179656 | tf_op jit(solution)/shard_map/ppermute | solution.py:16
  18.5 5.1 %collective-permute-start.6 = (f32[1,1536]{1,0:T(1,128)S(1)}, f32[1,1536]{1,0:T(1,128)S(1)}, u32[]{:S(2)}, u32[]{:S(2)}) collective-permute-start(f32[1,1536]{1,0:T(1,128)S(1)} %constant_dynamic-slice_fusion.4), channel_id=1, source_target_pairs={{0,2},{2,0},{4,6},{6,4},{8,10},{10,8},{12,14},{14,12},{16,18},{18,... | collective-permute-start | bytes 18440 | tf_op jit(solution)/shard_map/ppermute | solution.py:11
  18.5 18.8 %collective-permute-start.2 = (f32[2,128,384]{2,1,0:T(8,128)S(1)}, f32[2,128,384]{2,1,0:T(8,128)S(1)}, u32[]{:S(2)}, u32[]{:S(2)}) collective-permute-start(f32[2,128,384]{2,1,0:T(8,128)S(1)} %pad_maximum_fusion.3), channel_id=1, source_target_pairs={{0,4},{2,6},{4,0},{6,2},{8,12},{10,14},{12,8},{14,10},{16,20},{18,... | collective-permute-start | bytes 1179656 | tf_op jit(solution)/shard_map/ppermute | solution.py:11
  20.1 12.9 %collective-permute-start.8 = (f32[2,128,384]{2,1,0:T(8,128)S(1)}, f32[2,128,384]{2,1,0:T(8,128)S(1)}, u32[]{:S(2)}, u32[]{:S(2)}) collective-permute-start(f32[2,128,384]{2,1,0:T(8,128)S(1)} %collective-permute-done.1.far0), channel_id=1, source_target_pairs={{0,24},{2,26},{4,28},{6,30},{8,0},{10,2},{12,4},{14,6},{16,8},{18,... | collective-permute-start | bytes 1179656 | tf_op jit(solution)/shard_map/ppermute | solution.py:16
  23.6 6.6 %collective-permute-start.7 = (f32[1,768]{1,0:T(1,128)S(1)}, f32[1,768]{1,0:T(1,128)S(1)}, u32[]{:S(2)}, u32[]{:S(2)}) collective-permute-start(f32[1,768]{1,0:T(1,128)S(1)} %constant_dynamic-slice_fusion.2), channel_id=1, source_target_pairs={{0,4},{2,6},{4,0},{6,2},{8,12},{10,14},{12,8},{14,10},{16,20},{18,... | collective-permute-start | bytes 9224 | tf_op jit(solution)/shard_map/ppermute | solution.py:11
  24.2 17.3 %copy-start.3 = (f32[2,128,384]{2,1,0:T(8,128)}, f32[2,128,384]{2,1,0:T(8,128)S(1)}, u32[]{:S(2)}) copy-start(f32[2,128,384]{2,1,0:T(8,128)S(1)} %collective-permute-done.14.refs_0_) | copy-start | bytes 1179652
  24.2 17.2 %collective-permute-start.15 = (f32[2,128,384]{2,1,0:T(8,128)S(1)}, f32[2,128,384]{2,1,0:T(8,128)S(1)}, u32[]{:S(2)}, u32[]{:S(2)}) collective-permute-start(f32[2,128,384]{2,1,0:T(8,128)S(1)} %collective-permute-done.14.refs_0_), channel_id=1, source_target_pairs={{0,24},{2,26},{4,28},{6,30},{8,0},{10,2},{12,4},{14,6},{16,8},{18,... | collective-permute-start | bytes 1179656 | tf_op jit(solution)/shard_map/ppermute | solution.py:16
  33.0 9.5 %copy-start = (f32[2,128,384]{2,1,0:T(8,128)}, f32[2,128,384]{2,1,0:T(8,128)S(1)}, u32[]{:S(2)}) copy-start(f32[2,128,384]{2,1,0:T(8,128)S(1)} %collective-permute-done.8.refs_0_) | copy-start | bytes 1179652
  33.0 16.1 %collective-permute-start.13 = (f32[2,128,384]{2,1,0:T(8,128)S(1)}, f32[2,128,384]{2,1,0:T(8,128)S(1)}, u32[]{:S(2)}, u32[]{:S(2)}) collective-permute-start(f32[2,128,384]{2,1,0:T(8,128)S(1)} %collective-permute-done.8.refs_0_), channel_id=1, source_target_pairs={{0,24},{2,26},{4,28},{6,30},{8,0},{10,2},{12,4},{14,6},{16,8},{18,... | collective-permute-start | bytes 1179656 | tf_op jit(solution)/shard_map/ppermute | solution.py:16
  37.3 4.1 %copy-start.2 = (f32[2,128,384]{2,1,0:T(8,128)}, f32[2,128,384]{2,1,0:T(8,128)S(1)}, u32[]{:S(2)}) copy-start(f32[2,128,384]{2,1,0:T(8,128)S(1)} %collective-permute-done.2.far1) | copy-start | bytes 1179652
  51.2 5.9 %collective-permute-start.16 = (f32[2,2,8,64,128]{4,3,2,1,0:T(8,128)}, f32[2,2,8,64,128]{4,3,2,1,0:T(8,128)}, u32[]{:S(2)}, u32[]{:S(2)}) collective-permute-start(f32[2,2,8,64,128]{4,3,2,1,0:T(8,128)} %get-tuple-element.33), channel_id=1, source_target_pairs={{0,2},{2,0},{4,6},{6,4},{8,10},{10,8},{12,14},{14,12},{16,18},{18,... | collective-permute-start | bytes 3145736 | tf_op jit(solution)/shard_map/ppermute | solution.py:11
  51.2 4.8 %collective-permute-start.9 = (f32[2,2,4,64,128]{4,3,2,1,0:T(8,128)}, f32[2,2,4,64,128]{4,3,2,1,0:T(8,128)}, u32[]{:S(2)}, u32[]{:S(2)}) collective-permute-start(f32[2,2,4,64,128]{4,3,2,1,0:T(8,128)} %get-tuple-element.27), channel_id=1, source_target_pairs={{0,2},{2,0},{4,6},{6,4},{8,10},{10,8},{12,14},{14,12},{16,18},{18,... | collective-permute-start | bytes 1572872 | tf_op jit(solution)/shard_map/ppermute | solution.py:11
  51.7 13.8 %collective-permute-start.18 = (f32[2,128,384]{2,1,0:T(8,128)S(1)}, f32[2,128,384]{2,1,0:T(8,128)S(1)}, u32[]{:S(2)}, u32[]{:S(2)}) collective-permute-start(f32[2,128,384]{2,1,0:T(8,128)S(1)} %pad_maximum_fusion.2.near1), channel_id=1, source_target_pairs={{0,24},{2,26},{4,28},{6,30},{8,0},{10,2},{12,4},{14,6},{16,8},{18,... | collective-permute-start | bytes 1179656 | tf_op jit(solution)/shard_map/ppermute | solution.py:16
  56.0 17.1 %collective-permute-start.17 = (f32[2,128,384]{2,1,0:T(8,128)}, f32[2,128,384]{2,1,0:T(8,128)S(1)}, u32[]{:S(2)}, u32[]{:S(2)}) collective-permute-start(f32[2,128,384]{2,1,0:T(8,128)} %copy-done.2), channel_id=1, source_target_pairs={{0,24},{2,26},{4,28},{6,30},{8,0},{10,2},{12,4},{14,6},{16,8},{18,... | collective-permute-start | bytes 1179656 | tf_op jit(solution)/shard_map/ppermute | solution.py:16
  58.6 8.3 %copy-start.4 = (f32[2,128,384]{2,1,0:T(8,128)S(1)}, f32[2,128,384]{2,1,0:T(8,128)}, u32[]{:S(2)}) copy-start(f32[2,128,384]{2,1,0:T(8,128)} %copy-done.3) | copy-start | bytes 1179652
  58.7 16.2 %collective-permute-start.22 = (f32[8,64,128]{2,1,0:T(8,128)S(1)}, f32[8,64,128]{2,1,0:T(8,128)S(1)}, u32[]{:S(2)}, u32[]{:S(2)}) collective-permute-start(f32[8,64,128]{2,1,0:T(8,128)S(1)} %dynamic-slice_bitcast_fusion), channel_id=1, source_target_pairs={{0,1},{1,0},{2,3},{3,2},{4,5},{5,4},{6,7},{7,6},{8,9},{9,8},{10,11... | collective-permute-start | bytes 786440 | tf_op jit(solution)/shard_map/ppermute | solution.py:26
  60.3 16.1 %collective-permute-start.20 = (f32[8,64,128]{2,1,0:T(8,128)S(1)}, f32[8,64,128]{2,1,0:T(8,128)S(1)}, u32[]{:S(2)}, u32[]{:S(2)}) collective-permute-start(f32[8,64,128]{2,1,0:T(8,128)S(1)} %get-tuple-element.57), channel_id=1, source_target_pairs={{0,4},{1,5},{2,6},{3,7},{4,0},{5,1},{6,2},{7,3},{8,12},{9,13},{10,... | collective-permute-start | bytes 786440 | tf_op jit(solution)/shard_map/ppermute | solution.py:26
  60.8 16.1 %collective-permute-start.21 = (f32[8,64,128]{2,1,0:T(8,128)S(1)}, f32[8,64,128]{2,1,0:T(8,128)S(1)}, u32[]{:S(2)}, u32[]{:S(2)}) collective-permute-start(f32[8,64,128]{2,1,0:T(8,128)S(1)} %get-tuple-element.58), channel_id=1, source_target_pairs={{0,5},{1,4},{2,7},{3,6},{4,1},{5,0},{6,3},{7,2},{8,13},{9,12},{10,... | collective-permute-start | bytes 786440 | tf_op jit(solution)/shard_map/ppermute | solution.py:26
  62.4 10.7 %copy-start.1 = (f32[2,128,384]{2,1,0:T(8,128)S(1)}, f32[2,128,384]{2,1,0:T(8,128)}, u32[]{:S(2)}) copy-start(f32[2,128,384]{2,1,0:T(8,128)} %copy-done) | copy-start | bytes 1179652
  65.5 15.7 %collective-permute-start.11 = (f32[4,64,128]{2,1,0:T(8,128)S(1)}, f32[4,64,128]{2,1,0:T(8,128)S(1)}, u32[]{:S(2)}, u32[]{:S(2)}) collective-permute-start(f32[4,64,128]{2,1,0:T(8,128)S(1)} %get-tuple-element.69), channel_id=1, source_target_pairs={{0,5},{1,4},{2,7},{3,6},{4,1},{5,0},{6,3},{7,2},{8,13},{9,12},{10,... | collective-permute-start | bytes 393224 | tf_op jit(solution)/shard_map/ppermute | solution.py:26
  74.1 4.7 %collective-permute-start.19 = (f32[2,2,4,64,128]{4,3,2,1,0:T(8,128)S(1)}, f32[2,2,4,64,128]{4,3,2,1,0:T(8,128)S(1)}, u32[]{:S(2)}, u32[]{:S(2)}) collective-permute-start(f32[2,2,4,64,128]{4,3,2,1,0:T(8,128)S(1)} %get-tuple-element.41), channel_id=1, source_target_pairs={{0,2},{2,0},{4,6},{6,4},{8,10},{10,8},{12,14},{14,12},{16,18},{18,... | collective-permute-start | bytes 1572872 | tf_op jit(solution)/shard_map/ppermute | solution.py:11
  74.9 7.3 %collective-permute-start.10 = (f32[4,64,128]{2,1,0:T(8,128)S(1)}, f32[4,64,128]{2,1,0:T(8,128)S(1)}, u32[]{:S(2)}, u32[]{:S(2)}) collective-permute-start(f32[4,64,128]{2,1,0:T(8,128)S(1)} %get-tuple-element.70), channel_id=1, source_target_pairs={{0,4},{1,5},{2,6},{3,7},{4,0},{5,1},{6,2},{7,3},{8,12},{9,13},{10,... | collective-permute-start | bytes 393224 | tf_op jit(solution)/shard_map/ppermute | solution.py:26
  76.4 7.4 %collective-permute-start.12 = (f32[4,64,128]{2,1,0:T(8,128)S(1)}, f32[4,64,128]{2,1,0:T(8,128)S(1)}, u32[]{:S(2)}, u32[]{:S(2)}) collective-permute-start(f32[4,64,128]{2,1,0:T(8,128)S(1)} %get-tuple-element.67), channel_id=1, source_target_pairs={{0,1},{1,0},{2,3},{3,2},{4,5},{5,4},{6,7},{7,6},{8,9},{9,8},{10,11... | collective-permute-start | bytes 393224 | tf_op jit(solution)/shard_map/ppermute | solution.py:26
  77.7 9.0 %collective-permute-start.26 = (f32[4,64,128]{2,1,0:T(8,128)S(1)}, f32[4,64,128]{2,1,0:T(8,128)S(1)}, u32[]{:S(2)}, u32[]{:S(2)}) collective-permute-start(f32[4,64,128]{2,1,0:T(8,128)S(1)} %get-tuple-element.61), channel_id=1, source_target_pairs={{0,16},{2,18},{4,20},{6,22},{8,24},{10,26},{12,28},{14,30},{16,0},... | collective-permute-start | bytes 393224 | tf_op jit(solution)/shard_map/ppermute | solution.py:16
  79.0 7.7 %collective-permute-start.24 = (f32[4,64,128]{2,1,0:T(8,128)S(1)}, f32[4,64,128]{2,1,0:T(8,128)S(1)}, u32[]{:S(2)}, u32[]{:S(2)}) collective-permute-start(f32[4,64,128]{2,1,0:T(8,128)S(1)} %get-tuple-element.65), channel_id=1, source_target_pairs={{0,5},{1,4},{2,7},{3,6},{4,1},{5,0},{6,3},{7,2},{8,13},{9,12},{10,... | collective-permute-start | bytes 393224 | tf_op jit(solution)/shard_map/ppermute | solution.py:26
  81.2 6.7 %copy-start.6 = (f32[4,64,128]{2,1,0:T(8,128)}, f32[4,64,128]{2,1,0:T(8,128)S(1)}, u32[]{:S(2)}) copy-start(f32[4,64,128]{2,1,0:T(8,128)S(1)} %collective-permute-done.11.refs_2_) | copy-start | bytes 393220
  81.2 6.6 %collective-permute-start.23 = (f32[4,64,128]{2,1,0:T(8,128)S(1)}, f32[4,64,128]{2,1,0:T(8,128)S(1)}, u32[]{:S(2)}, u32[]{:S(2)}) collective-permute-start(f32[4,64,128]{2,1,0:T(8,128)S(1)} %get-tuple-element.66), channel_id=1, source_target_pairs={{0,4},{1,5},{2,6},{3,7},{4,0},{5,1},{6,2},{7,3},{8,12},{9,13},{10,... | collective-permute-start | bytes 393224 | tf_op jit(solution)/shard_map/ppermute | solution.py:26
  82.2 5.7 %copy-start.7 = (f32[4,64,128]{2,1,0:T(8,128)}, f32[4,64,128]{2,1,0:T(8,128)S(1)}, u32[]{:S(2)}) copy-start(f32[4,64,128]{2,1,0:T(8,128)S(1)} %collective-permute-done.10.refs_1_) | copy-start | bytes 393220
  82.2 5.7 %collective-permute-start.25 = (f32[4,64,128]{2,1,0:T(8,128)S(1)}, f32[4,64,128]{2,1,0:T(8,128)S(1)}, u32[]{:S(2)}, u32[]{:S(2)}) collective-permute-start(f32[4,64,128]{2,1,0:T(8,128)S(1)} %get-tuple-element.63), channel_id=1, source_target_pairs={{0,1},{1,0},{2,3},{3,2},{4,5},{5,4},{6,7},{7,6},{8,9},{9,8},{10,11... | collective-permute-start | bytes 393224 | tf_op jit(solution)/shard_map/ppermute | solution.py:26
  83.8 4.1 %copy-start.8 = (f32[4,64,128]{2,1,0:T(8,128)}, f32[4,64,128]{2,1,0:T(8,128)S(1)}, u32[]{:S(2)}) copy-start(f32[4,64,128]{2,1,0:T(8,128)S(1)} %collective-permute-done.12.refs_3_) | copy-start | bytes 393220
  86.7 1.2 %copy-start.9 = (f32[4,64,128]{2,1,0:T(8,128)}, f32[4,64,128]{2,1,0:T(8,128)S(1)}, u32[]{:S(2)}) copy-start(f32[4,64,128]{2,1,0:T(8,128)S(1)} %collective-permute-done.26.refs_9_) | copy-start | bytes 393220
  86.7 1.2 %copy-start.10 = (f32[4,64,128]{2,1,0:T(8,128)}, f32[4,64,128]{2,1,0:T(8,128)S(1)}, u32[]{:S(2)}) copy-start(f32[4,64,128]{2,1,0:T(8,128)S(1)} %collective-permute-done.24.refs_6_) | copy-start | bytes 393220
  87.8 0.7 copy-start.11
  87.9 0.6 copy-start.12

commit v7 on v6

--- a/solution.py
+++ b/solution.py
@@ -232,10 +232,9 @@
             2 * flops,
         )
     keep, send = outs
-    first_total = exchange(*own)
-    shares = [messages(first_total, shard)]
-    total = after(exchange(keep, send), first_total)
+    total = exchange(keep, send)
     last = messages(total, shard)
+    shares = [messages(after(exchange(*own), total), shard)]
     pending = last
 
     mean = after(mean, total)

time: 91.5 us -> 91.5 us (level)
  no operation moved by 1% of the time
where the time goes in v7:
time: 91.5 us; the launch traced here: 90.7 us
  waiting for transfers between devices  36.7 us (40%)
  starting transfers between devices  35.9 us (39%)
  Pallas kernels  9.92 us (11%)
  local copies, waits for them, and re-layouts  4.46 us (5%)
  other arithmetic  3.41 us (4%)
    ppermute x7, waiting for transfers between devices, shift(): lax.ppermute(value, 'blk', [(k, (k + steps) % count) for k in range(count)])  22.1 us
    ppermute x7, starting transfers between devices, shift(): lax.ppermute(value, 'blk', [(k, (k + steps) % count) for k in range(count)])  15.7 us
    ppermute x11, waiting for transfers between devices, swap(): lax.ppermute(value, 'blk', [(k, k ^ mask) for k in range(lax.axis_size('b...  12.4 us
    ppermute x11, starting transfers between devices, swap(): lax.ppermute(value, 'blk', [(k, k ^ mask) for k in range(lax.axis_size('b...  10.6 us
    ppermute x9, starting transfers between devices, hop(): return lax.ppermute(value, ('blk', 'par'), pairs)  9.64 us
    pallas_call x5, Pallas kernels, call(): pl.pallas_call(kernel, out_shape=outs, in_specs=[SMEM] * len(scalars) + [...  7.74 us
    add x3, other arithmetic, exchange(): return keep + swap(send, 1)  2.52 us
    ppermute x9, waiting for transfers between devices, hop(): return lax.ppermute(value, ('blk', 'par'), pairs)  2.27 us
  transfers between devices with their start and end apart: 27, of which 12 were waited for; matrix products, arithmetic and copies ran while one was open for 7% of the time, Pallas kernels for 6%

profile of v7, /device:TPU:0, one launch (start us, length us, event | category | flops | bytes accessed | tf_op | source)
XLA Modules:
  0.0 90.7 jit_solution(11506947335755972521)
XLA Ops:
  0.0 1.3 %constant_dynamic-slice_fusion.6 = f32[128,1536]{1,0:T(8,128)S(1)} fusion(f32[128,3072]{1,0:T(8,128)} %param.1, s32[]{:T(128)S(6)} %select_n.113), kind=kLoop, calls=%fused_computation.32 | loop fusion | bytes 1572868 | tf_op jit(solution)/shard_map/dynamic_slice | solution.py:176
  1.3 0.5 collective-permute-start
  1.8 0.1 reduce_sum.9
  1.9 4.9 %collective-permute-start.5 = (f32[1,3072]{1,0:T(1,128)S(1)}, f32[1,3072]{1,0:T(1,128)S(1)}, u32[]{:S(2)}, u32[]{:S(2)}) collective-permute-start(f32[1,3072]{1,0:T(1,128)S(1)} %bitcast.48), channel_id=1, source_target_pairs={{0,24},{2,26},{4,28},{6,30},{8,16},{10,18},{12,20},{14,22},{16,8},... | collective-permute-start | bytes 36872 | tf_op jit(solution)/shard_map/ppermute | solution.py:11
  6.8 0.6 collective-permute-start.3
  7.5 0.1 dynamic-slice_bitcast_fusion.5
  7.6 0.1 dynamic-slice_bitcast_fusion.4
  7.7 1.7 %collective-permute-start.1 = (f32[2,128,384]{2,1,0:T(8,128)S(1)}, f32[2,128,384]{2,1,0:T(8,128)S(1)}, u32[]{:S(2)}, u32[]{:S(2)}) collective-permute-start(f32[2,128,384]{2,1,0:T(8,128)S(1)} %pad_maximum_fusion.1), channel_id=1, source_target_pairs={{0,4},{2,6},{4,0},{6,2},{8,12},{10,14},{12,8},{14,10},{16,20},{18,... | collective-permute-start | bytes 1179656 | tf_op jit(solution)/shard_map/ppermute | solution.py:11
  9.4 2.0 %collective-permute-done.4 = f32[1,3072]{1,0:T(1,128)S(1)} collective-permute-done((f32[1,3072]{1,0:T(1,128)S(1)}, f32[1,3072]{1,0:T(1,128)S(1)}, u32[]{:S(2)}, u32[]{:S(2)}) %collective-permute-start.4) | collective-permute-done | bytes 12320 | tf_op jit(solution)/shard_map/ppermute | solution.py:11
  11.5 1.7 %collective-permute-start.11 = (f32[2,128,384]{2,1,0:T(8,128)S(1)}, f32[2,128,384]{2,1,0:T(8,128)S(1)}, u32[]{:S(2)}, u32[]{:S(2)}) collective-permute-start(f32[2,128,384]{2,1,0:T(8,128)S(1)} %pad_maximum_fusion.near0), channel_id=1, source_target_pairs={{0,24},{2,26},{4,28},{6,30},{8,0},{10,2},{12,4},{14,6},{16,8},{18,... | collective-permute-start | bytes 1179656 | tf_op jit(solution)/shard_map/ppermute | solution.py:16
  13.2 5.3 %collective-permute-done.1.far0 = f32[2,128,384]{2,1,0:T(8,128)S(1)} collective-permute-done((f32[2,128,384]{2,1,0:T(8,128)S(1)}, f32[2,128,384]{2,1,0:T(8,128)S(1)}, u32[]{:S(2)}, u32[]{:S(2)}) %collective-permute-start.1) | collective-permute-done | bytes 393248 | tf_op jit(solution)/shard_map/ppermute | solution.py:11
  18.5 0.0 collective-permute-start.6
  18.5 1.6 %collective-permute-start.2 = (f32[2,128,384]{2,1,0:T(8,128)S(1)}, f32[2,128,384]{2,1,0:T(8,128)S(1)}, u32[]{:S(2)}, u32[]{:S(2)}) collective-permute-start(f32[2,128,384]{2,1,0:T(8,128)S(1)} %pad_maximum_fusion.3), channel_id=1, source_target_pairs={{0,4},{2,6},{4,0},{6,2},{8,12},{10,14},{12,8},{14,10},{16,20},{18,... | collective-permute-start | bytes 1179656 | tf_op jit(solution)/shard_map/ppermute | solution.py:11
  20.1 3.5 %collective-permute-start.8 = (f32[2,128,384]{2,1,0:T(8,128)S(1)}, f32[2,128,384]{2,1,0:T(8,128)S(1)}, u32[]{:S(2)}, u32[]{:S(2)}) collective-permute-start(f32[2,128,384]{2,1,0:T(8,128)S(1)} %collective-permute-done.1.far0), channel_id=1, source_target_pairs={{0,24},{2,26},{4,28},{6,30},{8,0},{10,2},{12,4},{14,6},{16,8},{18,... | collective-permute-start | bytes 1179656 | tf_op jit(solution)/shard_map/ppermute | solution.py:16
  23.6 0.0 collective-permute-done.6
  23.6 0.6 collective-permute-start.7
  24.2 0.9 collective-permute-start.12
  25.1 5.1 %collective-permute-done.7 = f32[1,768]{1,0:T(1,128)S(1)} collective-permute-done((f32[1,768]{1,0:T(1,128)S(1)}, f32[1,768]{1,0:T(1,128)S(1)}, u32[]{:S(2)}, u32[]{:S(2)}) %collective-permute-start.7) | collective-permute-done | bytes 3104 | tf_op jit(solution)/shard_map/ppermute | solution.py:11
  30.2 2.9 %collective-permute-done.8.refs_0_ = f32[2,128,384]{2,1,0:T(8,128)S(1)} collective-permute-done((f32[2,128,384]{2,1,0:T(8,128)S(1)}, f32[2,128,384]{2,1,0:T(8,128)S(1)}, u32[]{:S(2)}, u32[]{:S(2)}) %collective-permute-start.8) | collective-permute-done | bytes 393248 | tf_op jit(solution)/shard_map/ppermute | solution.py:16
  33.0 4.3 %collective-permute-start.10 = (f32[2,128,384]{2,1,0:T(8,128)S(1)}, f32[2,128,384]{2,1,0:T(8,128)S(1)}, u32[]{:S(2)}, u32[]{:S(2)}) collective-permute-start(f32[2,128,384]{2,1,0:T(8,128)S(1)} %collective-permute-done.8.refs_0_), channel_id=1, source_target_pairs={{0,24},{2,26},{4,28},{6,30},{8,0},{10,2},{12,4},{14,6},{16,8},{18,... | collective-permute-start | bytes 1179656 | tf_op jit(solution)/shard_map/ppermute | solution.py:16
  37.4 2.7 %shard_map.17 = (f32[2,2,4,64,128]{4,3,2,1,0:T(8,128)S(1)}, f32[2,2,4,64,128]{4,3,2,1,0:T(8,128)}, bf16[2,2,256,384]{3,2,1,0:T(8,128)(2,1)S(1)}, bf16[2,2,256,384]{3,2,1,0:T(8,128)(2,1)S(1)}) custom-call(f32[2,128,384]{2,1,0:T(8,128)S(1)} %pad_maximum_fusion.near0, f32[2,128,384]{2,1,0:T(8,128)S(1)} %collective-permute-done.1.far0, ...), custom_call_target="tpu_custom_call" | custom-call | tf_op jit(solution)/shard_map/pallas_call | solution.py:119
  40.0 1.4 %collective-permute-done.12.right_ref = f32[2,128,384]{2,1,0:T(8,128)S(1)} collective-permute-done((f32[2,128,384]{2,1,0:T(8,128)S(1)}, f32[2,128,384]{2,1,0:T(8,128)S(1)}, u32[]{:S(2)}, u32[]{:S(2)}) %collective-permute-start.12) | collective-permute-done | bytes 393248 | tf_op jit(solution)/shard_map/ppermute | solution.py:16
  41.5 1.0 %shard_map.18 = (f32[2,2,8,64,128]{4,3,2,1,0:T(8,128)S(1)}, f32[2,2,8,64,128]{4,3,2,1,0:T(8,128)S(1)}) custom-call(f32[2,1,384]{2,1,0:T(1,128)S(1)} %pad_maximum_fusion.4.mean_ref, bf16[2,2,256,384]{3,2,1,0:T(8,128)(2,1)S(1)} %get-tuple-element.28.high_ref, bf16[2,2,256,384]{3,2,1,0:T(8,128)(2,1)S(1)} %get-tuple-element.29.low_ref, ...), custom_call_target="tpu_custom_call" | custom-call | tf_op jit(solution)/shard_map/pallas_call | solution.py:119
  42.5 6.7 %collective-permute-done.10.right_ref = f32[2,128,384]{2,1,0:T(8,128)S(1)} collective-permute-done((f32[2,128,384]{2,1,0:T(8,128)S(1)}, f32[2,128,384]{2,1,0:T(8,128)S(1)}, u32[]{:S(2)}, u32[]{:S(2)}) %collective-permute-start.10) | collective-permute-done | bytes 393248 | tf_op jit(solution)/shard_map/ppermute | solution.py:16
  49.2 2.0 %shard_map.19 = (f32[2,2,8,64,128]{4,3,2,1,0:T(8,128)S(1)}, f32[2,2,8,64,128]{4,3,2,1,0:T(8,128)}) custom-call(f32[2,1,384]{2,1,0:T(1,128)S(1)} %pad_maximum_fusion.4.mean_ref, bf16[2,2,256,384]{3,2,1,0:T(8,128)(2,1)S(1)} %get-tuple-element.28.high_ref, bf16[2,2,256,384]{3,2,1,0:T(8,128)(2,1)S(1)} %get-tuple-element.29.low_ref, ...), custom_call_target="tpu_custom_call" | custom-call | tf_op jit(solution)/shard_map/pallas_call | solution.py:119
  51.2 0.0 collective-permute-start.13
  51.2 0.5 collective-permute-start.9
  51.7 4.3 %collective-permute-start.18 = (f32[2,128,384]{2,1,0:T(8,128)S(1)}, f32[2,128,384]{2,1,0:T(8,128)S(1)}, u32[]{:S(2)}, u32[]{:S(2)}) collective-permute-start(f32[2,128,384]{2,1,0:T(8,128)S(1)} %pad_maximum_fusion.2.near1), channel_id=1, source_target_pairs={{0,24},{2,26},{4,28},{6,30},{8,0},{10,2},{12,4},{14,6},{16,8},{18,... | collective-permute-start | bytes 1179656 | tf_op jit(solution)/shard_map/ppermute | solution.py:16
  56.0 0.0 collective-permute-start.17
  56.0 0.0 collective-permute-done.9
  56.1 1.1 %add.197 = f32[2,2,4,64,128]{4,3,2,1,0:T(8,128)S(1)} add(f32[2,2,4,64,128]{4,3,2,1,0:T(8,128)S(1)} %get-tuple-element.26, f32[2,2,4,64,128]{4,3,2,1,0:T(8,128)} %collective-permute-done.9) | non-fusion elementwise | flops 131072 | bytes 1572864 | tf_op jit(solution)/shard_map/add | solution.py:130
  57.2 1.4 %add.198 = f32[2,2,8,64,128]{4,3,2,1,0:T(8,128)S(1)} add(f32[2,2,8,64,128]{4,3,2,1,0:T(8,128)S(1)} %get-tuple-element.32, f32[2,2,8,64,128]{4,3,2,1,0:T(8,128)} %collective-permute-done.13) | non-fusion elementwise | flops 262144 | bytes 3145728 | tf_op jit(solution)/shard_map/add | solution.py:130
  58.5 0.1 fusion.5
  58.7 1.6 %collective-permute-start.22 = (f32[8,64,128]{2,1,0:T(8,128)S(1)}, f32[8,64,128]{2,1,0:T(8,128)S(1)}, u32[]{:S(2)}, u32[]{:S(2)}) collective-permute-start(f32[8,64,128]{2,1,0:T(8,128)S(1)} %dynamic-slice_bitcast_fusion), channel_id=1, source_target_pairs={{0,1},{1,0},{2,3},{3,2},{4,5},{5,4},{6,7},{7,6},{8,9},{9,8},{10,11... | collective-permute-start | bytes 786440 | tf_op jit(solution)/shard_map/ppermute | solution.py:26
  60.3 0.6 collective-permute-start.20
  60.8 1.5 %collective-permute-start.21 = (f32[8,64,128]{2,1,0:T(8,128)S(1)}, f32[8,64,128]{2,1,0:T(8,128)S(1)}, u32[]{:S(2)}, u32[]{:S(2)}) collective-permute-start(f32[8,64,128]{2,1,0:T(8,128)S(1)} %get-tuple-element.58), channel_id=1, source_target_pairs={{0,5},{1,4},{2,7},{3,6},{4,1},{5,0},{6,3},{7,2},{8,13},{9,12},{10,... | collective-permute-start | bytes 786440 | tf_op jit(solution)/shard_map/ppermute | solution.py:26
  62.4 3.1 %collective-permute-done.18.refs_1_ = f32[2,128,384]{2,1,0:T(8,128)S(1)} collective-permute-done((f32[2,128,384]{2,1,0:T(8,128)S(1)}, f32[2,128,384]{2,1,0:T(8,128)S(1)}, u32[]{:S(2)}, u32[]{:S(2)}) %collective-permute-start.18) | collective-permute-done | bytes 393248 | tf_op jit(solution)/shard_map/ppermute | solution.py:16
  65.5 1.4 %collective-permute-start.15 = (f32[4,64,128]{2,1,0:T(8,128)S(1)}, f32[4,64,128]{2,1,0:T(8,128)S(1)}, u32[]{:S(2)}, u32[]{:S(2)}) collective-permute-start(f32[4,64,128]{2,1,0:T(8,128)S(1)} %get-tuple-element.69), channel_id=1, source_target_pairs={{0,5},{1,4},{2,7},{3,6},{4,1},{5,0},{6,3},{7,2},{8,13},{9,12},{10,... | collective-permute-start | bytes 393224 | tf_op jit(solution)/shard_map/ppermute | solution.py:26
  67.0 1.0 %shard_map.20 = (f32[2,2,4,64,128]{4,3,2,1,0:T(8,128)S(1)}, f32[2,2,4,64,128]{4,3,2,1,0:T(8,128)S(1)}) custom-call(s32[1]{0:T(128)} %bitcast.15.flag_ref, f32[2,1,384]{2,1,0:T(1,128)S(1)} %pad_maximum_fusion.4.mean_ref, bf16[2,2,256,384]{3,2,1,0:T(8,128)(2,1)S(1)} %get-tuple-element.28.high_ref, bf16[2,2,256,384]{3,2,1,0:T(8,128)(2,1)S(1)} %get-tuple-element.29.low_ref, ...), custom_call_target="tpu_custom_call" | custom-call | tf_op jit(solution)/shard_map/pallas_call | solution.py:119
  68.0 5.1 %collective-permute-done.17.refs_1_ = f32[2,128,384]{2,1,0:T(8,128)S(1)} collective-permute-done((f32[2,128,384]{2,1,0:T(8,128)}, f32[2,128,384]{2,1,0:T(8,128)S(1)}, u32[]{:S(2)}, u32[]{:S(2)}) %collective-permute-start.17) | collective-permute-done | bytes 393248 | tf_op jit(solution)/shard_map/ppermute | solution.py:16
  73.1 1.0 %shard_map.21 = (f32[2,2,4,64,128]{4,3,2,1,0:T(8,128)S(1)}, f32[2,2,4,64,128]{4,3,2,1,0:T(8,128)S(1)}) custom-call(s32[1]{0:T(128)} %bitcast.15.flag_ref, f32[2,1,384]{2,1,0:T(1,128)S(1)} %pad_maximum_fusion.4.mean_ref, bf16[2,2,256,384]{3,2,1,0:T(8,128)(2,1)S(1)} %get-tuple-element.28.high_ref, bf16[2,2,256,384]{3,2,1,0:T(8,128)(2,1)S(1)} %get-tuple-element.29.low_ref, ...), custom_call_target="tpu_custom_call" | custom-call | tf_op jit(solution)/shard_map/pallas_call | solution.py:119
  74.1 0.1 collective-permute-start.19
  74.2 0.7 dynamic-slice_bitcast_fusion.16
  74.9 0.5 collective-permute-start.14
  75.4 1.0 %collective-permute-done.20 = f32[8,64,128]{2,1,0:T(8,128)S(1)} collective-permute-done((f32[8,64,128]{2,1,0:T(8,128)S(1)}, f32[8,64,128]{2,1,0:T(8,128)S(1)}, u32[]{:S(2)}, u32[]{:S(2)}) %collective-permute-start.20) | collective-permute-done | bytes 262176 | tf_op jit(solution)/shard_map/ppermute | solution.py:26
  76.4 0.5 collective-permute-start.16
  76.9 0.1 add_add_fusion
  77.0 0.7 fusion.8
  77.7 1.1 %collective-permute-start.26 = (f32[4,64,128]{2,1,0:T(8,128)S(1)}, f32[4,64,128]{2,1,0:T(8,128)S(1)}, u32[]{:S(2)}, u32[]{:S(2)}) collective-permute-start(f32[4,64,128]{2,1,0:T(8,128)S(1)} %get-tuple-element.61), channel_id=1, source_target_pairs={{0,16},{2,18},{4,20},{6,22},{8,24},{10,26},{12,28},{14,30},{16,0},... | collective-permute-start | bytes 393224 | tf_op jit(solution)/shard_map/ppermute | solution.py:16
  78.8 0.0 collective-permute-done.19
  78.8 0.1 add.207
  79.0 1.6 %collective-permute-start.24 = (f32[4,64,128]{2,1,0:T(8,128)S(1)}, f32[4,64,128]{2,1,0:T(8,128)S(1)}, u32[]{:S(2)}, u32[]{:S(2)}) collective-permute-start(f32[4,64,128]{2,1,0:T(8,128)S(1)} %get-tuple-element.65), channel_id=1, source_target_pairs={{0,5},{1,4},{2,7},{3,6},{4,1},{5,0},{6,3},{7,2},{8,13},{9,12},{10,... | collective-permute-start | bytes 393224 | tf_op jit(solution)/shard_map/ppermute | solution.py:26
  80.5 0.7 dynamic-slice_bitcast_fusion.12
  81.2 0.0 collective-permute-done.15.refs_2_
  81.2 1.0 %collective-permute-start.23 = (f32[4,64,128]{2,1,0:T(8,128)S(1)}, f32[4,64,128]{2,1,0:T(8,128)S(1)}, u32[]{:S(2)}, u32[]{:S(2)}) collective-permute-start(f32[4,64,128]{2,1,0:T(8,128)S(1)} %get-tuple-element.66), channel_id=1, source_target_pairs={{0,4},{1,5},{2,6},{3,7},{4,0},{5,1},{6,2},{7,3},{8,12},{9,13},{10,... | collective-permute-start | bytes 393224 | tf_op jit(solution)/shard_map/ppermute | solution.py:26
  82.2 1.0 %collective-permute-start.25 = (f32[4,64,128]{2,1,0:T(8,128)S(1)}, f32[4,64,128]{2,1,0:T(8,128)S(1)}, u32[]{:S(2)}, u32[]{:S(2)}) collective-permute-start(f32[4,64,128]{2,1,0:T(8,128)S(1)} %get-tuple-element.63), channel_id=1, source_target_pairs={{0,1},{1,0},{2,3},{3,2},{4,5},{5,4},{6,7},{7,6},{8,9},{9,8},{10,11... | collective-permute-start | bytes 393224 | tf_op jit(solution)/shard_map/ppermute | solution.py:26
  83.2 0.6 xor_add_fusion.where_ref
  83.8 2.9 %collective-permute-done.26.refs_9_ = f32[4,64,128]{2,1,0:T(8,128)S(1)} collective-permute-done((f32[4,64,128]{2,1,0:T(8,128)S(1)}, f32[4,64,128]{2,1,0:T(8,128)S(1)}, u32[]{:S(2)}, u32[]{:S(2)}) %collective-permute-start.26) | collective-permute-done | bytes 131104 | tf_op jit(solution)/shard_map/ppermute | solution.py:16
  86.7 0.0 collective-permute-done.24.refs_6_
  86.7 1.1 %collective-permute-done.23.refs_5_ = f32[4,64,128]{2,1,0:T(8,128)S(1)} collective-permute-done((f32[4,64,128]{2,1,0:T(8,128)S(1)}, f32[4,64,128]{2,1,0:T(8,128)S(1)}, u32[]{:S(2)}, u32[]{:S(2)}) %collective-permute-start.23) | collective-permute-done | bytes 131104 | tf_op jit(solution)/shard_map/ppermute | solution.py:26
  87.8 0.1 collective-permute-done.25.refs_7_
  87.9 0.5 copy-done.11
  88.4 0.1 copy-done.12
  88.5 2.2 %shard_map.22 = f32[9,64,128]{2,1,0:T(8,128)} custom-call(s32[9]{0:T(128)} %xor_add_fusion.where_ref, f32[4,64,128]{2,1,0:T(8,128)} %get-tuple-element.68.refs_0_, f32[4,64,128]{2,1,0:T(8,128)} %copy-done.7, f32[4,64,128]{2,1,0:T(8,128)} %copy-done.6, f32[4,64,128]{2,1,0:T(8,128)} %copy-done.8, f32[4,64,128]{2,1,0:T(8,128)} %get-tuple-element.64.refs_4_, ...), custom_call_target="tpu_custom_call" | custom-call | tf_op jit(solution)/shard_map/pallas_call | solution.py:270
  (53 shorter events, 0.4 us)
Async XLA Ops:
  0.0 1.8 %copy-start.5 = (f32[128,3072]{1,0:T(8,128)S(1)}, f32[128,3072]{1,0:T(8,128)}, u32[]{:S(2)}) copy-start(f32[128,3072]{1,0:T(8,128)} %param.1) | copy-start | bytes 4718596
  1.3 6.3 %collective-permute-start = (f32[128,1536]{1,0:T(8,128)S(1)}, f32[128,1536]{1,0:T(8,128)S(1)}, u32[]{:S(2)}, u32[]{:S(2)}) collective-permute-start(f32[128,1536]{1,0:T(8,128)S(1)} %constant_dynamic-slice_fusion.6), channel_id=1, source_target_pairs={{0,2},{2,0},{4,6},{6,4},{8,10},{10,8},{12,14},{14,12},{16,18},{18,... | collective-permute-start | bytes 2359304 | tf_op jit(solution)/shard_map/ppermute | solution.py:11
  1.9 7.5 %collective-permute-start.5 = (f32[1,3072]{1,0:T(1,128)S(1)}, f32[1,3072]{1,0:T(1,128)S(1)}, u32[]{:S(2)}, u32[]{:S(2)}) collective-permute-start(f32[1,3072]{1,0:T(1,128)S(1)} %bitcast.48), channel_id=1, source_target_pairs={{0,24},{2,26},{4,28},{6,30},{8,16},{10,18},{12,20},{14,22},{16,8},... | collective-permute-start | bytes 36872 | tf_op jit(solution)/shard_map/ppermute | solution.py:11
  6.8 4.6 %collective-permute-start.4 = (f32[1,3072]{1,0:T(1,128)S(1)}, f32[1,3072]{1,0:T(1,128)S(1)}, u32[]{:S(2)}, u32[]{:S(2)}) collective-permute-start(f32[1,3072]{1,0:T(1,128)S(1)} %bitcast.49), channel_id=1, source_target_pairs={{0,16},{2,18},{4,20},{6,22},{8,24},{10,26},{12,28},{14,30},{16,0},... | collective-permute-start | bytes 36872 | tf_op jit(solution)/shard_map/ppermute | solution.py:11
  6.8 4.6 %collective-permute-start.3 = (f32[1,3072]{1,0:T(1,128)S(1)}, f32[1,3072]{1,0:T(1,128)S(1)}, u32[]{:S(2)}, u32[]{:S(2)}) collective-permute-start(f32[1,3072]{1,0:T(1,128)S(1)} %bitcast.50), channel_id=1, source_target_pairs={{0,8},{2,10},{4,12},{6,14},{8,0},{10,2},{12,4},{14,6},{16,24},{18,... | collective-permute-start | bytes 36872 | tf_op jit(solution)/shard_map/ppermute | solution.py:11
  7.7 10.8 %collective-permute-start.1 = (f32[2,128,384]{2,1,0:T(8,128)S(1)}, f32[2,128,384]{2,1,0:T(8,128)S(1)}, u32[]{:S(2)}, u32[]{:S(2)}) collective-permute-start(f32[2,128,384]{2,1,0:T(8,128)S(1)} %pad_maximum_fusion.1), channel_id=1, source_target_pairs={{0,4},{2,6},{4,0},{6,2},{8,12},{10,14},{12,8},{14,10},{16,20},{18,... | collective-permute-start | bytes 1179656 | tf_op jit(solution)/shard_map/ppermute | solution.py:11
  11.5 12.7 %collective-permute-start.11 = (f32[2,128,384]{2,1,0:T(8,128)S(1)}, f32[2,128,384]{2,1,0:T(8,128)S(1)}, u32[]{:S(2)}, u32[]{:S(2)}) collective-permute-start(f32[2,128,384]{2,1,0:T(8,128)S(1)} %pad_maximum_fusion.near0), channel_id=1, source_target_pairs={{0,24},{2,26},{4,28},{6,30},{8,0},{10,2},{12,4},{14,6},{16,8},{18,... | collective-permute-start | bytes 1179656 | tf_op jit(solution)/shard_map/ppermute | solution.py:16
  18.5 5.1 %collective-permute-start.6 = (f32[1,1536]{1,0:T(1,128)S(1)}, f32[1,1536]{1,0:T(1,128)S(1)}, u32[]{:S(2)}, u32[]{:S(2)}) collective-permute-start(f32[1,1536]{1,0:T(1,128)S(1)} %constant_dynamic-slice_fusion.4), channel_id=1, source_target_pairs={{0,2},{2,0},{4,6},{6,4},{8,10},{10,8},{12,14},{14,12},{16,18},{18,... | collective-permute-start | bytes 18440 | tf_op jit(solution)/shard_map/ppermute | solution.py:11
  18.5 18.8 %collective-permute-start.2 = (f32[2,128,384]{2,1,0:T(8,128)S(1)}, f32[2,128,384]{2,1,0:T(8,128)S(1)}, u32[]{:S(2)}, u32[]{:S(2)}) collective-permute-start(f32[2,128,384]{2,1,0:T(8,128)S(1)} %pad_maximum_fusion.3), channel_id=1, source_target_pairs={{0,4},{2,6},{4,0},{6,2},{8,12},{10,14},{12,8},{14,10},{16,20},{18,... | collective-permute-start | bytes 1179656 | tf_op jit(solution)/shard_map/ppermute | solution.py:11
  20.1 12.9 %collective-permute-start.8 = (f32[2,128,384]{2,1,0:T(8,128)S(1)}, f32[2,128,384]{2,1,0:T(8,128)S(1)}, u32[]{:S(2)}, u32[]{:S(2)}) collective-permute-start(f32[2,128,384]{2,1,0:T(8,128)S(1)} %collective-permute-done.1.far0), channel_id=1, source_target_pairs={{0,24},{2,26},{4,28},{6,30},{8,0},{10,2},{12,4},{14,6},{16,8},{18,... | collective-permute-start | bytes 1179656 | tf_op jit(solution)/shard_map/ppermute | solution.py:16
  23.6 6.6 %collective-permute-start.7 = (f32[1,768]{1,0:T(1,128)S(1)}, f32[1,768]{1,0:T(1,128)S(1)}, u32[]{:S(2)}, u32[]{:S(2)}) collective-permute-start(f32[1,768]{1,0:T(1,128)S(1)} %constant_dynamic-slice_fusion.2), channel_id=1, source_target_pairs={{0,4},{2,6},{4,0},{6,2},{8,12},{10,14},{12,8},{14,10},{16,20},{18,... | collective-permute-start | bytes 9224 | tf_op jit(solution)/shard_map/ppermute | solution.py:11
  24.2 17.3 %copy-start.3 = (f32[2,128,384]{2,1,0:T(8,128)}, f32[2,128,384]{2,1,0:T(8,128)S(1)}, u32[]{:S(2)}) copy-start(f32[2,128,384]{2,1,0:T(8,128)S(1)} %collective-permute-done.11.refs_0_) | copy-start | bytes 1179652
  24.2 17.2 %collective-permute-start.12 = (f32[2,128,384]{2,1,0:T(8,128)S(1)}, f32[2,128,384]{2,1,0:T(8,128)S(1)}, u32[]{:S(2)}, u32[]{:S(2)}) collective-permute-start(f32[2,128,384]{2,1,0:T(8,128)S(1)} %collective-permute-done.11.refs_0_), channel_id=1, source_target_pairs={{0,24},{2,26},{4,28},{6,30},{8,0},{10,2},{12,4},{14,6},{16,8},{18,... | collective-permute-start | bytes 1179656 | tf_op jit(solution)/shard_map/ppermute | solution.py:16
  33.0 9.5 %copy-start = (f32[2,128,384]{2,1,0:T(8,128)}, f32[2,128,384]{2,1,0:T(8,128)S(1)}, u32[]{:S(2)}) copy-start(f32[2,128,384]{2,1,0:T(8,128)S(1)} %collective-permute-done.8.refs_0_) | copy-start | bytes 1179652
  33.0 16.1 %collective-permute-start.10 = (f32[2,128,384]{2,1,0:T(8,128)S(1)}, f32[2,128,384]{2,1,0:T(8,128)S(1)}, u32[]{:S(2)}, u32[]{:S(2)}) collective-permute-start(f32[2,128,384]{2,1,0:T(8,128)S(1)} %collective-permute-done.8.refs_0_), channel_id=1, source_target_pairs={{0,24},{2,26},{4,28},{6,30},{8,0},{10,2},{12,4},{14,6},{16,8},{18,... | collective-permute-start | bytes 1179656 | tf_op jit(solution)/shard_map/ppermute | solution.py:16
  37.3 4.1 %copy-start.2 = (f32[2,128,384]{2,1,0:T(8,128)}, f32[2,128,384]{2,1,0:T(8,128)S(1)}, u32[]{:S(2)}) copy-start(f32[2,128,384]{2,1,0:T(8,128)S(1)} %collective-permute-done.2.far1) | copy-start | bytes 1179652
  51.2 5.9 %collective-permute-start.13 = (f32[2,2,8,64,128]{4,3,2,1,0:T(8,128)}, f32[2,2,8,64,128]{4,3,2,1,0:T(8,128)}, u32[]{:S(2)}, u32[]{:S(2)}) collective-permute-start(f32[2,2,8,64,128]{4,3,2,1,0:T(8,128)} %get-tuple-element.33), channel_id=1, source_target_pairs={{0,2},{2,0},{4,6},{6,4},{8,10},{10,8},{12,14},{14,12},{16,18},{18,... | collective-permute-start | bytes 3145736 | tf_op jit(solution)/shard_map/ppermute | solution.py:11
  51.2 4.8 %collective-permute-start.9 = (f32[2,2,4,64,128]{4,3,2,1,0:T(8,128)}, f32[2,2,4,64,128]{4,3,2,1,0:T(8,128)}, u32[]{:S(2)}, u32[]{:S(2)}) collective-permute-start(f32[2,2,4,64,128]{4,3,2,1,0:T(8,128)} %get-tuple-element.27), channel_id=1, source_target_pairs={{0,2},{2,0},{4,6},{6,4},{8,10},{10,8},{12,14},{14,12},{16,18},{18,... | collective-permute-start | bytes 1572872 | tf_op jit(solution)/shard_map/ppermute | solution.py:11
  51.7 13.8 %collective-permute-start.18 = (f32[2,128,384]{2,1,0:T(8,128)S(1)}, f32[2,128,384]{2,1,0:T(8,128)S(1)}, u32[]{:S(2)}, u32[]{:S(2)}) collective-permute-start(f32[2,128,384]{2,1,0:T(8,128)S(1)} %pad_maximum_fusion.2.near1), channel_id=1, source_target_pairs={{0,24},{2,26},{4,28},{6,30},{8,0},{10,2},{12,4},{14,6},{16,8},{18,... | collective-permute-start | bytes 1179656 | tf_op jit(solution)/shard_map/ppermute | solution.py:16
  56.0 17.1 %collective-permute-start.17 = (f32[2,128,384]{2,1,0:T(8,128)}, f32[2,128,384]{2,1,0:T(8,128)S(1)}, u32[]{:S(2)}, u32[]{:S(2)}) collective-permute-start(f32[2,128,384]{2,1,0:T(8,128)} %copy-done.2), channel_id=1, source_target_pairs={{0,24},{2,26},{4,28},{6,30},{8,0},{10,2},{12,4},{14,6},{16,8},{18,... | collective-permute-start | bytes 1179656 | tf_op jit(solution)/shard_map/ppermute | solution.py:16
  58.6 8.3 %copy-start.4 = (f32[2,128,384]{2,1,0:T(8,128)S(1)}, f32[2,128,384]{2,1,0:T(8,128)}, u32[]{:S(2)}) copy-start(f32[2,128,384]{2,1,0:T(8,128)} %copy-done.3) | copy-start | bytes 1179652
  58.7 16.2 %collective-permute-start.22 = (f32[8,64,128]{2,1,0:T(8,128)S(1)}, f32[8,64,128]{2,1,0:T(8,128)S(1)}, u32[]{:S(2)}, u32[]{:S(2)}) collective-permute-start(f32[8,64,128]{2,1,0:T(8,128)S(1)} %dynamic-slice_bitcast_fusion), channel_id=1, source_target_pairs={{0,1},{1,0},{2,3},{3,2},{4,5},{5,4},{6,7},{7,6},{8,9},{9,8},{10,11... | collective-permute-start | bytes 786440 | tf_op jit(solution)/shard_map/ppermute | solution.py:26
  60.3 16.1 %collective-permute-start.20 = (f32[8,64,128]{2,1,0:T(8,128)S(1)}, f32[8,64,128]{2,1,0:T(8,128)S(1)}, u32[]{:S(2)}, u32[]{:S(2)}) collective-permute-start(f32[8,64,128]{2,1,0:T(8,128)S(1)} %get-tuple-element.57), channel_id=1, source_target_pairs={{0,4},{1,5},{2,6},{3,7},{4,0},{5,1},{6,2},{7,3},{8,12},{9,13},{10,... | collective-permute-start | bytes 786440 | tf_op jit(solution)/shard_map/ppermute | solution.py:26
  60.8 16.1 %collective-permute-start.21 = (f32[8,64,128]{2,1,0:T(8,128)S(1)}, f32[8,64,128]{2,1,0:T(8,128)S(1)}, u32[]{:S(2)}, u32[]{:S(2)}) collective-permute-start(f32[8,64,128]{2,1,0:T(8,128)S(1)} %get-tuple-element.58), channel_id=1, source_target_pairs={{0,5},{1,4},{2,7},{3,6},{4,1},{5,0},{6,3},{7,2},{8,13},{9,12},{10,... | collective-permute-start | bytes 786440 | tf_op jit(solution)/shard_map/ppermute | solution.py:26
  62.4 10.7 %copy-start.1 = (f32[2,128,384]{2,1,0:T(8,128)S(1)}, f32[2,128,384]{2,1,0:T(8,128)}, u32[]{:S(2)}) copy-start(f32[2,128,384]{2,1,0:T(8,128)} %copy-done) | copy-start | bytes 1179652
  65.5 15.7 %collective-permute-start.15 = (f32[4,64,128]{2,1,0:T(8,128)S(1)}, f32[4,64,128]{2,1,0:T(8,128)S(1)}, u32[]{:S(2)}, u32[]{:S(2)}) collective-permute-start(f32[4,64,128]{2,1,0:T(8,128)S(1)} %get-tuple-element.69), channel_id=1, source_target_pairs={{0,5},{1,4},{2,7},{3,6},{4,1},{5,0},{6,3},{7,2},{8,13},{9,12},{10,... | collective-permute-start | bytes 393224 | tf_op jit(solution)/shard_map/ppermute | solution.py:26
  74.1 4.7 %collective-permute-start.19 = (f32[2,2,4,64,128]{4,3,2,1,0:T(8,128)S(1)}, f32[2,2,4,64,128]{4,3,2,1,0:T(8,128)S(1)}, u32[]{:S(2)}, u32[]{:S(2)}) collective-permute-start(f32[2,2,4,64,128]{4,3,2,1,0:T(8,128)S(1)} %get-tuple-element.41), channel_id=1, source_target_pairs={{0,2},{2,0},{4,6},{6,4},{8,10},{10,8},{12,14},{14,12},{16,18},{18,... | collective-permute-start | bytes 1572872 | tf_op jit(solution)/shard_map/ppermute | solution.py:11
  74.9 7.3 %collective-permute-start.14 = (f32[4,64,128]{2,1,0:T(8,128)S(1)}, f32[4,64,128]{2,1,0:T(8,128)S(1)}, u32[]{:S(2)}, u32[]{:S(2)}) collective-permute-start(f32[4,64,128]{2,1,0:T(8,128)S(1)} %get-tuple-element.70), channel_id=1, source_target_pairs={{0,4},{1,5},{2,6},{3,7},{4,0},{5,1},{6,2},{7,3},{8,12},{9,13},{10,... | collective-permute-start | bytes 393224 | tf_op jit(solution)/shard_map/ppermute | solution.py:26
  76.4 7.4 %collective-permute-start.16 = (f32[4,64,128]{2,1,0:T(8,128)S(1)}, f32[4,64,128]{2,1,0:T(8,128)S(1)}, u32[]{:S(2)}, u32[]{:S(2)}) collective-permute-start(f32[4,64,128]{2,1,0:T(8,128)S(1)} %get-tuple-element.67), channel_id=1, source_target_pairs={{0,1},{1,0},{2,3},{3,2},{4,5},{5,4},{6,7},{7,6},{8,9},{9,8},{10,11... | collective-permute-start | bytes 393224 | tf_op jit(solution)/shard_map/ppermute | solution.py:26
  77.7 9.0 %collective-permute-start.26 = (f32[4,64,128]{2,1,0:T(8,128)S(1)}, f32[4,64,128]{2,1,0:T(8,128)S(1)}, u32[]{:S(2)}, u32[]{:S(2)}) collective-permute-start(f32[4,64,128]{2,1,0:T(8,128)S(1)} %get-tuple-element.61), channel_id=1, source_target_pairs={{0,16},{2,18},{4,20},{6,22},{8,24},{10,26},{12,28},{14,30},{16,0},... | collective-permute-start | bytes 393224 | tf_op jit(solution)/shard_map/ppermute | solution.py:16
  79.0 7.7 %collective-permute-start.24 = (f32[4,64,128]{2,1,0:T(8,128)S(1)}, f32[4,64,128]{2,1,0:T(8,128)S(1)}, u32[]{:S(2)}, u32[]{:S(2)}) collective-permute-start(f32[4,64,128]{2,1,0:T(8,128)S(1)} %get-tuple-element.65), channel_id=1, source_target_pairs={{0,5},{1,4},{2,7},{3,6},{4,1},{5,0},{6,3},{7,2},{8,13},{9,12},{10,... | collective-permute-start | bytes 393224 | tf_op jit(solution)/shard_map/ppermute | solution.py:26
  81.2 6.7 %copy-start.6 = (f32[4,64,128]{2,1,0:T(8,128)}, f32[4,64,128]{2,1,0:T(8,128)S(1)}, u32[]{:S(2)}) copy-start(f32[4,64,128]{2,1,0:T(8,128)S(1)} %collective-permute-done.15.refs_2_) | copy-start | bytes 393220
  81.2 6.6 %collective-permute-start.23 = (f32[4,64,128]{2,1,0:T(8,128)S(1)}, f32[4,64,128]{2,1,0:T(8,128)S(1)}, u32[]{:S(2)}, u32[]{:S(2)}) collective-permute-start(f32[4,64,128]{2,1,0:T(8,128)S(1)} %get-tuple-element.66), channel_id=1, source_target_pairs={{0,4},{1,5},{2,6},{3,7},{4,0},{5,1},{6,2},{7,3},{8,12},{9,13},{10,... | collective-permute-start | bytes 393224 | tf_op jit(solution)/shard_map/ppermute | solution.py:26
  82.2 5.7 %copy-start.7 = (f32[4,64,128]{2,1,0:T(8,128)}, f32[4,64,128]{2,1,0:T(8,128)S(1)}, u32[]{:S(2)}) copy-start(f32[4,64,128]{2,1,0:T(8,128)S(1)} %collective-permute-done.14.refs_1_) | copy-start | bytes 393220
  82.2 5.7 %collective-permute-start.25 = (f32[4,64,128]{2,1,0:T(8,128)S(1)}, f32[4,64,128]{2,1,0:T(8,128)S(1)}, u32[]{:S(2)}, u32[]{:S(2)}) collective-permute-start(f32[4,64,128]{2,1,0:T(8,128)S(1)} %get-tuple-element.63), channel_id=1, source_target_pairs={{0,1},{1,0},{2,3},{3,2},{4,5},{5,4},{6,7},{7,6},{8,9},{9,8},{10,11... | collective-permute-start | bytes 393224 | tf_op jit(solution)/shard_map/ppermute | solution.py:26
  83.8 4.1 %copy-start.8 = (f32[4,64,128]{2,1,0:T(8,128)}, f32[4,64,128]{2,1,0:T(8,128)S(1)}, u32[]{:S(2)}) copy-start(f32[4,64,128]{2,1,0:T(8,128)S(1)} %collective-permute-done.16.refs_3_) | copy-start | bytes 393220
  86.7 1.2 %copy-start.9 = (f32[4,64,128]{2,1,0:T(8,128)}, f32[4,64,128]{2,1,0:T(8,128)S(1)}, u32[]{:S(2)}) copy-start(f32[4,64,128]{2,1,0:T(8,128)S(1)} %collective-permute-done.26.refs_9_) | copy-start | bytes 393220
  86.7 1.2 %copy-start.10 = (f32[4,64,128]{2,1,0:T(8,128)}, f32[4,64,128]{2,1,0:T(8,128)S(1)}, u32[]{:S(2)}) copy-start(f32[4,64,128]{2,1,0:T(8,128)S(1)} %collective-permute-done.24.refs_6_) | copy-start | bytes 393220
  87.8 0.7 copy-start.11
  87.9 0.6 copy-start.12
